TPU v7x, 32 devices: a whole 2x2x4 slice. The times are simulated.
32 devices in a mesh: section: 2 (over core), expert: 4 (over y, x), shard: 4 (over z).
Axes of the slice: x: 2, y: 2, z: 4, core: 2. Of those that a mesh axis runs over, the one named last changes fastest.
Arguments:
- x_in: bfloat16 [2, 16, 256, 768], P(None, ('expert', 'shard')), may hold values from -6 to 6
- cotangent: float32 [2, 16, 256, 768], P(None, ('expert', 'shard')), may hold values from -6 to 6
- gate_prev: bfloat16 [2, 16, 256, 8], P(None, ('expert', 'shard')), may hold values from -4 to 4
- segments: int32 [2, 16, 256], P(None, ('expert', 'shard')), may hold values from 0 to 3, never falling along the last dimension, each value on 1 to 128 neighbouring positions
- routes: int32 [2, 2, 16, 256, 2], P('section', None, ('expert', 'shard')), may hold values from 0 to 7, all different within a row
- priority: int32 [2, 2, 16, 256], P('section', None, ('expert', 'shard')), may hold values from 0 to 255, each once within a row
- attn_qkv: bfloat16 [2, 768, 2304], P('section', ('expert', 'shard')), may hold values from -0.21875 to 0.21875
- attn_out: bfloat16 [2, 768, 768], P('section', ('expert', 'shard')), may hold values from -0.875 to 0.875
- router: bfloat16 [2, 768, 8], P('section', ('expert', 'shard')), may hold values from -0.15625 to 0.15625
- const_proj: bfloat16 [2, 768, 4], P('section', ('expert', 'shard')), may hold values from -0.21875 to 0.21875
- const_vec: bfloat16 [2, 768, 2], P('section', ('expert', 'shard')), may hold values from -5 to 5
- gains: bfloat16 [2, 768, 2], P('section', ('expert', 'shard')), may hold values from 0.5 to 1.5
- gate_mix: float32 [2, 8, 8], P('section'), may hold values from -2 to 2
- expert_in: bfloat16 [2, 4, 768, 4096], P('section', 'expert', 'shard'), may hold values from -0.21875 to 0.21875
- expert_out: bfloat16 [2, 4, 2048, 768], P('section', 'expert', 'shard'), may hold values from -0.25 to 0.25
Outputs:
- section_out: bfloat16 [2, 2, 16, 256, 768], P('section', None, ('expert', 'shard'))
- section_grad: float32 [2, 2, 16, 256, 768], P('section', None, ('expert', 'shard'))
- gate_grad: float32 [2, 2, 16, 256, 8], P('section', None, ('expert', 'shard'))
- attn_qkv_grad: float32 [2, 768, 2304], P('section', ('expert', 'shard'))
- attn_out_grad: float32 [2, 768, 768], P('section', ('expert', 'shard'))
- router_grad: float32 [2, 768, 8], P('section', ('expert', 'shard'))
- const_proj_grad: float32 [2, 768, 4], P('section', ('expert', 'shard'))
- const_vec_grad: float32 [2, 768, 2], P('section', ('expert', 'shard'))
- gains_grad: float32 [2, 768, 2], P('section', ('expert', 'shard'))
- gate_mix_grad: float32 [2, 8, 8], P('section')
- expert_in_grad: float32 [2, 4, 768, 4096], P('section', 'expert', 'shard')
- expert_out_grad: float32 [2, 4, 2048, 768], P('section', 'expert', 'shard')
Inputs may be any that keep to these rules, and one draw needn't show every extreme that they name: `routes`: the 2 experts of a token differ; indices below 4 are feed-forward experts, then the zero, the copy and the 2 constant experts. `priority`: each sequence's tokens hold each number once. `segments`: segment numbers never fall along a sequence.
All inputs are finite; a program needn't handle non-finite values.
Results may differ from a plain program's by a relative error of at most 0.024.
Values may be sent and summed in bfloat16 or wider, within the bound.
A program may use at most 256 MiB of HBM per device.

v0:
```python
import math

import jax
import jax.numpy as jnp
from jax import lax
from jax.sharding import PartitionSpec as P

HEADS = 12
HEAD = 64
TOP = 2


HIGH_PRECISION = lax.Precision.HIGHEST
norm_eps = 1e-06
masked_score = -1e30


def from_behind(x, axis, by):
    devices = lax.axis_size(axis)
    pairs = [(i, i + by) for i in range(devices) if 0 <= i + by < devices]
    return lax.ppermute(x, axis, pairs)


def as_sent(x):

    def short(part):
        return part.astype(jnp.bfloat16) if part.dtype == jnp.float32 else part

    return jax.tree.map(short, x)


def normed(values):
    inverse = lax.rsqrt(jnp.mean(values * values, axis=-1, keepdims=True) + norm_eps)
    return (values * inverse, inverse)


def norm_back(grad_unit, unit, inverse):
    return inverse * (grad_unit - unit * jnp.mean(grad_unit * unit, axis=-1, keepdims=True))


def rotate(values, cosine, sine):
    half_head = values.shape[-1] // 2
    first = values[..., :half_head]
    second = values[..., half_head:]
    return jnp.concatenate(
        [first * cosine - second * sine, first * sine + second * cosine], axis=-1
    )


def rotate_back(grads, cosine, sine):
    half_head = grads.shape[-1] // 2
    first = grads[..., :half_head]
    second = grads[..., half_head:]
    return jnp.concatenate(
        [first * cosine + second * sine, second * cosine - first * sine], axis=-1
    )


def make_tables(seg, route_ids, prio, nffn, capacity, nexp):
    seq_len = seg.shape[0]
    place = lax.iota(jnp.int32, seq_len)
    allowed = (seg[:, None] == seg[None, :]) & (place[None, :] <= place[:, None])
    positions = jnp.sum(allowed.astype(jnp.float32), axis=1) - 1.0
    rates = jnp.exp(lax.iota(jnp.float32, HEAD // 2) * (-2.0 * math.log(10000.0) / HEAD))
    angles = positions[:, None] * rates[None, :]
    cosine = jnp.cos(angles)[:, None, :]
    sine = jnp.sin(angles)[:, None, :]
    choose = (route_ids[:, :, None] == lax.iota(jnp.int32, nexp)[None, None, :]).astype(jnp.float32)
    routed = jnp.sum(choose[:, :, :nffn], axis=1).astype(jnp.bfloat16)
    before = (prio[None, :] < prio[:, None]).astype(jnp.bfloat16)
    rank = jnp.dot(before, routed, preferred_element_type=jnp.float32)
    rank_k = jnp.sum(choose[:, :, :nffn] * rank[:, None, :], axis=-1)
    slot = route_ids.astype(jnp.float32) * capacity + rank_k
    keep = (route_ids < nffn) & (rank_k < capacity)
    columns = lax.iota(jnp.float32, nffn * capacity)
    table = (keep[:, :, None] & (slot[:, :, None] == columns[None, None, :])).astype(jnp.bfloat16)
    return (allowed, cosine, sine, choose, table)


def layer_forward(x_here, r_here, tables, weights, experts, mix_matrix, capacity):
    w_qkv, w_attn, w_router, w_const, const_values, gain_pair = weights
    allowed, cosine, sine, choose, table = tables
    w_in, w_out = experts
    seq_len, width = x_here.shape
    owners = lax.axis_size("expert")
    local_count = w_in.shape[0]
    nffn = owners * local_count
    hidden_units = w_in.shape[2] // 2
    scale = HEAD ** (-0.5)
    gain_f = gain_pair.astype(jnp.float32)
    unit_first, inverse_first = normed(x_here)
    first_b = (unit_first * gain_f[:, 0]).astype(jnp.bfloat16)
    projected = jnp.dot(first_b, w_qkv, preferred_element_type=jnp.float32)
    queries = rotate(projected[:, :width].reshape(seq_len, HEADS, HEAD), cosine, sine).astype(
        jnp.bfloat16
    )
    keys_rot = rotate(
        projected[:, width : 2 * width].reshape(seq_len, HEADS, HEAD), cosine, sine
    ).astype(jnp.bfloat16)
    values_b = projected[:, 2 * width :].reshape(seq_len, HEADS, HEAD).astype(jnp.bfloat16)
    scores = (
        jnp.einsum("qhd,khd->hqk", queries, keys_rot, preferred_element_type=jnp.float32) * scale
    )
    scores = jnp.where(allowed[None], scores, masked_score)
    top_score = jnp.max(scores, axis=-1, keepdims=True)
    log_total = top_score + jnp.log(jnp.sum(jnp.exp(scores - top_score), axis=-1, keepdims=True))
    probs_att = jnp.exp(scores - log_total).astype(jnp.bfloat16)
    attended = jnp.einsum("hqk,khd->qhd", probs_att, values_b, preferred_element_type=jnp.float32)
    attended = attended.reshape(seq_len, width).astype(jnp.bfloat16)
    after_attn = x_here + jnp.dot(attended, w_attn, preferred_element_type=jnp.float32)
    unit_second, inverse_second = normed(after_attn)
    second = unit_second * gain_f[:, 1]
    second_b = second.astype(jnp.bfloat16)
    logits = jnp.dot(second_b, w_router, preferred_element_type=jnp.float32) + jnp.dot(
        r_here, mix_matrix, precision=HIGH_PRECISION
    )
    probs = jax.nn.softmax(logits, axis=-1)
    gate_values = jnp.sum(choose * probs[:, None, :], axis=-1)
    dispatch = table[:, 0] + table[:, 1]
    buffer = jnp.einsum("sc,sd->cd", dispatch, second_b, preferred_element_type=jnp.float32).astype(
        jnp.bfloat16
    )
    arrived = lax.all_to_all(
        buffer.reshape(owners, local_count, capacity, width),
        "expert",
        split_axis=0,
        concat_axis=0,
        tiled=True,
    )
    gate_up = jnp.einsum("sjcd,jdf->sjcf", arrived, w_in, preferred_element_type=jnp.float32)
    hidden = (jax.nn.silu(gate_up[..., :hidden_units]) * gate_up[..., hidden_units:]).astype(
        jnp.bfloat16
    )
    made = jnp.einsum("sjch,jhd->sjcd", hidden, w_out, preferred_element_type=jnp.float32).astype(
        jnp.bfloat16
    )
    returned = lax.all_to_all(made, "expert", split_axis=0, concat_axis=0, tiled=True).reshape(
        nffn * capacity, width
    )
    picked = jnp.einsum("skc,cd->skd", table, returned, preferred_element_type=jnp.float32)
    extra = jnp.einsum("sk,ske->se", gate_values, choose[:, :, nffn:], precision=HIGH_PRECISION)
    const_mix = jax.nn.softmax(
        jnp.dot(second_b, w_const, preferred_element_type=jnp.float32).reshape(seq_len, -1, 2),
        axis=-1,
    )
    coefficient = extra[:, 1] + jnp.sum(extra[:, 2:] * const_mix[:, :, 0], axis=-1)
    const_f = const_values.astype(jnp.float32)
    result = (
        after_attn
        + jnp.sum(gate_values[:, :, None] * picked, axis=1)
        + coefficient[:, None] * second
    )
    result = result + jnp.dot(
        extra[:, 2:] * const_mix[:, :, 1], const_f.T, precision=HIGH_PRECISION
    )
    kept = (
        unit_first,
        inverse_first,
        first_b,
        queries,
        keys_rot,
        values_b,
        log_total,
        attended,
        unit_second,
        inverse_second,
        second,
        second_b,
        r_here,
        probs,
        gate_values,
        picked,
        const_mix,
        extra,
        arrived,
        gate_up,
        hidden,
    )
    return (result, logits, kept)


def layer_backward(grad_y, grad_log_in, kept, tables, weights, experts, mix_matrix, capacity):
    (
        unit_first,
        inverse_first,
        first_b,
        queries,
        keys_rot,
        values_b,
        log_total,
        attended,
        unit_second,
        inverse_second,
        second,
        second_b,
        r_here,
        probs,
        gate_values,
        picked,
        const_mix,
        extra,
        arrived,
        gate_up,
        hidden,
    ) = kept
    w_qkv, w_attn, w_router, w_const, const_values, gain_pair = weights
    allowed, cosine, sine, choose, table = tables
    w_in, w_out = experts
    seq_len, width = grad_y.shape
    owners = lax.axis_size("expert")
    local_count = w_in.shape[0]
    nffn = owners * local_count
    hidden_units = w_in.shape[2] // 2
    scale = HEAD ** (-0.5)
    gain_f = gain_pair.astype(jnp.float32)
    const_f = const_values.astype(jnp.float32)
    grad_picked = (gate_values[:, :, None] * grad_y[:, None, :]).astype(jnp.bfloat16)
    grad_gates = jnp.sum(picked * grad_y[:, None, :], axis=-1)
    grad_returned = jnp.einsum(
        "skc,skd->cd", table, grad_picked, preferred_element_type=jnp.float32
    ).astype(jnp.bfloat16)
    grad_made = lax.all_to_all(
        grad_returned.reshape(owners, local_count, capacity, width),
        "expert",
        split_axis=0,
        concat_axis=0,
        tiled=True,
    )
    grad_w_out = jnp.einsum("sjch,sjcd->jhd", hidden, grad_made, preferred_element_type=jnp.float32)
    grad_hidden = jnp.einsum("sjcd,jhd->sjch", grad_made, w_out, preferred_element_type=jnp.float32)
    gate_part = gate_up[..., :hidden_units]
    up_part = gate_up[..., hidden_units:]
    sigmoid = jax.nn.sigmoid(gate_part)
    grad_gate = grad_hidden * up_part * sigmoid * (1.0 + gate_part * (1.0 - sigmoid))
    grad_up = grad_hidden * gate_part * sigmoid
    grad_gate_up = jnp.concatenate([grad_gate, grad_up], axis=-1).astype(jnp.bfloat16)
    grad_w_in = jnp.einsum(
        "sjcd,sjcf->jdf", arrived, grad_gate_up, preferred_element_type=jnp.float32
    )
    grad_arrived = jnp.einsum(
        "sjcf,jdf->sjcd", grad_gate_up, w_in, preferred_element_type=jnp.float32
    ).astype(jnp.bfloat16)
    grad_buffer = lax.all_to_all(
        grad_arrived, "expert", split_axis=0, concat_axis=0, tiled=True
    ).reshape(nffn * capacity, width)
    dispatch = table[:, 0] + table[:, 1]
    grad_second = jnp.dot(dispatch, grad_buffer, preferred_element_type=jnp.float32)
    along_second = jnp.sum(grad_y * second, axis=-1)
    along_const = jnp.dot(grad_y, const_f, precision=HIGH_PRECISION)
    coefficient = extra[:, 1] + jnp.sum(extra[:, 2:] * const_mix[:, :, 0], axis=-1)
    grad_second = grad_second + coefficient[:, None] * grad_y
    grad_const_f = jnp.dot(grad_y.T, extra[:, 2:] * const_mix[:, :, 1], precision=HIGH_PRECISION)
    grad_mixing = jnp.stack(
        [extra[:, 2:] * along_second[:, None], extra[:, 2:] * along_const], axis=-1
    )
    grad_extra = jnp.concatenate(
        [
            jnp.zeros_like(along_second)[:, None],
            along_second[:, None],
            const_mix[:, :, 0] * along_second[:, None] + const_mix[:, :, 1] * along_const,
        ],
        axis=1,
    )
    grad_mix_logits = const_mix * (
        grad_mixing - jnp.sum(const_mix * grad_mixing, axis=-1, keepdims=True)
    )
    grad_mix_logits = grad_mix_logits.reshape(seq_len, -1)
    second_f = second_b.astype(jnp.float32)
    grad_w_const = jnp.dot(second_f.T, grad_mix_logits, precision=HIGH_PRECISION)
    grad_second = grad_second + jnp.dot(
        grad_mix_logits, w_const.astype(jnp.float32).T, precision=HIGH_PRECISION
    )
    grad_gates = grad_gates + jnp.einsum(
        "se,ske->sk", grad_extra, choose[:, :, nffn:], precision=HIGH_PRECISION
    )
    grad_probs = jnp.einsum("sk,ske->se", grad_gates, choose, precision=HIGH_PRECISION)
    grad_logits = (
        probs * (grad_probs - jnp.sum(probs * grad_probs, axis=-1, keepdims=True)) + grad_log_in
    )
    grad_w_router = jnp.dot(second_f.T, grad_logits, precision=HIGH_PRECISION)
    grad_second = grad_second + jnp.dot(
        grad_logits, w_router.astype(jnp.float32).T, precision=HIGH_PRECISION
    )
    grad_mix = jnp.dot(r_here.T, grad_logits, precision=HIGH_PRECISION)
    grad_r = jnp.dot(grad_logits, mix_matrix.T, precision=HIGH_PRECISION)
    grad_gain_second = jnp.sum(grad_second * unit_second, axis=0)
    grad_after = grad_y + norm_back(grad_second * gain_f[:, 1], unit_second, inverse_second)
    grad_branch = grad_after.astype(jnp.bfloat16)
    grad_w_attn = jnp.einsum("sd,se->de", attended, grad_branch, preferred_element_type=jnp.float32)
    grad_attended = jnp.einsum("se,de->sd", grad_branch, w_attn, preferred_element_type=jnp.float32)
    grad_attended = grad_attended.astype(jnp.bfloat16).reshape(seq_len, HEADS, HEAD)
    scores = (
        jnp.einsum("qhd,khd->hqk", queries, keys_rot, preferred_element_type=jnp.float32) * scale
    )
    scores = jnp.where(allowed[None], scores, masked_score)
    probs_att = jnp.exp(scores - log_total)
    grad_probs_att = jnp.einsum(
        "qhd,khd->hqk", grad_attended, values_b, preferred_element_type=jnp.float32
    )
    grad_values = jnp.einsum(
        "hqk,qhd->khd",
        probs_att.astype(jnp.bfloat16),
        grad_attended,
        preferred_element_type=jnp.float32,
    )
    grad_scores = probs_att * (
        grad_probs_att - jnp.sum(probs_att * grad_probs_att, axis=-1, keepdims=True)
    )
    grad_scores = grad_scores.astype(jnp.bfloat16)
    grad_queries = (
        jnp.einsum("hqk,khd->qhd", grad_scores, keys_rot, preferred_element_type=jnp.float32)
        * scale
    )
    grad_keys = (
        jnp.einsum("hqk,qhd->khd", grad_scores, queries, preferred_element_type=jnp.float32) * scale
    )
    grad_projected = jnp.concatenate(
        [
            rotate_back(grad_queries, cosine, sine).reshape(seq_len, width),
            rotate_back(grad_keys, cosine, sine).reshape(seq_len, width),
            grad_values.reshape(seq_len, width),
        ],
        axis=1,
    ).astype(jnp.bfloat16)
    grad_w_qkv = jnp.einsum(
        "sd,sf->df", first_b, grad_projected, preferred_element_type=jnp.float32
    )
    grad_first = jnp.einsum("sf,df->sd", grad_projected, w_qkv, preferred_element_type=jnp.float32)
    grad_gain_first = jnp.sum(grad_first * unit_first, axis=0)
    grad_x = grad_after + norm_back(grad_first * gain_f[:, 0], unit_first, inverse_first)
    grad_gain = jnp.stack([grad_gain_first, grad_gain_second], axis=1)
    weight_grads = (grad_w_qkv, grad_w_attn, grad_w_router, grad_w_const, grad_const_f, grad_gain)
    return (grad_x, grad_r, weight_grads, grad_mix, (grad_w_in, grad_w_out))


def take_item(stack, position):
    return lax.dynamic_index_in_dim(stack, position, 0, keepdims=False)


def store_item(stack, position, in_range, update):
    current = take_item(stack, position)
    return lax.dynamic_update_index_in_dim(stack, jnp.where(in_range, update, current), position, 0)


def local(
    x_in,
    cotangent,
    gate_prev,
    segments,
    routes,
    priority,
    attn_qkv,
    attn_out,
    router,
    const_proj,
    const_vec,
    gains,
    gate_mix,
    expert_in,
    expert_out,
):
    micro = x_in.shape[0]
    seq_len = x_in.shape[2]
    width = x_in.shape[3]
    nexp = gate_prev.shape[-1]
    nffn = lax.axis_size("expert") * expert_in.shape[1]
    capacity = (5 * TOP * seq_len + 4 * nexp - 1) // (4 * nexp)
    section_index = lax.axis_index("section")
    is_first = section_index == 0
    inputs = x_in[:, 0]
    upstream = cotangent[:, 0]
    residual_in = gate_prev[:, 0]
    seg_all = segments[:, 0]
    route_all = routes[0, :, 0]
    prio_all = priority[0, :, 0]
    mix_matrix = gate_mix[0]
    local_pieces = (attn_qkv[0], attn_out[0], router[0], const_proj[0], const_vec[0], gains[0])
    expert_pieces = (expert_in[0], expert_out[0])
    weights = (
        lax.all_gather(local_pieces[0], ("expert", "shard"), axis=0, tiled=True),
        lax.all_gather(local_pieces[1], ("expert", "shard"), axis=0, tiled=True),
        lax.all_gather(local_pieces[2], ("expert", "shard"), axis=0, tiled=True),
        lax.all_gather(local_pieces[3], ("expert", "shard"), axis=0, tiled=True),
        lax.all_gather(local_pieces[4], ("expert", "shard"), axis=0, tiled=True),
        lax.all_gather(local_pieces[5], ("expert", "shard"), axis=0, tiled=True),
    )
    experts = (
        lax.all_gather(expert_pieces[0], "shard", axis=1, tiled=True),
        lax.all_gather(expert_pieces[1], "shard", axis=1, tiled=True),
    )
    incoming = (jnp.zeros((seq_len, width), jnp.bfloat16), jnp.zeros((seq_len, nexp), jnp.bfloat16))
    outputs = jnp.zeros((micro, seq_len, width), jnp.bfloat16)
    kept_all = None
    for step in range(micro + 1):
        offset = step - section_index
        in_range = (offset >= 0) & (offset < micro)
        position = jnp.clip(offset, 0, micro - 1)
        x_here = jnp.where(is_first, take_item(inputs, position), incoming[0]).astype(jnp.float32)
        r_here = jnp.where(is_first, take_item(residual_in, position), incoming[1]).astype(
            jnp.float32
        )
        tables = make_tables(
            take_item(seg_all, position),
            take_item(route_all, position),
            take_item(prio_all, position),
            nffn,
            capacity,
            nexp,
        )
        result, logits, kept = layer_forward(
            x_here, r_here, tables, weights, experts, mix_matrix, capacity
        )
        sent_out = result.astype(jnp.bfloat16)
        outputs = store_item(outputs, position, in_range, sent_out)
        if kept_all is None:
            kept_all = jax.tree.map(lambda item: jnp.zeros((micro,) + item.shape, item.dtype), kept)
        kept_all = jax.tree.map(
            lambda stack, item: store_item(stack, position, in_range, item), kept_all, kept
        )
        if step < micro:
            incoming = from_behind((sent_out, logits.astype(jnp.bfloat16)), "section", 1)
    weights = (
        lax.all_gather(local_pieces[0], ("expert", "shard"), axis=0, tiled=True),
        lax.all_gather(local_pieces[1], ("expert", "shard"), axis=0, tiled=True),
        lax.all_gather(local_pieces[2], ("expert", "shard"), axis=0, tiled=True),
        lax.all_gather(local_pieces[3], ("expert", "shard"), axis=0, tiled=True),
        lax.all_gather(local_pieces[4], ("expert", "shard"), axis=0, tiled=True),
        lax.all_gather(local_pieces[5], ("expert", "shard"), axis=0, tiled=True),
    )
    experts = (
        lax.all_gather(expert_pieces[0], "shard", axis=1, tiled=True),
        lax.all_gather(expert_pieces[1], "shard", axis=1, tiled=True),
    )
    returning = (
        jnp.zeros((seq_len, width), jnp.bfloat16),
        jnp.zeros((seq_len, nexp), jnp.bfloat16),
    )
    input_grads = jnp.zeros((micro, seq_len, width), jnp.float32)
    residual_grads = jnp.zeros((micro, seq_len, nexp), jnp.float32)
    totals = None
    for step in range(micro + 1):
        offset = micro - step - section_index
        in_range = (offset >= 0) & (offset < micro)
        position = jnp.clip(offset, 0, micro - 1)
        grad_y = jnp.where(
            is_first, returning[0].astype(jnp.float32), take_item(upstream, position)
        )
        grad_log_in = jnp.where(is_first, returning[1].astype(jnp.float32), 0.0)
        kept = jax.tree.map(lambda stack: take_item(stack, position), kept_all)
        tables = make_tables(
            take_item(seg_all, position),
            take_item(route_all, position),
            take_item(prio_all, position),
            nffn,
            capacity,
            nexp,
        )
        grad_x, grad_r, weight_grads, grad_mix, expert_grads = layer_backward(
            grad_y, grad_log_in, kept, tables, weights, experts, mix_matrix, capacity
        )
        contribution = (weight_grads, grad_mix, expert_grads)
        masked = jax.tree.map(lambda grad_item: jnp.where(in_range, grad_item, 0.0), contribution)
        if totals is None:
            totals = masked
        else:
            totals = jax.tree.map(jnp.add, totals, masked)
        input_grads = store_item(input_grads, position, in_range, grad_x)
        residual_grads = store_item(residual_grads, position, in_range, grad_r)
        if step < micro:
            returning = from_behind(
                (grad_x.astype(jnp.bfloat16), grad_r.astype(jnp.bfloat16)), "section", -1
            )
    weight_totals, mix_total, expert_totals = totals
    attn_sums = lax.psum_scatter(
        weight_totals, ("expert", "shard"), scatter_dimension=0, tiled=True
    )
    mix_sum = lax.psum(mix_total, ("expert", "shard"))
    expert_sums = jax.tree.map(
        lambda part: part.astype(jnp.float32),
        lax.psum_scatter(as_sent(expert_totals), "shard", scatter_dimension=1, tiled=True),
    )
    return (
        outputs[None, :, None],
        input_grads[None, :, None],
        residual_grads[None, :, None],
        attn_sums[0][None],
        attn_sums[1][None],
        attn_sums[2][None],
        attn_sums[3][None],
        attn_sums[4][None],
        attn_sums[5][None],
        mix_sum[None],
        expert_sums[0][None],
        expert_sums[1][None],
    )


def solution(mesh):
    placed = (
        P(None, ("expert", "shard"), None, None),
        P(None, ("expert", "shard"), None, None),
        P(None, ("expert", "shard"), None, None),
        P(None, ("expert", "shard"), None),
        P("section", None, ("expert", "shard"), None, None),
        P("section", None, ("expert", "shard"), None),
        P("section", ("expert", "shard"), None),
        P("section", ("expert", "shard"), None),
        P("section", ("expert", "shard"), None),
        P("section", ("expert", "shard"), None),
        P("section", ("expert", "shard"), None),
        P("section", ("expert", "shard"), None),
        P("section", None, None),
        P("section", "expert", "shard", None),
        P("section", "expert", "shard", None),
    )
    return jax.shard_map(
        local,
        mesh=mesh,
        in_specs=placed,
        out_specs=(
            P("section", None, ("expert", "shard"), None, None),
            P("section", None, ("expert", "shard"), None, None),
            P("section", None, ("expert", "shard"), None, None),
            P("section", ("expert", "shard"), None),
            P("section", ("expert", "shard"), None),
            P("section", ("expert", "shard"), None),
            P("section", ("expert", "shard"), None),
            P("section", ("expert", "shard"), None),
            P("section", ("expert", "shard"), None),
            P("section", None, None),
            P("section", "expert", "shard", None),
            P("section", "expert", "shard", None),
        ),
        check_vma=False,
    )
```

profile of v0, /device:TPU:0, one launch (start us, length us, event | category | flops | bytes accessed | tf_op | source)
XLA Modules:
  0.0 1625.3 jit_solution(16556035214746999540)
XLA Ops:
  12.8 48.5 %all-gather.7 = bf16[1,768,2]{2,0,1:T(2,128)(2,1)S(1)} all-gather(bf16[1,48,2]{2,0,1:T(2,128)(2,1)S(1)} %copy.287), channel_id=9, replica_groups=mesh['section'=2,'expert'=4,'shard'=4] {'expert','shard'}, dimensions={1}, use_global_device_ids=true | all-gather | bytes 3264 | tf_op jit(solution)/shard_map/all_gather | solution.py:384
  61.7 42.5 %all-gather = bf16[1,768,2]{2,0,1:T(2,128)(2,1)S(1)} all-gather(bf16[1,48,2]{2,0,1:T(2,128)(2,1)S(1)} %copy.275), channel_id=2, replica_groups=mesh['section'=2,'expert'=4,'shard'=4] {'expert','shard'}, dimensions={1}, use_global_device_ids=true | all-gather | bytes 3264 | tf_op jit(solution)/shard_map/all_gather | solution.py:385
  105.2 44.5 %all-gather.6 = bf16[1,768,4]{2,0,1:T(2,128)(2,1)S(1)} all-gather(bf16[1,48,4]{2,0,1:T(2,128)(2,1)S(1)} %copy.284), channel_id=8, replica_groups=mesh['section'=2,'expert'=4,'shard'=4] {'expert','shard'}, dimensions={1}, use_global_device_ids=true | all-gather | bytes 6528 | tf_op jit(solution)/shard_map/all_gather | solution.py:383
  151.3 45.4 %all-gather.3 = bf16[1,768,8]{2,0,1:T(2,128)(2,1)S(1)} all-gather(bf16[1,48,8]{2,0,1:T(2,128)(2,1)S(1)} %copy.280), channel_id=5, replica_groups=mesh['section'=2,'expert'=4,'shard'=4] {'expert','shard'}, dimensions={1}, use_global_device_ids=true | all-gather | bytes 13056 | tf_op jit(solution)/shard_map/all_gather | solution.py:382
  240.5 25.8 %all-gather.17.cloned.1.call-done = bf16[1,1,768,4096]{3,2,1,0:T(8,128)(2,1)} async-done(((bf16[1,1,192,4096]{3,2,1,0:T(8,128)(2,1)}), bf16[1,1,768,4096]{3,2,1,0:T(8,128)(2,1)}) %all-gather.17.cloned.1.call-update) | async-done | bytes 6291472 | tf_op jit(solution)/shard_map/all_gather | solution.py:388
  281.6 48.2 %all-gather.19.cloned.1.call-done = bf16[1,1,2048,768]{3,2,1,0:T(8,128)(2,1)} async-done(((bf16[1,1,512,768]{3,2,1,0:T(8,128)(2,1)}), bf16[1,1,2048,768]{3,2,1,0:T(8,128)(2,1)}) %all-gather.19.cloned.1.call-update) | async-done | bytes 3145744 | tf_op jit(solution)/shard_map/all_gather | solution.py:389
  401.3 9.1 bitcast_dynamic-update-slice_fusion.1
  488.7 10.6 bitcast_dynamic-update-slice_fusion
  499.4 11.7 dynamic-slice_bitcast_fusion
  530.9 5.9 fusion.106
  605.5 6.7 all-to-all-done.9
  671.5 6.8 all-to-all-done.11
  698.2 9.0 fusion.52
  710.6 6.5 fusion.78
  717.1 6.5 fusion.77
  723.7 13.3 fusion.18
  767.7 39.3 %psum.7 = f32[1,8,8]{2,1,0:T(8,128)} all-reduce(f32[1,8,8]{2,1,0:T(8,128)S(1)} %fusion.205), channel_id=1, replica_groups=mesh['section'=2,'expert'=4,'shard'=4] {'expert','shard'}, use_global_device_ids=true, to_apply=%region_78.79 | all-reduce | flops 64 | bytes 512 | tf_op jit(solution)/shard_map/psum | solution.py:477
  808.5 92.3 %reduce-scatter.27.cloned.1.call-done = f32[48,4]{1,0:T(8,128)} async-done(((f32[768,4]{1,0:T(8,128)}), f32[48,4]{1,0:T(8,128)}) %reduce-scatter.27.cloned.1.call-update) | async-done | bytes 784
  902.1 124.0 %reduce-scatter.25.cloned.1.call-done = f32[48,8]{1,0:T(8,128)} async-done(((f32[768,8]{1,0:T(8,128)}), f32[48,8]{1,0:T(8,128)}) %reduce-scatter.25.cloned.1.call-update) | async-done | bytes 1552
  1030.1 122.1 %reduce-scatter.31.cloned.1.call-done = f32[48,2]{1,0:T(8,128)} async-done(((f32[768,2]{1,0:T(8,128)}), f32[48,2]{1,0:T(8,128)}) %reduce-scatter.31.cloned.1.call-update) | async-done | bytes 400
  1153.5 60.9 %reduce-scatter.23.cloned.1.call-done = bf16[1,512,768]{2,1,0:T(8,128)(2,1)} async-done(((bf16[1,2048,768]{2,1,0:T(8,128)(2,1)}), bf16[1,512,768]{2,1,0:T(8,128)(2,1)}) %reduce-scatter.23.cloned.1.call-update) | async-done | bytes 786448 | tf_op jit(solution)/shard_map/reduce_scatter | solution.py:480
  1216.8 110.6 %reduce-scatter.21.cloned.1.call-done = bf16[1,192,4096]{2,1,0:T(8,128)(2,1)} async-done(((bf16[1,768,4096]{2,1,0:T(8,128)(2,1)}), bf16[1,192,4096]{2,1,0:T(8,128)(2,1)}) %reduce-scatter.21.cloned.1.call-update) | async-done | bytes 1572880 | tf_op jit(solution)/shard_map/reduce_scatter | solution.py:480
  1330.8 130.2 %reduce-scatter.19.cloned.1.call-done = f32[48,768]{1,0:T(8,128)} async-done(((f32[768,768]{1,0:T(8,128)}), f32[48,768]{1,0:T(8,128)}) %reduce-scatter.19.cloned.1.call-update) | async-done | bytes 147472 | tf_op jit(solution)/shard_map/reduce_scatter | solution.py:474
  1461.0 156.9 %reduce-scatter.17.cloned.1.call-done = f32[48,2304]{1,0:T(8,128)} async-done(((f32[768,2304]{1,0:T(8,128)}), f32[48,2304]{1,0:T(8,128)}) %reduce-scatter.17.cloned.1.call-update) | async-done | bytes 442384 | tf_op jit(solution)/shard_map/reduce_scatter | solution.py:474
  (1047 shorter events, 429.1 us)
Async XLA Ops:
  7.2 197.2 %all-gather.13.cloned.1.call-start = ((), (), s32[]{:S(2)}) async-start(), calls=%async_computation.24 | async-start | bytes 3760128 | tf_op jit(solution)/shard_map/all_gather | solution.py:380
  8.0 206.6 %all-gather.15.cloned.1.call-start = ((), (), s32[]{:S(2)}) async-start(), calls=%async_computation.25 | async-start | bytes 1253376 | tf_op jit(solution)/shard_map/all_gather | solution.py:381
  8.7 257.6 %all-gather.17.cloned.1.call-start = ((), (), s32[]{:S(2)}) async-start(), calls=%async_computation.26 | async-start | bytes 7864320 | tf_op jit(solution)/shard_map/all_gather | solution.py:388
  9.5 320.3 %all-gather.19.cloned.1.call-start = ((), (), s32[]{:S(2)}) async-start(), calls=%async_computation.27 | async-start | bytes 3932160 | tf_op jit(solution)/shard_map/all_gather | solution.py:389
  221.8 18.7 %all-to-all-start = ((bf16[4,1,80,768]{3,2,1,0:T(8,128)(2,1)}), bf16[4,1,80,768]{3,2,1,0:T(8,128)(2,1)}, u32[]{:S(2)}, u32[]{:S(2)}) async-start(bf16[4,1,80,768]{3,2,1,0:T(8,128)(2,1)} %bitcast.20), calls=%async_computation | async-start | bytes 983040 | tf_op jit(solution)/shard_map/all_to_all | solution.py:123
  225.9 148.6 %collective-permute-start.1 = (bf16[256,8]{0,1:T(8,128)(2,1)}, bf16[256,8]{0,1:T(8,128)(2,1)}, u32[]{:S(2)}, u32[]{:S(2)}) collective-permute-start(bf16[256,8]{0,1:T(8,128)(2,1)} %get-tuple-element.141), channel_id=1, source_target_pairs={{0,16},{1,17},{2,18},{3,19},{4,20},{5,21},{6,22},{7,23},{8,24},{9,... | collective-permute-start | bytes 12296 | tf_op jit(solution)/shard_map/ppermute | solution.py:21
  379.8 21.5 %all-to-all-start.2 = ((bf16[4,1,80,768]{3,2,1,0:T(8,128)(2,1)}), bf16[4,1,80,768]{3,2,1,0:T(8,128)(2,1)}, u32[]{:S(2)}, u32[]{:S(2)}) async-start(bf16[4,1,80,768]{3,2,1,0:T(8,128)(2,1)} %bitcast.1400), calls=%async_computation.2 | async-start | bytes 983040 | tf_op jit(solution)/shard_map/all_to_all | solution.py:123
  385.9 68.7 %collective-permute-start.3 = (bf16[256,8]{0,1:T(8,128)(2,1)}, bf16[256,8]{0,1:T(8,128)(2,1)}, u32[]{:S(2)}, u32[]{:S(2)}) collective-permute-start(bf16[256,8]{0,1:T(8,128)(2,1)} %get-tuple-element.139), channel_id=1, source_target_pairs={{0,16},{1,17},{2,18},{3,19},{4,20},{5,21},{6,22},{7,23},{8,24},{9,... | collective-permute-start | bytes 12296 | tf_op jit(solution)/shard_map/ppermute | solution.py:21
  466.6 17.7 %all-to-all-start.4 = ((bf16[4,1,80,768]{3,2,1,0:T(8,128)(2,1)}), bf16[4,1,80,768]{3,2,1,0:T(8,128)(2,1)}, u32[]{:S(2)}, u32[]{:S(2)}) async-start(bf16[4,1,80,768]{3,2,1,0:T(8,128)(2,1)} %bitcast.1399), calls=%async_computation.4 | async-start | bytes 983040 | tf_op jit(solution)/shard_map/all_to_all | solution.py:123
  484.4 33.5 %all-to-all-start.6 = ((bf16[4,1,80,768]{3,2,1,0:T(8,128)(2,1)}), bf16[4,1,80,768]{3,2,1,0:T(8,128)(2,1)}, u32[]{:S(2)}, u32[]{:S(2)}) async-start(bf16[4,1,80,768]{3,2,1,0:T(8,128)(2,1)} %bitcast.1444), calls=%async_computation.6 | async-start | bytes 983040 | tf_op jit(solution)/shard_map/all_to_all | solution.py:222
  517.9 18.9 %all-to-all-start.5 = ((bf16[4,1,80,768]{3,2,1,0:T(8,128)(2,1)}), bf16[4,1,80,768]{3,2,1,0:T(8,128)(2,1)}, u32[]{:S(2)}, u32[]{:S(2)}) async-start(bf16[4,1,80,768]{3,2,1,0:T(8,128)(2,1)} %fusion.175), calls=%async_computation.5 | async-start | bytes 983040 | tf_op jit(solution)/shard_map/all_to_all | solution.py:137
  568.1 12.3 collective-permute-start.5
  576.3 13.1 all-to-all-start.8
  581.2 70.9 %collective-permute-start.7 = (bf16[256,8]{0,1:T(8,128)(2,1)}, bf16[256,8]{0,1:T(8,128)(2,1)}, u32[]{:S(2)}, u32[]{:S(2)}) collective-permute-start(bf16[256,8]{0,1:T(8,128)(2,1)} %get-tuple-element.249), channel_id=1, source_target_pairs={{16,0},{17,1},{18,2},{19,3},{20,4},{21,5},{22,6},{23,7},{24,8},{25... | collective-permute-start | bytes 12296 | tf_op jit(solution)/shard_map/ppermute | solution.py:21
  599.7 12.6 all-to-all-start.9
  642.9 13.1 all-to-all-start.10
  647.0 160.1 %reduce-scatter.29.cloned.1.call-start = ((), (), s32[]{:S(2)}) async-start(), calls=%async_computation.30 | async-start | bytes 417792
  649.7 251.0 %reduce-scatter.27.cloned.1.call-start = ((), (), s32[]{:S(2)}) async-start(), calls=%async_computation.29 | async-start | bytes 417792
  652.0 374.1 %reduce-scatter.25.cloned.1.call-start = ((), (), s32[]{:S(2)}) async-start(), calls=%async_computation.28 | async-start | bytes 417792
  669.8 482.4 %reduce-scatter.31.cloned.1.call-start = ((), (), s32[]{:S(2)}) async-start(), calls=%async_computation.31 | async-start | bytes 417792
  698.2 516.3 %reduce-scatter.23.cloned.1.call-start = ((), (), s32[]{:S(2)}) async-start(), calls=%async_computation.23 | async-start | bytes 3932160 | tf_op jit(solution)/shard_map/reduce_scatter | solution.py:480
  707.2 620.1 %reduce-scatter.21.cloned.1.call-start = ((), (), s32[]{:S(2)}) async-start(), calls=%async_computation.22 | async-start | bytes 7864320 | tf_op jit(solution)/shard_map/reduce_scatter | solution.py:480
  737.0 724.0 %reduce-scatter.19.cloned.1.call-start = ((), (), s32[]{:S(2)}) async-start(), calls=%async_computation.21 | async-start | bytes 2506752 | tf_op jit(solution)/shard_map/reduce_scatter | solution.py:474
  750.9 867.1 %reduce-scatter.17.cloned.1.call-start = ((), (), s32[]{:S(2)}) async-start(), calls=%async_computation.20 | async-start | bytes 7520256 | tf_op jit(solution)/shard_map/reduce_scatter | solution.py:474
  (287 other events, 3611.8 us)
Sparse Core Ops, SparseCore 0:
  10.8 77.5 all-gather.12
  91.2 56.7 all-gather.14
  149.5 116.7 all-gather.16
  267.7 61.9 all-gather.18
  652.2 122.4 reduce-scatter.28
  779.9 120.7 reduce-scatter.26
  905.4 120.6 reduce-scatter.24
  1031.5 120.6 reduce-scatter.30
  1155.1 59.3 reduce-scatter.22
  1216.6 110.7 reduce-scatter.20
  1332.9 128.0 reduce-scatter.18
  1467.6 150.2 reduce-scatter.16
where the time goes:
time: 1640 us; the launch traced here: 1630 us
  waiting for transfers between devices  890 us (54%)
  blocking collectives  220 us (13%)
  matrix products  219 us (13%)
  local copies, waits for them, and re-layouts  128 us (8%)
  other arithmetic  84.3 us (5%)
  starting transfers between devices  64.5 us (4%)
  between operations  18.9 us (1%)
    unnamed x16, waiting for transfers between devices  341 us
    reduce_scatter x2, waiting for transfers between devices, local(): lax.psum_scatter(weight_totals, ('expert', 'shard'), scatter_dimension=0,...  287 us
    reduce_scatter x2, waiting for transfers between devices, local(): lax.psum_scatter(as_sent(expert_totals), 'shard', scatter_dimension=1, ti...  171 us
    all_gather x1, blocking collectives, local(): lax.all_gather(local_pieces[4], ('expert', 'shard'), axis=0, tiled=True)  48.5 us
    all_gather x1, waiting for transfers between devices, local(): lax.all_gather(expert_pieces[1], 'shard', axis=1, tiled=True)  48.2 us
    dynamic_update_slice x58, other arithmetic, store_item(): lax.dynamic_update_index_in_dim(stack, jnp.where(in_range, update, curren...  47.4 us
    all_gather x1, blocking collectives, local(): lax.all_gather(local_pieces[2], ('expert', 'shard'), axis=0, tiled=True)  45.4 us
    all_gather x1, blocking collectives, local(): lax.all_gather(local_pieces[3], ('expert', 'shard'), axis=0, tiled=True)  44.5 us
  transfers between devices with their start and end apart: 32, of which 14 were waited for; matrix products, arithmetic and copies ran while one was open for 23% of the time, Pallas kernels for 0%

commit v1 on v0

v1 whole, which is shorter than its diff:
```python
import math

import jax
import jax.numpy as jnp
from jax import lax
from jax.experimental import pallas as pl
from jax.experimental.pallas import tpu as pltpu
from jax.sharding import PartitionSpec as P

HEADS = 12
HEAD = 64
TOP = 2
CHUNK = 256
LANES = 128
AT_PROJ = 16
AT_VEC = 24
AT_GAIN = 28
AT_MIX = 32

HIGH = lax.Precision.HIGHEST
norm_eps = 1e-06
masked_score = -1e30
F32 = jnp.float32
BF16 = jnp.bfloat16


def mm(a, b, contract=((1,), (0,)), precision=None):
    return lax.dot_general(a, b, (contract, ((), ())), precision=precision, preferred_element_type=F32)


NT = ((1,), (1,))
TN = ((0,), (0,))


def lane_of(rows, columns=LANES):
    return lax.broadcasted_iota(jnp.int32, (rows, columns), 1)


def inverse_norm(values):
    return lax.rsqrt(jnp.mean(values * values, axis=-1, keepdims=True) + norm_eps)


def norm_back(grad_unit, unit, inverse):
    return inverse * (grad_unit - unit * jnp.mean(grad_unit * unit, axis=-1, keepdims=True))


def roll(x, by):
    return jnp.roll(x, by, axis=1)


def turned(x, lane):
    return jnp.where(lane % HEAD < HEAD // 2, roll(x, LANES - HEAD // 2), roll(x, HEAD // 2))


def hi_lo(x):
    high = x.astype(BF16)
    return high, (x - high.astype(F32)).astype(BF16)


def attention_body(x, w_qkv, w_attn, gain_first, cosine, sine, seg_col, seg_row):
    seq_len, width = x.shape
    first_b = (x * inverse_norm(x) * gain_first).astype(BF16)
    place_q = lax.broadcasted_iota(jnp.int32, (seq_len, seq_len), 0)
    place_k = lax.broadcasted_iota(jnp.int32, (seq_len, seq_len), 1)
    allowed = (seg_col == seg_row) & (place_k <= place_q)
    lane = lane_of(seq_len)
    low_head = lane < HEAD
    parts_q, parts_k, parts_v, parts_a, parts_p = [], [], [], [], []
    for pair in range(width // LANES):
        at = pair * LANES
        q = mm(first_b, w_qkv[:, at : at + LANES])
        k = mm(first_b, w_qkv[:, width + at : width + at + LANES])
        v = mm(first_b, w_qkv[:, 2 * width + at : 2 * width + at + LANES]).astype(BF16)
        q = (q * cosine + turned(q, lane) * sine).astype(BF16)
        k = (k * cosine + turned(k, lane) * sine).astype(BF16)
        outs = []
        for keep in (low_head, ~low_head):
            scores = mm(jnp.where(keep, q, 0), k, NT) * (HEAD**-0.5)
            scores = jnp.where(allowed, scores, masked_score)
            scores = jnp.exp(scores - jnp.max(scores, axis=-1, keepdims=True))
            probs = (scores / jnp.sum(scores, axis=-1, keepdims=True)).astype(BF16)
            parts_p.append(probs)
            outs.append(mm(probs, v))
        parts_a.append(jnp.where(low_head, outs[0], outs[1]).astype(BF16))
        parts_q.append(q)
        parts_k.append(k)
        parts_v.append(v)
    attended = jnp.concatenate(parts_a, axis=1)
    qkv = jnp.concatenate(parts_q + parts_k + parts_v, axis=1)
    after = x + mm(attended, w_attn)
    return after, qkv, jnp.stack(parts_p), attended


def gating_body(after, r, small, mix, gain_second, ints, prio_row, nffn, nexp, capacity, slots):
    rows = after.shape[0]
    second = after * inverse_norm(after) * gain_second
    second_b = second.astype(BF16)
    lane = lane_of(rows)
    logits = mm(second_b, small)
    full = logits + mm(r, mix, precision=HIGH)
    inside = lane < nexp
    top = jnp.max(jnp.where(inside, full, -jnp.inf), axis=-1, keepdims=True)
    raised = jnp.where(inside, jnp.exp(jnp.where(inside, full, top) - top), 0.0)
    probs = raised / jnp.sum(raised, axis=-1, keepdims=True)
    other = jnp.where(lane % 2 == 0, roll(logits, LANES - 1), roll(logits, 1))
    bigger = jnp.maximum(logits, other)
    mine_e = jnp.exp(logits - bigger)
    mixes = mine_e / (mine_e + jnp.exp(other - bigger))
    before = (prio_row < ints[:, 2:3]).astype(BF16)
    route = (ints[:, 0:1], ints[:, 1:2])
    routed = (((lane == route[0]) | (lane == route[1])) & (lane < nffn)).astype(BF16)
    rank = mm(before, routed)
    columns = []
    dispatch = jnp.zeros((rows, slots), BF16)
    stride = slots // nffn
    for k in range(TOP):
        chosen = lane == route[k]
        gate = jnp.sum(jnp.where(chosen, probs, 0.0), axis=-1, keepdims=True)
        rank_k = jnp.sum(jnp.where(chosen, rank, 0.0), axis=-1, keepdims=True).astype(jnp.int32)
        kept = (route[k] < nffn) & (rank_k < capacity)
        slot = jnp.where(kept, route[k] * stride + rank_k, -1)
        dispatch = dispatch + (slot == lane_of(rows, slots)).astype(BF16)
        columns.append((gate, slot))
    buffer = mm(dispatch, second_b, TN).astype(BF16)
    packed = jnp.where(inside, probs, jnp.where((lane >= AT_PROJ) & (lane < AT_VEC), mixes, 0.0))
    packed = jnp.where(lane == AT_VEC, columns[0][0], packed)
    packed = jnp.where(lane == AT_VEC + 1, columns[1][0], packed)
    slot_pair = jnp.where(lane == 0, columns[0][1], columns[1][1])
    return full, packed, slot_pair, buffer


def extras(packed, ints, nffn, nconst):
    gates = (packed[:, AT_VEC : AT_VEC + 1], packed[:, AT_VEC + 1 : AT_VEC + 2])

    def of(expert):
        return sum(jnp.where(ints[:, k : k + 1] == expert, gates[k], 0.0) for k in range(TOP))

    def mixes(c):
        at = AT_PROJ + 2 * c
        return packed[:, at : at + 1], packed[:, at + 1 : at + 2]

    return gates, of(nffn + 1), [of(nffn + 2 + c) for c in range(nconst)], [mixes(c) for c in range(nconst)]


def combine_body(after, packed, slot_pair, ints, returned, gain_second, vec_rows, nffn):
    rows = after.shape[0]
    nconst = vec_rows.shape[0]
    second = after * inverse_norm(after) * gain_second
    gates, copied, const, mixes = extras(packed, ints, nffn, nconst)
    made = (returned[0].astype(F32) + returned[1].astype(F32)).astype(BF16)
    slot_lane = lane_of(rows, made.shape[0])
    picked = [mm((slot_pair[:, k : k + 1] == slot_lane).astype(BF16), made) for k in range(TOP)]
    coefficient = copied
    for c in range(nconst):
        coefficient = coefficient + const[c] * mixes[c][0]
    out = after + gates[0] * picked[0] + gates[1] * picked[1] + coefficient * second
    for c in range(nconst):
        out = out + (const[c] * mixes[c][1]) * vec_rows[c : c + 1]
    return out, [p.astype(BF16) for p in picked]


def expert_chunk(arrived, w_in):
    both = mm(arrived, w_in)
    gate, up = both[:, :CHUNK], both[:, CHUNK:]
    return gate, up, jax.nn.sigmoid(gate)


def expert_forward(arrived, w_in, w_out):
    total = 0.0
    for chunk in range(w_out.shape[0] // CHUNK):
        gate, up, sig = expert_chunk(arrived, w_in[:, 2 * CHUNK * chunk : 2 * CHUNK * (chunk + 1)])
        hidden = (gate * sig * up).astype(BF16)
        total = total + mm(hidden, w_out[CHUNK * chunk : CHUNK * (chunk + 1)])
    return total.astype(BF16)


def expert_backward(grad_made, arrived, w_in, w_out):
    total = 0.0
    grads_in, grads_out = [], []
    for chunk in range(w_out.shape[0] // CHUNK):
        piece = w_in[:, 2 * CHUNK * chunk : 2 * CHUNK * (chunk + 1)]
        gate, up, sig = expert_chunk(arrived, piece)
        hidden = (gate * sig * up).astype(BF16)
        grad_hidden = mm(grad_made, w_out[CHUNK * chunk : CHUNK * (chunk + 1)], NT)
        grads_out.append(mm(hidden, grad_made, TN).astype(BF16))
        grad_gate = grad_hidden * up * sig * (1.0 + gate * (1.0 - sig))
        grad_up = grad_hidden * gate * sig
        grad_both = jnp.concatenate([grad_gate, grad_up], axis=1).astype(BF16)
        grads_in.append(mm(arrived, grad_both, TN).astype(BF16))
        total = total + mm(grad_both, piece, NT)
    return total.astype(BF16), jnp.concatenate(grads_in, axis=1), jnp.concatenate(grads_out, axis=0)


def return_body(grad_y, packed, slot_pair, slots):
    rows = grad_y.shape[0]
    slot_lane = lane_of(rows, slots)
    total = 0.0
    for k in range(TOP):
        gate = packed[:, AT_VEC + k : AT_VEC + k + 1]
        table = (slot_pair[:, k : k + 1] == slot_lane).astype(BF16)
        total = total + mm(table, (gate * grad_y).astype(BF16), TN)
    return total.astype(BF16)


def moe_back_body(
    grad_y, grad_log_in, after, packed, slot_pair, ints, picked, returned, r, small, mix, gain_second, vec_rows, nffn, nexp
):
    rows = grad_y.shape[0]
    nconst = vec_rows.shape[0]
    lane = lane_of(rows)
    inverse = inverse_norm(after)
    unit = after * inverse
    second = unit * gain_second
    second_b = second.astype(BF16)
    gates, copied, const, mixes = extras(packed, ints, nffn, nconst)
    grad_buffer = (returned[0].astype(F32) + returned[1].astype(F32)).astype(BF16)
    slot_lane = lane_of(rows, grad_buffer.shape[0])
    dispatch = sum((slot_pair[:, k : k + 1] == slot_lane).astype(BF16) for k in range(TOP))
    grad_second = mm(dispatch, grad_buffer)
    along_second = jnp.sum(grad_y * second, axis=-1, keepdims=True)
    coefficient = copied
    grad_extra = [(nffn + 1, along_second)]
    grad_lanes = jnp.zeros((rows, LANES), F32)
    vec_grads = []
    for c in range(nconst):
        along = jnp.sum(grad_y * vec_rows[c : c + 1], axis=-1, keepdims=True)
        m0, m1 = mixes[c]
        coefficient = coefficient + const[c] * m0
        grad_extra.append((nffn + 2 + c, m0 * along_second + m1 * along))
        d0, d1 = const[c] * along_second, const[c] * along
        mean = m0 * d0 + m1 * d1
        at = AT_PROJ + 2 * c
        grad_lanes = jnp.where(lane == at, m0 * (d0 - mean), grad_lanes)
        grad_lanes = jnp.where(lane == at + 1, m1 * (d1 - mean), grad_lanes)
        vec_grads.append(jnp.sum(grad_y * (const[c] * m1), axis=0, keepdims=True))
    grad_second = grad_second + coefficient * grad_y
    grad_probs = jnp.zeros((rows, LANES), F32)
    for k in range(TOP):
        grad_gate = jnp.sum(picked[k].astype(F32) * grad_y, axis=-1, keepdims=True)
        for expert, value in grad_extra:
            grad_gate = grad_gate + jnp.where(ints[:, k : k + 1] == expert, value, 0.0)
        grad_probs = grad_probs + jnp.where(lane == ints[:, k : k + 1], grad_gate, 0.0)
    probs = jnp.where(lane < nexp, packed, 0.0)
    grad_logits = probs * (grad_probs - jnp.sum(probs * grad_probs, axis=-1, keepdims=True)) + grad_log_in
    grad_mix = mm(r, grad_logits, TN, HIGH)
    grad_r = mm(grad_logits, mix, NT, HIGH)
    high, low = hi_lo(jnp.where(lane < nexp, grad_logits, grad_lanes))
    small_rows = mm(high, second_b, TN) + mm(low, second_b, TN)
    grad_second = grad_second + mm(high, small, NT) + mm(low, small, NT)
    grad_gain = jnp.sum(grad_second * unit, axis=0, keepdims=True)
    grad_after = grad_y + norm_back(grad_second * gain_second, unit, inverse)
    row = lax.broadcasted_iota(jnp.int32, small_rows.shape, 0)
    small_rows = jnp.where(row < AT_VEC, small_rows, 0.0)
    for c in range(nconst):
        small_rows = jnp.where(row == AT_VEC + c, vec_grads[c], small_rows)
    small_rows = jnp.where(row == AT_GAIN + 1, grad_gain, small_rows)
    return grad_after, grad_r, grad_mix, small_rows


def attention_back_body(grad_after, x, qkv, probs_att, attended, small_rows, w_qkv, w_attn, gain_first, cosine, sine):
    seq_len, width = x.shape
    inverse = inverse_norm(x)
    unit = x * inverse
    first_b = (unit * gain_first).astype(BF16)
    grad_branch = grad_after.astype(BF16)
    grad_w_attn = mm(attended, grad_branch, TN).astype(BF16)
    grad_attended = mm(grad_branch, w_attn, NT).astype(BF16)
    lane = lane_of(seq_len)
    low_head = lane < HEAD
    scale = HEAD**-0.5
    parts_q, parts_k, parts_v = [], [], []
    for pair in range(width // LANES):
        at = pair * LANES
        q = qkv[:, at : at + LANES]
        k = qkv[:, width + at : width + at + LANES]
        v = qkv[:, 2 * width + at : 2 * width + at + LANES]
        g = grad_attended[:, at : at + LANES]
        dq, dk, dv = [], [], []
        for half, keep in enumerate((low_head, ~low_head)):
            probs = probs_att[2 * pair + half]
            grad_p = mm(jnp.where(keep, g, 0), v, NT)
            p = probs.astype(F32)
            grad_s = (p * (grad_p - jnp.sum(p * grad_p, axis=-1, keepdims=True))).astype(BF16)
            dv.append(mm(probs, g, TN))
            dq.append(mm(grad_s, k))
            dk.append(mm(grad_s, q, TN))
        dq = jnp.where(low_head, dq[0], dq[1]) * scale
        dk = jnp.where(low_head, dk[0], dk[1]) * scale
        parts_q.append((dq * cosine - turned(dq, lane) * sine).astype(BF16))
        parts_k.append((dk * cosine - turned(dk, lane) * sine).astype(BF16))
        parts_v.append(jnp.where(low_head, dv[0], dv[1]).astype(BF16))
    grad_qkv = jnp.concatenate(parts_q + parts_k + parts_v, axis=1)
    grad_w_qkv = mm(first_b, grad_qkv, TN).astype(BF16)
    grad_first = mm(grad_qkv, w_qkv, NT)
    grad_gain = jnp.sum(grad_first * unit, axis=0, keepdims=True)
    grad_x = grad_after + norm_back(grad_first * gain_first, unit, inverse)
    row = lax.broadcasted_iota(jnp.int32, small_rows.shape, 0)
    small_rows = jnp.where(row == AT_GAIN, grad_gain, small_rows)
    return grad_x, grad_w_qkv, grad_w_attn, small_rows.T


def local(
    x_in,
    cotangent,
    gate_prev,
    segments,
    routes,
    priority,
    attn_qkv,
    attn_out,
    router,
    const_proj,
    const_vec,
    gains,
    gate_mix,
    expert_in,
    expert_out,
):
    seq_len, width = x_in.shape[2:]
    nexp = gate_prev.shape[-1]
    owners, pieces = lax.axis_size("expert"), lax.axis_size("shard")
    nffn = owners * expert_in.shape[1]
    nconst = const_vec.shape[-1]
    capacity = (5 * TOP * seq_len + 4 * nexp - 1) // (4 * nexp)
    room = -(-capacity // 16) * 16
    slots = nffn * room
    core = lax.axis_index("section")
    first_core = core == 0

    def swap(item):
        return lax.ppermute(item, "section", [(0, 1), (1, 0)])

    def mine(stack, axis=0):
        return lax.dynamic_index_in_dim(stack, core, axis, keepdims=False)

    def others(stack, axis=0):
        return lax.dynamic_index_in_dim(stack, 1 - core, axis, keepdims=False)

    def by_section(own, other):
        return jnp.where(first_core, own, other), jnp.where(first_core, other, own)

    in_rows, columns = expert_in.shape[2:]
    hidden_here = expert_out.shape[2] // 2
    chunks = pieces * hidden_here // CHUNK
    w_in = expert_in[0, 0].reshape(in_rows, 2, pieces, 2, hidden_here)

    def as_chunks(half):
        half = half.reshape(in_rows, 2, chunks, CHUNK)
        return jnp.swapaxes(half, 1, 2).reshape(in_rows, columns // 2)

    w_out = expert_out[0, 0].reshape(2, hidden_here, width)
    ins = by_section(as_chunks(mine(w_in, 3)), swap(as_chunks(others(w_in, 3))))
    outs = by_section(mine(w_out), swap(others(w_out)))
    experts = [
        (
            lax.all_gather(ins[s], "shard", axis=0, tiled=True),
            lax.all_gather(outs[s], "shard", axis=0, tiled=True),
        )
        for s in range(2)
    ]
    rows = attn_qkv.shape[1]

    def lanes(array, upto):
        return jnp.pad(array, ((0, 0), (0, upto - array.shape[1])))

    small = jnp.concatenate(
        [
            lanes(router[0], AT_PROJ),
            lanes(const_proj[0], AT_VEC - AT_PROJ),
            lanes(const_vec[0], AT_GAIN - AT_VEC),
            lanes(gains[0], LANES - AT_GAIN),
        ],
        axis=1,
    )
    shared = jnp.concatenate([attn_qkv[0], attn_out[0], small], axis=1)
    shared = lax.all_gather(shared, ("expert", "shard"), axis=0, tiled=True)
    shared = by_section(shared, swap(shared))
    mix_own = jnp.pad(gate_mix[0], ((0, LANES - nexp), (0, LANES - nexp)))
    mix_all = by_section(mix_own, swap(mix_own))
    ints_own = jnp.concatenate([routes[0, :, 0], priority[0, :, 0, :, None]], axis=-1)
    ints_all = by_section(mine(ints_own), swap(others(ints_own)))
    x_first = mine(x_in[:, 0]).astype(F32)
    r_first = jnp.pad(mine(gate_prev[:, 0]).astype(F32), ((0, 0), (0, LANES - nexp)))
    upstream = mine(cotangent[:, 0])
    seg = mine(segments[:, 0])
    place = lax.iota(jnp.int32, seq_len)
    start = jnp.sum((seg[None, :] < seg[:, None]).astype(F32), axis=1)
    angles = (place.astype(F32) - start)[:, None] * jnp.exp(
        lax.iota(F32, HEAD // 2) * (-2.0 * math.log(10000.0) / HEAD)
    )[None, :]
    cosine, sine = jnp.cos(angles), jnp.sin(angles)
    cosine = jnp.concatenate([cosine] * 4, axis=1)
    sine = jnp.concatenate([-sine, sine, -sine, sine], axis=1)

    def to_owners(blocks):
        blocks = lax.all_to_all(
            blocks.reshape(owners, room, width), "expert", split_axis=0, concat_axis=0, tiled=True
        ).reshape(slots, width)
        return jnp.concatenate(by_section(blocks, swap(blocks)), axis=0)

    def to_tokens(blocks):
        blocks = blocks.reshape(2, slots, width)

        def back(part):
            return lax.all_to_all(
                part.reshape(owners, room, width), "expert", split_axis=0, concat_axis=0, tiled=True
            ).reshape(slots, width)

        return back(mine(blocks)), back(swap(others(blocks)))

    kept = []
    x, r = x_first, r_first
    results = []
    for s in range(2):
        packed_w = shared[s]
        w_qkv = packed_w[:, : 3 * width]
        w_attn = packed_w[:, 3 * width : 4 * width]
        w_small = packed_w[:, 4 * width :]
        small_t = w_small.astype(F32).T
        gain = (small_t[AT_GAIN : AT_GAIN + 1], small_t[AT_GAIN + 1 : AT_GAIN + 2])
        vec_rows = small_t[AT_VEC : AT_VEC + nconst]
        ints = ints_all[s]
        after, qkv, probs_att, attended = attention_body(
            x, w_qkv, w_attn, gain[0], cosine, sine, seg[:, None], seg[None, :]
        )
        logits, packed, slot_pair, buffer = gating_body(
            after, r, w_small, mix_all[s], gain[1], ints, ints[:, 2][None], nffn, nexp, capacity, slots
        )
        arrived = to_owners(buffer)
        returned = to_tokens(expert_forward(arrived, *experts[s]))
        out, picked = combine_body(after, packed, slot_pair, ints, returned, gain[1], vec_rows, nffn)
        kept.append(
            (x, r, after, qkv, probs_att, attended, packed, slot_pair, arrived, picked, w_qkv, w_attn, w_small, gain, vec_rows, ints)
        )
        sent = out.astype(BF16)
        results.append(sent)
        x = sent.astype(F32)
        r = jnp.where(lane_of(seq_len) < nexp, logits, 0.0).astype(BF16).astype(F32)
    grad_y = upstream
    grad_log = jnp.zeros((seq_len, LANES), F32)
    x_grads, r_grads, sums = [None, None], [None, None], [None, None]
    for s in (1, 0):
        x, r, after, qkv, probs_att, attended, packed, slot_pair, arrived, picked, w_qkv, w_attn, w_small, gain, vec_rows, ints = kept[s]
        grad_made = to_owners(return_body(grad_y, packed, slot_pair, slots))
        grad_arrived, grad_in, grad_out = expert_backward(grad_made, arrived, *experts[s])
        in_sum = lax.psum_scatter(grad_in, "shard", scatter_dimension=0, tiled=True)
        out_sum = lax.psum_scatter(grad_out, "shard", scatter_dimension=0, tiled=True)
        returned = to_tokens(grad_arrived)
        grad_after, grad_r, grad_mix, small_rows = moe_back_body(
            grad_y, grad_log, after, packed, slot_pair, ints, picked, returned, r, w_small, mix_all[s], gain[1], vec_rows, nffn, nexp
        )
        grad_x, grad_w_qkv, grad_w_attn, small_grads = attention_back_body(
            grad_after, x, qkv, probs_att, attended, small_rows, w_qkv, w_attn, gain[0], cosine, sine
        )
        x_grads[s] = grad_x
        r_grads[s] = grad_r[:, :nexp]
        mix_lanes = -(-nexp * nexp // rows)
        mix_flat = jnp.pad(grad_mix[:nexp, :nexp].reshape(-1), (0, rows * mix_lanes - nexp * nexp)).reshape(rows, mix_lanes)
        mix_tile = jnp.tile(mix_flat, (owners * pieces, 1))
        small_grads = small_grads.at[:, AT_MIX : AT_MIX + mix_lanes].set(mix_tile)
        grads = jnp.concatenate([grad_w_qkv, grad_w_attn, small_grads.astype(BF16)], axis=1)
        sums[s] = (grads, in_sum, out_sum)
        grad_y = grad_x.astype(BF16).astype(F32)
        grad_log = grad_r.astype(BF16).astype(F32)
    shared_own = jnp.where(first_core, sums[0][0], sums[1][0])
    shared_other = jnp.where(first_core, sums[1][0], sums[0][0])
    shared_sum = (shared_own.astype(F32) + swap(shared_other).astype(F32)).astype(BF16)
    shared_sum = lax.psum_scatter(shared_sum, ("expert", "shard"), scatter_dimension=0, tiled=True).astype(F32)

    def halves(index):
        own = jnp.where(first_core, sums[0][index], sums[1][index])
        got = swap(jnp.where(first_core, sums[1][index], sums[0][index]))
        return jnp.where(first_core, own, got).astype(F32), jnp.where(first_core, got, own).astype(F32)

    in_halves = [
        jnp.swapaxes(half.reshape(in_rows, chunks, 2, CHUNK), 1, 2).reshape(in_rows, 2, pieces, hidden_here)
        for half in halves(1)
    ]
    in_grad = jnp.stack(in_halves, axis=3).reshape(in_rows, columns)
    out_grad = jnp.concatenate(halves(2), axis=0)

    def both_batches(pair):
        own = jnp.where(first_core, pair[0], pair[1])
        got = swap(jnp.where(first_core, pair[1], pair[0]))
        return jnp.stack(by_section(own, got))[None, :, None]

    small_sum = shared_sum[:, 4 * width :]
    mix_grad = small_sum[:, AT_MIX : AT_MIX + mix_lanes].reshape(-1)[: nexp * nexp].reshape(nexp, nexp)
    return (
        both_batches(results),
        both_batches(x_grads),
        both_batches(r_grads),
        shared_sum[None, :, : 3 * width],
        shared_sum[None, :, 3 * width : 4 * width],
        small_sum[None, :, :nexp],
        small_sum[None, :, AT_PROJ : AT_PROJ + const_proj.shape[-1]],
        small_sum[None, :, AT_VEC : AT_VEC + nconst],
        small_sum[None, :, AT_GAIN : AT_GAIN + 2],
        mix_grad[None],
        in_grad[None, None],
        out_grad[None, None],
    )


def solution(mesh):
    placed = (
        P(None, ("expert", "shard"), None, None),
        P(None, ("expert", "shard"), None, None),
        P(None, ("expert", "shard"), None, None),
        P(None, ("expert", "shard"), None),
        P("section", None, ("expert", "shard"), None, None),
        P("section", None, ("expert", "shard"), None),
        P("section", ("expert", "shard"), None),
        P("section", ("expert", "shard"), None),
        P("section", ("expert", "shard"), None),
        P("section", ("expert", "shard"), None),
        P("section", ("expert", "shard"), None),
        P("section", ("expert", "shard"), None),
        P("section", None, None),
        P("section", "expert", "shard", None),
        P("section", "expert", "shard", None),
    )
    return jax.shard_map(
        local,
        mesh=mesh,
        in_specs=placed,
        out_specs=(
            P("section", None, ("expert", "shard"), None, None),
            P("section", None, ("expert", "shard"), None, None),
            P("section", None, ("expert", "shard"), None, None),
            P("section", ("expert", "shard"), None),
            P("section", ("expert", "shard"), None),
            P("section", ("expert", "shard"), None),
            P("section", ("expert", "shard"), None),
            P("section", ("expert", "shard"), None),
            P("section", ("expert", "shard"), None),
            P("section", None, None),
            P("section", "expert", "shard", None),
            P("section", "expert", "shard", None),
        ),
        check_vma=False,
    )
```

time: 1640 us -> 814 us (0.50)
  waiting for transfers between devices: 890 us -> 274 us
  blocking collectives: 220 us -> 9.58 us
  Pallas kernels: 0 us -> 48.8 us
  local copies, waits for them, and re-layouts: 128 us -> 80.3 us
  other arithmetic: 84.3 us -> 123 us
  matrix products: 219 us -> 197 us
  starting transfers between devices: 64.5 us -> 47.4 us
    unnamed x16 -> x10, waiting for transfers between devices: 341 us -> 0.17 us
    reduce_scatter x4 -> x5, waiting for transfers between devices: 459 us -> 143 us  [the longest x1 131 us: local(): lax.psum_scatter(shared_sum, ('expert', 'shard'), scatter_dimension=0, ti...]
    all_gather x4 -> x0, blocking collectives: 181 us -> none  [the longest x1 48.5 us: local(): lax.all_gather(local_pieces[4], ('expert', 'shard'), axis=0, tiled=True)]
    unnamed x0 -> x24, Pallas kernels: none -> 48.8 us
    dynamic_update_slice x58 -> x0, other arithmetic: 47.4 us -> none  [store_item(): lax.dynamic_update_index_in_dim(stack, jnp.where(in_range, update, curren...]
    psum x1 -> x0, blocking collectives: 39.3 us -> none  [local(): mix_sum = lax.psum(mix_total, ('expert', 'shard'))]
    reduce_sum x34 -> x32, other arithmetic: 11.8 us -> 40.6 us  [the longest x24 36.3 us: attention_body(): probs = (scores / jnp.sum(scores, axis=-1, keepdims=True)).astype(BF16)]
    select_n x3 -> x21, other arithmetic: 0.07 us -> 28.3 us  [the longest x4 11.9 us: by_section(): jnp.where(first_core, other, own)]
  transfers between devices with their start and end apart: 32 -> 40, of which waited for: 14 -> 18; matrix products, arithmetic and copies ran while one was open for 23% -> 44% of each run, Pallas kernels for 0% -> 6%
where the time goes in v1:
time: 814 us; the launch traced here: 803 us
  waiting for transfers between devices  274 us (34%)
  matrix products  197 us (24%)
  other arithmetic  123 us (15%)
  local copies, waits for them, and re-layouts  80.3 us (10%)
  Pallas kernels  48.8 us (6%)
  starting transfers between devices  47.4 us (6%)
  between operations  23.6 us (3%)
  blocking collectives  9.58 us (1%)
    dot_general x244, matrix products, mm(): lax.dot_general(a, b, (contract, ((), ())), precision=precision, preferre...  197 us
    reduce_scatter x1, waiting for transfers between devices, local(): lax.psum_scatter(shared_sum, ('expert', 'shard'), scatter_dimension=0, ti...  131 us
    all_gather x1, waiting for transfers between devices, local(): shared = lax.all_gather(shared, ('expert', 'shard'), axis=0, tiled=True)  71.4 us
    unnamed x24, Pallas kernels  48.8 us
    reduce_sum x24, other arithmetic, attention_body(): probs = (scores / jnp.sum(scores, axis=-1, keepdims=True)).astype(BF16)  36.3 us
    all_to_all x8, starting transfers between devices, back(): lax.all_to_all(part.reshape(owners, room, width), 'expert', split_axis=0,...  31.1 us
    all_to_all x8, waiting for transfers between devices, back(): lax.all_to_all(part.reshape(owners, room, width), 'expert', split_axis=0,...  30.8 us
    unnamed x978, local copies, waits for them, and re-layouts  29.3 us
  transfers between devices with their start and end apart: 40, of which 18 were waited for; matrix products, arithmetic and copies ran while one was open for 44% of the time, Pallas kernels for 6%

profile of v1, /device:TPU:0, one launch (start us, length us, event | category | flops | bytes accessed | tf_op | source)
XLA Modules:
  0.0 803.2 jit_solution(11713718765901130162)
XLA Ops:
  25.8 71.4 %all-gather.6.cloned.1.call-done = bf16[768,3200]{1,0:T(8,128)(2,1)} async-done(((bf16[48,3200]{1,0:T(8,128)(2,1)}), bf16[768,3200]{1,0:T(8,128)(2,1)}) %all-gather.6.cloned.1.call-update) | async-done | bytes 4915216 | tf_op jit(solution)/shard_map/all_gather | solution.py:376
  99.2 6.0 collective-permute-done.5
  112.0 8.6 %broadcast_select_fusion.1 = (bf16[768,3200]{1,0:T(8,128)(2,1)}, bf16[768,3200]{1,0:T(8,128)(2,1)}) fusion(bf16[768,3200]{1,0:T(8,128)(2,1)} %collective-permute-done, bf16[768,3200]{1,0:T(8,128)(2,1)} %all-gather.6.cloned.1.call-done, pred[]{:T(512)S(6)} %eq.403), kind=kLoop, calls=%fused_computation.6 | loop fusion | flops 4915200 | bytes 19660800 | tf_op jit(solution)/shard_map/jit(_where)/select_n | solution.py:340
  196.3 6.5 all-to-all-done
  221.4 3.5 all-to-all-start.1
  225.8 7.6 all-to-all-done.1
  234.1 3.6 all-to-all-start.2
  239.9 5.4 all-to-all-done.2
  331.9 4.3 all-to-all-start.3
  350.3 4.1 all-to-all-start.6
  389.0 4.5 all-to-all-start.4
  403.6 4.2 all-to-all-start.5
  410.9 5.2 all-to-all-done.5
  416.1 4.1 all-to-all-start.7
  433.3 4.6 all-to-all-done.8
  471.7 9.6 %all_to_all.60 = bf16[4,80,768]{2,1,0:T(8,128)(2,1)S(1)} all-to-all(bf16[4,80,768]{2,1,0:T(8,128)(2,1)S(1)} %bitcast.488), channel_id=1, replica_groups=mesh['section'=2,'expert'=4,'shard'=4] {'expert'}, dimensions={0} | all-to-all | bytes 983040 | tf_op jit(solution)/shard_map/all_to_all | solution.py:396
  512.2 5.1 copy.1614
  559.4 4.1 all-to-all-start.11
  608.2 4.9 broadcast_select_fusion
  613.2 8.2 %collective-permute-done.16 = bf16[768,3200]{1,0:T(8,128)(2,1)S(1)} collective-permute-done((bf16[768,3200]{1,0:T(8,128)(2,1)S(1)}, bf16[768,3200]{1,0:T(8,128)(2,1)S(1)}, u32[]{:S(2)}, u32[]{:S(2)}) %collective-permute-start.16) | collective-permute-done | bytes 4915232 | tf_op jit(solution)/shard_map/ppermute | solution.py:331
  621.4 3.7 add_convert_fusion
  633.7 11.5 %reduce-scatter.16.cloned.1.call-done = bf16[192,2048]{1,0:T(8,128)(2,1)} async-done(((bf16[768,2048]{1,0:T(8,128)(2,1)}), bf16[192,2048]{1,0:T(8,128)(2,1)}) %reduce-scatter.16.cloned.1.call-update) | async-done | bytes 786448 | tf_op jit(solution)/shard_map/reduce_scatter | solution.py:446
  654.0 3.6 reshape.454
  657.7 131.1 %reduce-scatter.10.cloned.1.call-done = bf16[48,3200]{1,0:T(8,128)(2,1)} async-done(((bf16[768,3200]{1,0:T(8,128)(2,1)}), bf16[48,3200]{1,0:T(8,128)(2,1)}) %reduce-scatter.10.cloned.1.call-update) | async-done | bytes 307216 | tf_op jit(solution)/shard_map/reduce_scatter | solution.py:468
  (1672 shorter events, 454.1 us)
Async XLA Ops:
  7.2 90.0 %all-gather.6.cloned.1.call-start = ((), (), s32[]{:S(2)}) async-start(), calls=%async_computation.17 | async-start | bytes 5222400 | tf_op jit(solution)/shard_map/all_gather | solution.py:376
  12.2 193.4 %all-gather.8.cloned.1.call-start = ((), (), s32[]{:S(2)}) async-start(), calls=%async_computation.18 | async-start | bytes 3932160 | tf_op jit(solution)/shard_map/all_gather | solution.py:356
  25.8 191.3 %all-gather.10.cloned.1.call-start = ((), (), s32[]{:S(2)}) async-start(), calls=%async_computation.19 | async-start | bytes 1966080 | tf_op jit(solution)/shard_map/all_gather | solution.py:357
  97.2 14.8 %collective-permute-start = (bf16[768,3200]{1,0:T(8,128)(2,1)}, bf16[768,3200]{1,0:T(8,128)(2,1)}, u32[]{:S(2)}, u32[]{:S(2)}) collective-permute-start(bf16[768,3200]{1,0:T(8,128)(2,1)} %all-gather.6.cloned.1.call-done), channel_id=1, source_target_pairs={{0,16},{16,0},{1,17},{17,1},{2,18},{18,2},{3,19},{19,3},{4,20},{20... | collective-permute-start | bytes 14745608 | tf_op jit(solution)/shard_map/ppermute | solution.py:331
  97.2 13.4 %collective-permute-start.1 = (s32[256,3]{0,1:T(4,128)S(1)}, s32[256,3]{0,1:T(4,128)S(1)}, u32[]{:S(2)}, u32[]{:S(2)}) collective-permute-start(s32[256,3]{0,1:T(4,128)S(1)} %fusion.857), channel_id=1, source_target_pairs={{0,16},{16,0},{1,17},{17,1},{2,18},{18,2},{3,19},{19,3},{4,20},{20... | collective-permute-start | bytes 9224 | tf_op jit(solution)/shard_map/ppermute | solution.py:331
  97.8 13.5 %collective-permute-start.2 = (f32[128,128]{1,0:T(8,128)S(1)}, f32[128,128]{1,0:T(8,128)S(1)}, u32[]{:S(2)}, u32[]{:S(2)}) collective-permute-start(f32[128,128]{1,0:T(8,128)S(1)} %pad.44), channel_id=1, source_target_pairs={{0,16},{16,0},{1,17},{17,1},{2,18},{18,2},{3,19},{19,3},{4,20},{20... | collective-permute-start | bytes 196616 | tf_op jit(solution)/shard_map/ppermute | solution.py:331
  106.1 263.2 %all-gather.12.cloned.1.call-start = ((), (), s32[]{:S(2)}) async-start(), calls=%async_computation.20 | async-start | bytes 3932160 | tf_op jit(solution)/shard_map/all_gather | solution.py:356
  194.4 178.3 %all-gather.14.cloned.1.call-start = ((), (), s32[]{:S(2)}) async-start(), calls=%async_computation.21 | async-start | bytes 1966080 | tf_op jit(solution)/shard_map/all_gather | solution.py:357
  221.2 12.1 %collective-permute-start.6 = (bf16[320,768]{1,0:T(8,128)(2,1)}, bf16[320,768]{1,0:T(8,128)(2,1)S(1)}, u32[]{:S(2)}, u32[]{:S(2)}) collective-permute-start(bf16[320,768]{1,0:T(8,128)(2,1)} %get-tuple-element.253), channel_id=1, source_target_pairs={{0,16},{16,0},{1,17},{17,1},{2,18},{18,2},{3,19},{19,3},{4,20},{20... | collective-permute-start | bytes 1474568 | tf_op jit(solution)/shard_map/ppermute | solution.py:331
  221.4 11.9 %all-to-all-start.1 = ((bf16[4,80,768]{2,1,0:T(8,128)(2,1)}), bf16[4,80,768]{2,1,0:T(8,128)(2,1)S(1)}, u32[]{:S(2)}, u32[]{:S(2)}) async-start(bf16[4,80,768]{2,1,0:T(8,128)(2,1)} %bitcast.35), calls=%async_computation.1 | async-start | bytes 983040 | tf_op jit(solution)/shard_map/all_to_all | solution.py:405
  331.9 18.5 %all-to-all-start.3 = ((bf16[4,80,768]{2,1,0:T(8,128)(2,1)}), bf16[4,80,768]{2,1,0:T(8,128)(2,1)}, u32[]{:S(2)}, u32[]{:S(2)}) async-start(bf16[4,80,768]{2,1,0:T(8,128)(2,1)} %bitcast.493), calls=%async_computation.3 | async-start | bytes 983040 | tf_op jit(solution)/shard_map/all_to_all | solution.py:396
  388.5 15.1 %collective-permute-start.8 = (bf16[320,768]{1,0:T(8,128)(2,1)}, bf16[320,768]{1,0:T(8,128)(2,1)}, u32[]{:S(2)}, u32[]{:S(2)}) collective-permute-start(bf16[320,768]{1,0:T(8,128)(2,1)} %get-tuple-element.249), channel_id=1, source_target_pairs={{0,16},{16,0},{1,17},{17,1},{2,18},{18,2},{3,19},{19,3},{4,20},{20... | collective-permute-start | bytes 1474568 | tf_op jit(solution)/shard_map/ppermute | solution.py:331
  389.0 14.6 %all-to-all-start.4 = ((bf16[4,80,768]{2,1,0:T(8,128)(2,1)}), bf16[4,80,768]{2,1,0:T(8,128)(2,1)}, u32[]{:S(2)}, u32[]{:S(2)}) async-start(bf16[4,80,768]{2,1,0:T(8,128)(2,1)} %bitcast.479), calls=%async_computation.4 | async-start | bytes 983040 | tf_op jit(solution)/shard_map/all_to_all | solution.py:405
  400.6 27.2 %collective-permute-start.11 = (bf16[320,768]{1,0:T(8,128)(2,1)}, bf16[320,768]{1,0:T(8,128)(2,1)}, u32[]{:S(2)}, u32[]{:S(2)}) collective-permute-start(bf16[320,768]{1,0:T(8,128)(2,1)} %get-tuple-element.245), channel_id=1, source_target_pairs={{0,16},{16,0},{1,17},{17,1},{2,18},{18,2},{3,19},{19,3},{4,20},{20... | collective-permute-start | bytes 1474568 | tf_op jit(solution)/shard_map/ppermute | solution.py:331
  403.6 12.5 %all-to-all-start.5 = ((bf16[4,80,768]{2,1,0:T(8,128)(2,1)}), bf16[4,80,768]{2,1,0:T(8,128)(2,1)}, u32[]{:S(2)}, u32[]{:S(2)}) async-start(bf16[4,80,768]{2,1,0:T(8,128)(2,1)} %bitcast.59), calls=%async_computation.5 | async-start | bytes 983040 | tf_op jit(solution)/shard_map/all_to_all | solution.py:405
  407.8 224.5 %reduce-scatter.14.cloned.1.call-start = ((), (), s32[]{:S(2)}) async-start(), calls=%async_computation.24 | async-start | bytes 1966080 | tf_op jit(solution)/shard_map/reduce_scatter | solution.py:447
  431.3 201.0 %reduce-scatter.12.cloned.1.call-start = ((), (), s32[]{:S(2)}) async-start(), calls=%async_computation.23 | async-start | bytes 1966080 | tf_op jit(solution)/shard_map/reduce_scatter | solution.py:447
  486.8 146.9 %reduce-scatter.18.cloned.1.call-start = ((), (), s32[]{:S(2)}) async-start(), calls=%async_computation.26 | async-start | bytes 3932160 | tf_op jit(solution)/shard_map/reduce_scatter | solution.py:446
  542.2 17.1 %collective-permute-start.13 = (bf16[320,768]{1,0:T(8,128)(2,1)S(1)}, bf16[320,768]{1,0:T(8,128)(2,1)}, u32[]{:S(2)}, u32[]{:S(2)}) collective-permute-start(bf16[320,768]{1,0:T(8,128)(2,1)S(1)} %get-tuple-element.241), channel_id=1, source_target_pairs={{0,16},{16,0},{1,17},{17,1},{2,18},{18,2},{3,19},{19,3},{4,20},{20... | collective-permute-start | bytes 1474568 | tf_op jit(solution)/shard_map/ppermute | solution.py:331
  559.4 12.0 %all-to-all-start.11 = ((bf16[4,80,768]{2,1,0:T(8,128)(2,1)}), bf16[4,80,768]{2,1,0:T(8,128)(2,1)}, u32[]{:S(2)}, u32[]{:S(2)}) async-start(bf16[4,80,768]{2,1,0:T(8,128)(2,1)} %bitcast.94), calls=%async_computation.11 | async-start | bytes 983040 | tf_op jit(solution)/shard_map/all_to_all | solution.py:405
  563.5 81.6 %reduce-scatter.16.cloned.1.call-start = ((), (), s32[]{:S(2)}) async-start(), calls=%async_computation.25 | async-start | bytes 3932160 | tf_op jit(solution)/shard_map/reduce_scatter | solution.py:446
  568.6 220.1 %reduce-scatter.10.cloned.1.call-start = ((), (), s32[]{:S(2)}) async-start(), calls=%async_computation.22 | async-start | bytes 5222400 | tf_op jit(solution)/shard_map/reduce_scatter | solution.py:468
  631.1 15.3 %collective-permute-start.14 = (f32[256,768]{1,0:T(8,128)}, f32[256,768]{1,0:T(8,128)S(1)}, u32[]{:S(2)}, u32[]{:S(2)}) collective-permute-start(f32[256,768]{1,0:T(8,128)} %get-tuple-element.138), channel_id=1, source_target_pairs={{0,16},{16,0},{1,17},{17,1},{2,18},{18,2},{3,19},{19,3},{4,20},{20... | collective-permute-start | bytes 2359304 | tf_op jit(solution)/shard_map/ppermute | solution.py:331
  633.3 14.6 %collective-permute-start.18 = (bf16[256,768]{1,0:T(8,128)(2,1)S(1)}, bf16[256,768]{1,0:T(8,128)(2,1)S(1)}, u32[]{:S(2)}, u32[]{:S(2)}) collective-permute-start(bf16[256,768]{1,0:T(8,128)(2,1)S(1)} %broadcast_select_fusion.19), channel_id=1, source_target_pairs={{0,16},{16,0},{1,17},{17,1},{2,18},{18,2},{3,19},{19,3},{4,20},{20... | collective-permute-start | bytes 1179656 | tf_op jit(solution)/shard_map/ppermute | solution.py:331
  (502 other events, 4443.4 us)
Sparse Core Ops, SparseCore 0:
  12.3 84.8 all-gather.5
  99.3 62.0 all-gather.7
  163.6 35.7 all-gather.9
  201.4 62.3 all-gather.11
  265.8 35.7 all-gather.13
  411.2 35.4 reduce-scatter.13
  486.9 33.3 reduce-scatter.11
  522.7 59.2 reduce-scatter.17
  584.8 60.2 reduce-scatter.15
  650.2 138.4 reduce-scatter.9

commit v2 on v1

v2 whole, which is shorter than its diff:
```python
import functools
import math

import jax
import jax.numpy as jnp
from jax import lax
from jax.experimental import pallas as pl
from jax.experimental.pallas import tpu as pltpu
from jax.sharding import PartitionSpec as P

HEADS = 12
HEAD = 64
TOP = 2
CHUNK = 256
LANES = 128
AT_PROJ = 16
AT_VEC = 24
AT_GAIN = 28
AT_MIX = 32

HIGH = lax.Precision.HIGHEST
norm_eps = 1e-06
masked_score = -1e30
F32 = jnp.float32
BF16 = jnp.bfloat16


VMEM_BYTES = 56 * 1024 * 1024


def mm(a, b, contract=((1,), (0,)), precision=None):
    return lax.dot_general(a, b, (contract, ((), ())), precision=precision, preferred_element_type=F32)


NT = ((1,), (1,))
TN = ((0,), (0,))


def lane_of(rows, columns=LANES):
    return lax.broadcasted_iota(jnp.int32, (rows, columns), 1)


def inverse_norm(values):
    return lax.rsqrt(jnp.mean(values * values, axis=-1, keepdims=True) + norm_eps)


def norm_back(grad_unit, unit, inverse):
    return inverse * (grad_unit - unit * jnp.mean(grad_unit * unit, axis=-1, keepdims=True))


def roll(x, by):
    return pltpu.roll(x, by, 1)


def turned(x, lane):
    return jnp.where(lane % HEAD < HEAD // 2, roll(x, LANES - HEAD // 2), roll(x, HEAD // 2))


def hi_lo(x):
    high = x.astype(BF16)
    return high, (x - high.astype(F32)).astype(BF16)


def ones_where(condition):
    return jnp.where(condition, 1.0, 0.0).astype(BF16)


def small_rows_of(w, width):
    rows = w[:, 4 * width :].astype(F32).T
    return rows[AT_GAIN : AT_GAIN + 1], rows[AT_GAIN + 1 : AT_GAIN + 2], rows[AT_VEC:AT_GAIN]


def attention(x, w, gain_first, cosine, sine, seg_col, seg_row, qkv, probs_att, attended):
    seq_len, width = x.shape
    first_b = (x * inverse_norm(x) * gain_first).astype(BF16)
    place_q = lax.broadcasted_iota(jnp.int32, (seq_len, seq_len), 0)
    place_k = lax.broadcasted_iota(jnp.int32, (seq_len, seq_len), 1)
    bias = jnp.where((seg_col == seg_row) & (place_k <= place_q), 0.0, masked_score)
    lane = lane_of(seq_len)
    low_head = lane < HEAD
    for pair in range(width // LANES):
        at = pair * LANES
        q = mm(first_b, w[:, at : at + LANES])
        k = mm(first_b, w[:, width + at : width + at + LANES])
        v = mm(first_b, w[:, 2 * width + at : 2 * width + at + LANES]).astype(BF16)
        q = q * cosine + turned(q, lane) * sine
        k = (k * cosine + turned(k, lane) * sine).astype(BF16)
        outs = []
        for half in range(2):
            one = jnp.where(low_head if half == 0 else lane >= HEAD, q, 0.0).astype(BF16)
            scores = mm(one, k, NT) * (HEAD**-0.5) + bias
            scores = jnp.exp(scores - jnp.max(scores, axis=-1, keepdims=True))
            probs = (scores * (1.0 / jnp.sum(scores, axis=-1, keepdims=True))).astype(BF16)
            probs_att[2 * pair + half] = probs
            outs.append(mm(probs, v))
        attended[:, at : at + LANES] = jnp.where(low_head, outs[0], outs[1]).astype(BF16)
        qkv[:, at : at + LANES] = q.astype(BF16)
        qkv[:, width + at : width + at + LANES] = k
        qkv[:, 2 * width + at : 2 * width + at + LANES] = v
    return x + mm(attended[...], w[:, 3 * width : 4 * width])


def gating(after, r, small, mix, gain_second, ints, prio_row, dims, packed_ref, slot_ref, r_next, buffer):
    nffn, nexp, capacity, slots = dims
    rows = after.shape[0]
    second_b = (after * inverse_norm(after) * gain_second).astype(BF16)
    lane = lane_of(rows)
    logits = mm(second_b, small)
    full = logits + mm(r, mix, precision=HIGH)
    inside = lane < nexp
    full = jnp.where(inside, full, masked_score)
    raised = jnp.exp(full - jnp.max(full, axis=-1, keepdims=True))
    probs = raised / jnp.sum(raised, axis=-1, keepdims=True)
    other = jnp.where(lane % 2 == 0, roll(logits, LANES - 1), roll(logits, 1))
    bigger = jnp.maximum(logits, other)
    mine_e = jnp.exp(logits - bigger)
    mixes = mine_e / (mine_e + jnp.exp(other - bigger))
    before = ones_where(prio_row < ints[:, 2:3])
    route = (ints[:, 0:1], ints[:, 1:2])
    routed = ones_where(((lane == route[0]) | (lane == route[1])) & (lane < nffn))
    rank = mm(before, routed)
    gates, places = [], []
    dispatch = 0.0
    stride = slots // nffn
    for k in range(TOP):
        chosen = lane == route[k]
        gates.append(jnp.sum(jnp.where(chosen, probs, 0.0), axis=-1, keepdims=True))
        rank_k = jnp.sum(jnp.where(chosen, rank, 0.0), axis=-1, keepdims=True).astype(jnp.int32)
        kept = (route[k] < nffn) & (rank_k < capacity)
        places.append(jnp.where(kept, route[k] * stride + rank_k, -1))
        dispatch = dispatch + jnp.where(places[k] == lane_of(rows, slots), 1.0, 0.0)
    buffer[...] = mm(dispatch.astype(BF16), second_b, TN).astype(BF16)
    packed = jnp.where(inside, probs, jnp.where((lane >= AT_PROJ) & (lane < AT_VEC), mixes, 0.0))
    packed = jnp.where(lane == AT_VEC, gates[0], packed)
    packed_ref[...] = jnp.where(lane == AT_VEC + 1, gates[1], packed)
    slot_ref[...] = jnp.where(lane == 0, places[0], places[1])
    if r_next is not None:
        r_next[...] = jnp.where(inside, full, 0.0).astype(BF16)


def extras(packed, ints, nffn, nconst):
    gates = (packed[:, AT_VEC : AT_VEC + 1], packed[:, AT_VEC + 1 : AT_VEC + 2])

    def of(expert):
        return sum(jnp.where(ints[:, k : k + 1] == expert, gates[k], 0.0) for k in range(TOP))

    def mixes(c):
        at = AT_PROJ + 2 * c
        return packed[:, at : at + 1], packed[:, at + 1 : at + 2]

    return gates, of(nffn + 1), [of(nffn + 2 + c) for c in range(nconst)], [mixes(c) for c in range(nconst)]


def combine(after, packed, slot_pair, ints, parts, gain_second, vec_rows, dims, picked_ref):
    nffn, nexp, _, slots = dims
    nconst = nexp - nffn - 2
    rows = after.shape[0]
    second = after * inverse_norm(after) * gain_second
    gates, copied, const, mixes = extras(packed, ints, nffn, nconst)
    made = (parts[0][...].astype(F32) + parts[1][...].astype(F32)).astype(BF16)
    slot_lane = lane_of(rows, slots)
    coefficient = copied
    for c in range(nconst):
        coefficient = coefficient + const[c] * mixes[c][0]
    out = after + coefficient * second
    for k in range(TOP):
        picked = mm(ones_where(slot_pair[:, k : k + 1] == slot_lane), made)
        picked_ref[k] = picked.astype(BF16)
        out = out + gates[k] * picked
    for c in range(nconst):
        out = out + (const[c] * mixes[c][1]) * vec_rows[c : c + 1]
    return out


def give_back(grad_y, packed, slot_pair, dims, buffer):
    slots = dims[3]
    slot_lane = lane_of(grad_y.shape[0], slots)
    total = 0.0
    for k in range(TOP):
        gate = packed[:, AT_VEC + k : AT_VEC + k + 1]
        table = ones_where(slot_pair[:, k : k + 1] == slot_lane)
        total = total + mm(table, (gate * grad_y).astype(BF16), TN)
    buffer[...] = total.astype(BF16)


def moe_back(
    grad_y, grad_log_in, after, packed, slot_pair, ints, picked, parts, r, small, mix, gain_second, vec_rows, dims
):
    nffn, nexp, _, slots = dims
    nconst = nexp - nffn - 2
    rows = grad_y.shape[0]
    lane = lane_of(rows)
    inverse = inverse_norm(after)
    unit = after * inverse
    second = unit * gain_second
    second_b = second.astype(BF16)
    gates, copied, const, mixes = extras(packed, ints, nffn, nconst)
    grad_buffer = (parts[0][...].astype(F32) + parts[1][...].astype(F32)).astype(BF16)
    slot_lane = lane_of(rows, slots)
    dispatch = sum(jnp.where(slot_pair[:, k : k + 1] == slot_lane, 1.0, 0.0) for k in range(TOP))
    grad_second = mm(dispatch.astype(BF16), grad_buffer)
    along_second = jnp.sum(grad_y * second, axis=-1, keepdims=True)
    coefficient = copied
    grad_extra = [(nffn + 1, along_second)]
    grad_lanes = jnp.zeros((rows, LANES), F32)
    vec_grads = []
    for c in range(nconst):
        along = jnp.sum(grad_y * vec_rows[c : c + 1], axis=-1, keepdims=True)
        m0, m1 = mixes[c]
        coefficient = coefficient + const[c] * m0
        grad_extra.append((nffn + 2 + c, m0 * along_second + m1 * along))
        d0, d1 = const[c] * along_second, const[c] * along
        mean = m0 * d0 + m1 * d1
        at = AT_PROJ + 2 * c
        grad_lanes = jnp.where(lane == at, m0 * (d0 - mean), grad_lanes)
        grad_lanes = jnp.where(lane == at + 1, m1 * (d1 - mean), grad_lanes)
        vec_grads.append(jnp.sum(grad_y * (const[c] * m1), axis=0, keepdims=True))
    grad_second = grad_second + coefficient * grad_y
    grad_probs = jnp.zeros((rows, LANES), F32)
    for k in range(TOP):
        grad_gate = jnp.sum(picked[k].astype(F32) * grad_y, axis=-1, keepdims=True)
        for expert, value in grad_extra:
            grad_gate = grad_gate + jnp.where(ints[:, k : k + 1] == expert, value, 0.0)
        grad_probs = grad_probs + jnp.where(lane == ints[:, k : k + 1], grad_gate, 0.0)
    probs = jnp.where(lane < nexp, packed, 0.0)
    grad_logits = probs * (grad_probs - jnp.sum(probs * grad_probs, axis=-1, keepdims=True)) + grad_log_in
    grad_mix = mm(r, grad_logits, TN, HIGH)
    grad_r = mm(grad_logits, mix, NT, HIGH)
    high, low = hi_lo(jnp.where(lane < nexp, grad_logits, grad_lanes))
    small_rows = mm(high, second_b, TN) + mm(low, second_b, TN)
    grad_second = grad_second + mm(high, small, NT) + mm(low, small, NT)
    grad_gain = jnp.sum(grad_second * unit, axis=0, keepdims=True)
    grad_after = grad_y + norm_back(grad_second * gain_second, unit, inverse)
    row = lax.broadcasted_iota(jnp.int32, small_rows.shape, 0)
    small_rows = jnp.where(row < AT_VEC, small_rows, 0.0)
    for c in range(nconst):
        small_rows = jnp.where(row == AT_VEC + c, vec_grads[c], small_rows)
    small_rows = jnp.where(row == AT_GAIN + 1, grad_gain, small_rows)
    return grad_after, grad_r, grad_mix, small_rows


def attention_back(grad_after, x, qkv, probs_att, attended, small_rows, w, gain_first, cosine, sine, grads, grad_qkv):
    seq_len, width = x.shape
    inverse = inverse_norm(x)
    unit = x * inverse
    first_b = (unit * gain_first).astype(BF16)
    grad_branch = grad_after.astype(BF16)
    grads[:, 3 * width : 4 * width] = mm(attended[...], grad_branch, TN).astype(BF16)
    lane = lane_of(seq_len)
    low_head = lane < HEAD
    masks = (ones_where(low_head), ones_where(lane >= HEAD))
    scale = HEAD**-0.5
    for pair in range(width // LANES):
        at = pair * LANES
        q = qkv[:, at : at + LANES]
        k = qkv[:, width + at : width + at + LANES]
        v = qkv[:, 2 * width + at : 2 * width + at + LANES]
        g = mm(grad_branch, w[at : at + LANES, 3 * width : 4 * width], NT).astype(BF16)
        dq, dk, dv = [], [], []
        for half in range(2):
            probs = probs_att[2 * pair + half]
            grad_p = mm(g * masks[half], v, NT)
            p = probs.astype(F32)
            grad_s = (p * (grad_p - jnp.sum(p * grad_p, axis=-1, keepdims=True))).astype(BF16)
            dv.append(mm(probs, g, TN))
            dq.append(mm(grad_s, k))
            dk.append(mm(grad_s, q, TN))
        dq = jnp.where(low_head, dq[0], dq[1]) * scale
        dk = jnp.where(low_head, dk[0], dk[1]) * scale
        grad_qkv[:, at : at + LANES] = (dq * cosine - turned(dq, lane) * sine).astype(BF16)
        grad_qkv[:, width + at : width + at + LANES] = (dk * cosine - turned(dk, lane) * sine).astype(BF16)
        grad_qkv[:, 2 * width + at : 2 * width + at + LANES] = jnp.where(low_head, dv[0], dv[1]).astype(BF16)
    grads[:, : 3 * width] = mm(first_b, grad_qkv[...], TN).astype(BF16)
    grad_first = mm(grad_qkv[...], w[:, : 3 * width], NT)
    grad_gain = jnp.sum(grad_first * unit, axis=0, keepdims=True)
    grad_x = grad_after + norm_back(grad_first * gain_first, unit, inverse)
    row = lax.broadcasted_iota(jnp.int32, small_rows.shape, 0)
    small_rows = jnp.where(row == AT_GAIN, grad_gain, small_rows)
    grads[:, 4 * width :] = small_rows.T.astype(BF16)
    return grad_x


def attend_kernel(
    dims, x, r, w, mix, cosine, sine, seg_col, seg_row, ints, prio_row,
    after, qkv, probs_att, attended, packed, slot_pair, r_next, buffer,
):
    width = x.shape[1]
    gain_first, gain_second, _ = small_rows_of(w, width)
    after_v = attention(
        x[...].astype(F32), w, gain_first, cosine[...], sine[...], seg_col[...], seg_row[...], qkv, probs_att, attended
    )
    after[...] = after_v
    gating(
        after_v, r[...].astype(F32), w[:, 4 * width :], mix[...], gain_second, ints[...], prio_row[...], dims,
        packed, slot_pair, r_next, buffer,
    )


def combine_kernel(dims, after, packed, slot_pair, ints, part_0, part_1, w, out, picked):
    width = after.shape[1]
    _, gain_second, vec_rows = small_rows_of(w, width)
    out[...] = combine(
        after[...], packed[...], slot_pair[...], ints[...], (part_0, part_1), gain_second, vec_rows, dims, picked
    ).astype(BF16)


def give_back_kernel(dims, grad_y, packed, slot_pair, buffer):
    give_back(grad_y[...].astype(F32), packed[...], slot_pair[...], dims, buffer)


def back_kernel(
    dims, grad_y, grad_log, after, packed, slot_pair, ints, picked, part_0, part_1, r, w, mix,
    x, qkv, probs_att, attended, cosine, sine,
    grad_x, grad_r, grad_mix, grads, grad_qkv,
):
    width = x.shape[1]
    gain_first, gain_second, vec_rows = small_rows_of(w, width)
    grad_after, grad_r_v, grad_mix_v, small_rows = moe_back(
        grad_y[...].astype(F32), grad_log[...].astype(F32), after[...], packed[...], slot_pair[...], ints[...], picked,
        (part_0, part_1), r[...].astype(F32), w[:, 4 * width :], mix[...], gain_second, vec_rows, dims,
    )
    grad_r[...] = grad_r_v
    grad_mix[...] = grad_mix_v
    grad_x[...] = attention_back(
        grad_after, x[...].astype(F32), qkv, probs_att, attended, small_rows, w, gain_first, cosine[...], sine[...],
        grads, grad_qkv,
    )


def expert_kernel(arrived_0, arrived_1, w_in, w_out, made_0, made_1, total):
    slots = arrived_0.shape[0]
    step = pl.program_id(0)
    for part, arrived in enumerate((arrived_0, arrived_1)):
        at = part * slots
        both = mm(arrived[...], w_in[...])
        gate = both[:, :CHUNK]
        hidden = (gate * jax.nn.sigmoid(gate) * both[:, CHUNK:]).astype(BF16)
        more = mm(hidden, w_out[...])

        @pl.when(step == 0)
        def _():
            total[at : at + slots] = more

        @pl.when(step > 0)
        def _():
            total[at : at + slots] += more

    @pl.when(step == pl.num_programs(0) - 1)
    def _():
        made_0[...] = total[:slots].astype(BF16)
        made_1[...] = total[slots:].astype(BF16)


def expert_back_kernel(
    arrived_0, arrived_1, grad_0, grad_1, w_in, w_out, given_0, given_1, grad_in, grad_out, total
):
    slots = arrived_0.shape[0]
    step = pl.program_id(0)
    arrived = jnp.concatenate([arrived_0[...], arrived_1[...]], axis=0)
    grad_made = jnp.concatenate([grad_0[...], grad_1[...]], axis=0)
    both = mm(arrived, w_in[...])
    gate, up = both[:, :CHUNK], both[:, CHUNK:]
    sig = jax.nn.sigmoid(gate)
    hidden = (gate * sig * up).astype(BF16)
    grad_hidden = mm(grad_made, w_out[...], NT)
    grad_out[...] = mm(hidden, grad_made, TN).astype(BF16)
    grad_gate = grad_hidden * up * sig * (1.0 + gate * (1.0 - sig))
    grad_up = grad_hidden * gate * sig
    grad_both = jnp.concatenate([grad_gate, grad_up], axis=1).astype(BF16)
    grad_in[...] = mm(arrived, grad_both, TN).astype(BF16)
    more = mm(grad_both, w_in[...], NT)

    @pl.when(step == 0)
    def _():
        total[...] = more

    @pl.when(step > 0)
    def _():
        total[...] += more

    @pl.when(step == pl.num_programs(0) - 1)
    def _():
        given_0[...] = total[:slots].astype(BF16)
        given_1[...] = total[slots:].astype(BF16)


def shaped(shape, dtype):
    return jax.ShapeDtypeStruct(shape, dtype)


def run(kernel, out, args, flops=0):
    return pl.pallas_call(
        kernel,
        out_shape=out,
        compiler_params=pltpu.CompilerParams(vmem_limit_bytes=VMEM_BYTES),
        cost_estimate=pl.CostEstimate(flops=flops, bytes_accessed=8 << 20, transcendentals=0),
    )(*args)


def expert_specs(slots, width):
    whole = pl.BlockSpec((slots, width), lambda i: (0, 0))
    w_in = pl.BlockSpec((width, 2 * CHUNK), lambda i: (0, i))
    w_out = pl.BlockSpec((CHUNK, width), lambda i: (i, 0))
    return whole, w_in, w_out


def expert_forward(arrived, w_in, w_out):
    slots, width = arrived[0].shape
    whole, in_spec, out_spec = expert_specs(slots, width)
    return pl.pallas_call(
        expert_kernel,
        grid=(w_out.shape[0] // CHUNK,),
        in_specs=[whole, whole, in_spec, out_spec],
        out_specs=[whole, whole],
        out_shape=[shaped((slots, width), BF16)] * 2,
        scratch_shapes=[pltpu.VMEM((2 * slots, width), F32)],
        compiler_params=pltpu.CompilerParams(vmem_limit_bytes=VMEM_BYTES),
        cost_estimate=pl.CostEstimate(flops=12 * slots * width * w_out.shape[0], bytes_accessed=8 << 20, transcendentals=0),
    )(*arrived, w_in, w_out)


def expert_backward(grad_made, arrived, w_in, w_out):
    slots, width = arrived[0].shape
    whole, in_spec, out_spec = expert_specs(slots, width)
    return pl.pallas_call(
        expert_back_kernel,
        grid=(w_out.shape[0] // CHUNK,),
        in_specs=[whole, whole, whole, whole, in_spec, out_spec],
        out_specs=[whole, whole, in_spec, out_spec],
        out_shape=[shaped((slots, width), BF16)] * 2 + [shaped(w_in.shape, BF16), shaped(w_out.shape, BF16)],
        scratch_shapes=[pltpu.VMEM((2 * slots, width), F32)],
        compiler_params=pltpu.CompilerParams(vmem_limit_bytes=VMEM_BYTES),
        cost_estimate=pl.CostEstimate(flops=32 * slots * width * w_out.shape[0], bytes_accessed=16 << 20, transcendentals=0),
    )(*arrived, *grad_made, w_in, w_out)

def local(
    x_in,
    cotangent,
    gate_prev,
    segments,
    routes,
    priority,
    attn_qkv,
    attn_out,
    router,
    const_proj,
    const_vec,
    gains,
    gate_mix,
    expert_in,
    expert_out,
):
    seq_len, width = x_in.shape[2:]
    nexp = gate_prev.shape[-1]
    owners, pieces = lax.axis_size("expert"), lax.axis_size("shard")
    nffn = owners * expert_in.shape[1]
    nconst = const_vec.shape[-1]
    capacity = (5 * TOP * seq_len + 4 * nexp - 1) // (4 * nexp)
    room = -(-capacity // 16) * 16
    slots = nffn * room
    core = lax.axis_index("section")
    first_core = core == 0

    def swap(item):
        return lax.ppermute(item, "section", [(0, 1), (1, 0)])

    def mine(stack, axis=0):
        return lax.dynamic_index_in_dim(stack, core, axis, keepdims=False)

    def others(stack, axis=0):
        return lax.dynamic_index_in_dim(stack, 1 - core, axis, keepdims=False)

    def by_section(own, other):
        return jnp.where(first_core, own, other), jnp.where(first_core, other, own)

    in_rows, columns = expert_in.shape[2:]
    hidden_here = expert_out.shape[2] // 2
    chunks = pieces * hidden_here // CHUNK
    w_in = expert_in[0, 0].reshape(in_rows, 2, pieces, 2, hidden_here)

    def as_chunks(half):
        half = half.reshape(in_rows, 2, chunks, CHUNK)
        return jnp.swapaxes(half, 1, 2).reshape(in_rows, columns // 2)

    w_out = expert_out[0, 0].reshape(2, hidden_here, width)
    ins = by_section(as_chunks(mine(w_in, 3)), swap(as_chunks(others(w_in, 3))))
    outs = by_section(mine(w_out), swap(others(w_out)))
    experts = [
        (
            lax.all_gather(ins[s], "shard", axis=0, tiled=True),
            lax.all_gather(outs[s], "shard", axis=0, tiled=True),
        )
        for s in range(2)
    ]
    rows = attn_qkv.shape[1]

    def lanes(array, upto):
        return jnp.pad(array, ((0, 0), (0, upto - array.shape[1])))

    small = jnp.concatenate(
        [
            lanes(router[0], AT_PROJ),
            lanes(const_proj[0], AT_VEC - AT_PROJ),
            lanes(const_vec[0], AT_GAIN - AT_VEC),
            lanes(gains[0], LANES - AT_GAIN),
        ],
        axis=1,
    )
    shared = jnp.concatenate([attn_qkv[0], attn_out[0], small], axis=1)
    shared = lax.all_gather(shared, ("expert", "shard"), axis=0, tiled=True)
    shared = by_section(shared, swap(shared))
    mix_own = jnp.pad(gate_mix[0], ((0, LANES - nexp), (0, LANES - nexp)))
    mix_all = by_section(mix_own, swap(mix_own))
    ints_own = jnp.concatenate([routes[0, :, 0], priority[0, :, 0, :, None]], axis=-1)
    ints_all = by_section(mine(ints_own), swap(others(ints_own)))
    x_first = mine(x_in[:, 0])
    r_first = jnp.pad(mine(gate_prev[:, 0]), ((0, 0), (0, LANES - nexp)))
    upstream = mine(cotangent[:, 0])
    seg = mine(segments[:, 0])
    place = lax.iota(jnp.int32, seq_len)
    start = jnp.sum((seg[None, :] < seg[:, None]).astype(F32), axis=1)
    angles = (place.astype(F32) - start)[:, None] * jnp.exp(
        lax.iota(F32, HEAD // 2) * (-2.0 * math.log(10000.0) / HEAD)
    )[None, :]
    cosine, sine = jnp.cos(angles), jnp.sin(angles)
    cosine = jnp.concatenate([cosine] * 4, axis=1)
    sine = jnp.concatenate([-sine, sine, -sine, sine], axis=1)

    dims = (nffn, nexp, capacity, slots)
    heads = width // HEAD

    def exchanged(blocks):
        return lax.all_to_all(
            blocks.reshape(owners, room, width), "expert", split_axis=0, concat_axis=0, tiled=True
        ).reshape(slots, width)

    def to_owners(blocks):
        blocks = exchanged(blocks)
        return blocks, swap(blocks)

    def to_tokens(parts):
        return exchanged(parts[0]), exchanged(swap(parts[1]))

    kept = []
    x, r = x_first, r_first
    results = []
    seg_col, seg_row = seg[:, None], seg[None, :]
    for s in range(2):
        w, ints = shared[s], ints_all[s]
        after, qkv, probs_att, attended, packed, slot_pair, r_next, buffer = run(
            functools.partial(attend_kernel, dims),
            [
                shaped((seq_len, width), F32),
                shaped((seq_len, 3 * width), BF16),
                shaped((heads, seq_len, seq_len), BF16),
                shaped((seq_len, width), BF16),
                shaped((seq_len, LANES), F32),
                shaped((seq_len, LANES), jnp.int32),
                shaped((seq_len, LANES), BF16),
                shaped((slots, width), BF16),
            ],
            (x, r, w, mix_all[s], cosine, sine, seg_col, seg_row, ints, ints[:, 2][None]),
            flops=2 << 30,
        )
        arrived = to_owners(buffer)
        parts = to_tokens(expert_forward(arrived, *experts[s]))
        out, picked = run(
            functools.partial(combine_kernel, dims),
            [shaped((seq_len, width), BF16), shaped((TOP, seq_len, width), BF16)],
            (after, packed, slot_pair, ints, *parts, w),
        )
        kept.append((x, r, w, ints, after, qkv, probs_att, attended, packed, slot_pair, arrived, picked))
        results.append(out)
        x, r = out, r_next
    grad_y = upstream
    grad_log = jnp.zeros((seq_len, LANES), F32)
    x_grads, r_grads, sums = [None, None], [None, None], [None, None]
    for s in (1, 0):
        x, r, w, ints, after, qkv, probs_att, attended, packed, slot_pair, arrived, picked = kept[s]
        (buffer,) = run(
            functools.partial(give_back_kernel, dims),
            [shaped((slots, width), BF16)],
            (grad_y, packed, slot_pair),
        )
        given_0, given_1, grad_in, grad_out = expert_backward(to_owners(buffer), arrived, *experts[s])
        in_sum = lax.psum_scatter(grad_in, "shard", scatter_dimension=0, tiled=True)
        out_sum = lax.psum_scatter(grad_out, "shard", scatter_dimension=0, tiled=True)
        parts = to_tokens((given_0, given_1))
        grad_x, grad_r, grad_mix, grads, _ = run(
            functools.partial(back_kernel, dims),
            [
                shaped((seq_len, width), F32),
                shaped((seq_len, LANES), F32),
                shaped((LANES, LANES), F32),
                shaped(w.shape, BF16),
                shaped((seq_len, 3 * width), BF16),
            ],
            (
                grad_y, grad_log, after, packed, slot_pair, ints, picked, *parts, r, w, mix_all[s],
                x, qkv, probs_att, attended, cosine, sine,
            ),
            flops=5 << 30,
        )
        x_grads[s] = grad_x
        r_grads[s] = grad_r[:, :nexp]
        mix_lanes = -(-nexp * nexp // rows)
        mix_flat = jnp.pad(grad_mix[:nexp, :nexp].reshape(-1), (0, rows * mix_lanes - nexp * nexp)).reshape(rows, mix_lanes)
        mix_tile = jnp.tile(mix_flat, (owners * pieces, 1)).astype(BF16)
        at = 4 * width + AT_MIX
        grads = lax.dynamic_update_slice(grads, mix_tile, (0, at))
        sums[s] = (grads, in_sum, out_sum)
        grad_y = grad_x.astype(BF16)
        grad_log = grad_r.astype(BF16)
    shared_own = jnp.where(first_core, sums[0][0], sums[1][0])
    shared_other = jnp.where(first_core, sums[1][0], sums[0][0])
    shared_sum = (shared_own.astype(F32) + swap(shared_other).astype(F32)).astype(BF16)
    shared_sum = lax.psum_scatter(shared_sum, ("expert", "shard"), scatter_dimension=0, tiled=True).astype(F32)

    def halves(index):
        own = jnp.where(first_core, sums[0][index], sums[1][index])
        got = swap(jnp.where(first_core, sums[1][index], sums[0][index]))
        return jnp.where(first_core, own, got).astype(F32), jnp.where(first_core, got, own).astype(F32)

    in_halves = [
        jnp.swapaxes(half.reshape(in_rows, chunks, 2, CHUNK), 1, 2).reshape(in_rows, 2, pieces, hidden_here)
        for half in halves(1)
    ]
    in_grad = jnp.stack(in_halves, axis=3).reshape(in_rows, columns)
    out_grad = jnp.concatenate(halves(2), axis=0)

    def both_batches(pair):
        own = jnp.where(first_core, pair[0], pair[1])
        got = swap(jnp.where(first_core, pair[1], pair[0]))
        return jnp.stack(by_section(own, got))[None, :, None]

    small_sum = shared_sum[:, 4 * width :]
    mix_grad = small_sum[:, AT_MIX : AT_MIX + mix_lanes].reshape(-1)[: nexp * nexp].reshape(nexp, nexp)
    return (
        both_batches(results),
        both_batches(x_grads),
        both_batches(r_grads),
        shared_sum[None, :, : 3 * width],
        shared_sum[None, :, 3 * width : 4 * width],
        small_sum[None, :, :nexp],
        small_sum[None, :, AT_PROJ : AT_PROJ + const_proj.shape[-1]],
        small_sum[None, :, AT_VEC : AT_VEC + nconst],
        small_sum[None, :, AT_GAIN : AT_GAIN + 2],
        mix_grad[None],
        in_grad[None, None],
        out_grad[None, None],
    )


def solution(mesh):
    placed = (
        P(None, ("expert", "shard"), None, None),
        P(None, ("expert", "shard"), None, None),
        P(None, ("expert", "shard"), None, None),
        P(None, ("expert", "shard"), None),
        P("section", None, ("expert", "shard"), None, None),
        P("section", None, ("expert", "shard"), None),
        P("section", ("expert", "shard"), None),
        P("section", ("expert", "shard"), None),
        P("section", ("expert", "shard"), None),
        P("section", ("expert", "shard"), None),
        P("section", ("expert", "shard"), None),
        P("section", ("expert", "shard"), None),
        P("section", None, None),
        P("section", "expert", "shard", None),
        P("section", "expert", "shard", None),
    )
    return jax.shard_map(
        local,
        mesh=mesh,
        in_specs=placed,
        out_specs=(
            P("section", None, ("expert", "shard"), None, None),
            P("section", None, ("expert", "shard"), None, None),
            P("section", None, ("expert", "shard"), None, None),
            P("section", ("expert", "shard"), None),
            P("section", ("expert", "shard"), None),
            P("section", ("expert", "shard"), None),
            P("section", ("expert", "shard"), None),
            P("section", ("expert", "shard"), None),
            P("section", ("expert", "shard"), None),
            P("section", None, None),
            P("section", "expert", "shard", None),
            P("section", "expert", "shard", None),
        ),
        check_vma=False,
    )
```

time: 814 us -> 738 us (0.907)
  matrix products: 197 us -> 0 us
  waiting for transfers between devices: 274 us -> 410 us
  other arithmetic: 123 us -> 41.1 us
  Pallas kernels: 48.8 us -> 121 us
  blocking collectives: 9.58 us -> 48.8 us
  local copies, waits for them, and re-layouts: 80.3 us -> 60.7 us
  starting transfers between devices: 47.4 us -> 33.5 us
  between operations: 23.6 us -> 14.9 us
    dot_general x244 -> x0, matrix products: 197 us -> none  [mm(): lax.dot_general(a, b, (contract, ((), ())), precision=precision, preferre...]
    pallas_call x0 -> x12, Pallas kernels: none -> 121 us  [the longest x8 75.7 us: run(): pl.pallas_call(kernel, out_shape=out, compiler_params=pltpu.CompilerParam...]
    all_gather x2, waiting for transfers between devices: 0.01 us -> 89.8 us  [local(): lax.all_gather(ins[s], 'shard', axis=0, tiled=True)]
    reduce_scatter x2, waiting for transfers between devices: 11.5 us -> 79.7 us  [local(): in_sum = lax.psum_scatter(grad_in, 'shard', scatter_dimension=0, tiled=True)]
    unnamed x24 -> x0, Pallas kernels: 48.8 us -> none
    reduce_sum x31 -> x0, other arithmetic: 40.4 us -> none  [the longest x24 36.3 us: attention_body(): probs = (scores / jnp.sum(scores, axis=-1, keepdims=True)).astype(BF16)]
    all_to_all x1 -> x4, blocking collectives: 9.58 us -> 48.8 us  [exchanged(): lax.all_to_all(blocks.reshape(owners, room, width), 'expert', split_axis=...]
    unnamed x978 -> x78, local copies, waits for them, and re-layouts: 29.3 us -> 9.31 us
  transfers between devices with their start and end apart: 40 -> 37, of which waited for: 18 -> 19; matrix products, arithmetic and copies ran while one was open for 44% -> 11% of each run, Pallas kernels for 6% -> 17%
where the time goes in v2:
time: 738 us; the launch traced here: 730 us
  waiting for transfers between devices  410 us (56%)
  Pallas kernels  121 us (16%)
  local copies, waits for them, and re-layouts  60.7 us (8%)
  blocking collectives  48.8 us (7%)
  other arithmetic  41.1 us (6%)
  starting transfers between devices  33.5 us (5%)
  between operations  14.9 us (2%)
    reduce_scatter x1, waiting for transfers between devices, local(): lax.psum_scatter(shared_sum, ('expert', 'shard'), scatter_dimension=0, ti...  127 us
    all_gather x2, waiting for transfers between devices, local(): lax.all_gather(ins[s], 'shard', axis=0, tiled=True)  89.8 us
    reduce_scatter x2, waiting for transfers between devices, local(): in_sum = lax.psum_scatter(grad_in, 'shard', scatter_dimension=0, tiled=True)  79.7 us
    pallas_call x8, Pallas kernels, run(): pl.pallas_call(kernel, out_shape=out, compiler_params=pltpu.CompilerParam...  75.7 us
    all_gather x1, waiting for transfers between devices, local(): shared = lax.all_gather(shared, ('expert', 'shard'), axis=0, tiled=True)  60.8 us
    all_to_all x4, blocking collectives, exchanged(): lax.all_to_all(blocks.reshape(owners, room, width), 'expert', split_axis=...  48.8 us
    all_to_all x8, waiting for transfers between devices, exchanged(): lax.all_to_all(blocks.reshape(owners, room, width), 'expert', split_axis=...  35 us
    all_to_all x8, starting transfers between devices, exchanged(): lax.all_to_all(blocks.reshape(owners, room, width), 'expert', split_axis=...  29.1 us
  transfers between devices with their start and end apart: 37, of which 19 were waited for; matrix products, arithmetic and copies ran while one was open for 11% of the time, Pallas kernels for 17%

profile of v2, /device:TPU:0, one launch (start us, length us, event | category | flops | bytes accessed | tf_op | source)
XLA Modules:
  0.0 729.6 jit_solution(5729181451721216078)
XLA Ops:
  36.5 60.8 %all-gather.6.cloned.1.call-done = bf16[768,3200]{1,0:T(8,128)(2,1)} async-done(((bf16[48,3200]{1,0:T(8,128)(2,1)}), bf16[768,3200]{1,0:T(8,128)(2,1)}) %all-gather.6.cloned.1.call-update) | async-done | bytes 4915216 | tf_op jit(solution)/shard_map/all_gather | solution.py:510
  106.9 8.6 %broadcast_select_fusion.1 = (bf16[768,3200]{1,0:T(8,128)(2,1)}, bf16[768,3200]{1,0:T(8,128)(2,1)}) fusion(bf16[768,3200]{1,0:T(8,128)(2,1)} %collective-permute-done, bf16[768,3200]{1,0:T(8,128)(2,1)} %all-gather.6.cloned.1.call-done, pred[]{:T(512)S(6)} %eq.3), kind=kLoop, calls=%fused_computation.2 | loop fusion | flops 4915200 | bytes 19660800 | tf_op jit(solution)/shard_map/jit(_where)/select_n | solution.py:474
  115.5 11.2 %shard_map.238 = (f32[256,768]{1,0:T(8,128)}, bf16[256,2304]{1,0:T(8,128)(2,1)}, bf16[12,256,256]{2,1,0:T(8,128)(2,1)}, bf16[256,768]{1,0:T(8,128)(2,1)}, f32[25...) custom-call(bf16[256,768]{1,0:T(8,128)(2,1)} %dynamic-slice_bitcast_fusion.2.x, ...), custom_call_target="tpu_custom_call" | custom-call | flops 2147483648 | bytes 8388608 | tf_op jit(solution)/shard_map/pallas_call | solution.py:392
  126.7 12.5 %all_to_all.60 = bf16[4,80,768]{2,1,0:T(8,128)(2,1)S(1)} all-to-all(bf16[4,80,768]{2,1,0:T(8,128)(2,1)} %bitcast.150), channel_id=1, replica_groups=mesh['section'=2,'expert'=4,'shard'=4] {'expert'}, dimensions={0} | all-to-all | bytes 983040 | tf_op jit(solution)/shard_map/all_to_all | solution.py:533
  139.2 59.9 %all-gather.8.cloned.1.call-done.w_in = bf16[768,2048]{1,0:T(8,128)(2,1)} async-done(((bf16[192,2048]{1,0:T(8,128)(2,1)}), bf16[768,2048]{1,0:T(8,128)(2,1)}) %all-gather.8.cloned.1.call-update) | async-done | bytes 3145744 | tf_op jit(solution)/shard_map/all_gather | solution.py:490
  199.9 8.6 %shard_map.239 = (bf16[320,768]{1,0:T(8,128)(2,1)}, bf16[320,768]{1,0:T(8,128)(2,1)}) custom-call(bf16[320,768]{1,0:T(8,128)(2,1)} %bitcast.133, bf16[320,768]{1,0:T(8,128)(2,1)} %copy-done.32, bf16[768,2048]{1,0:T(8,128)(2,1)} %all-gather.8.cloned.1.call-done.w_in, bf16[1024,768]{1,0:T(8,128)(2,1)} %all-gather.10.cloned.1.call-done.w_out), custom_call_target="tpu_custom_call" | custom-call | flops 3019898880 | bytes 8388608 | tf_op jit(solution)/shard_map/pallas_call | solution.py:410
  208.5 13.4 %all_to_all.61 = bf16[4,80,768]{2,1,0:T(8,128)(2,1)} all-to-all(bf16[4,80,768]{2,1,0:T(8,128)(2,1)} %bitcast.151), channel_id=1, replica_groups=mesh['section'=2,'expert'=4,'shard'=4] {'expert'}, dimensions={0} | all-to-all | bytes 983040 | tf_op jit(solution)/shard_map/all_to_all | solution.py:533
  226.7 6.8 all-to-all-done.2
  239.5 11.1 %shard_map.241 = (f32[256,768]{1,0:T(8,128)}, bf16[256,2304]{1,0:T(8,128)(2,1)}, bf16[12,256,256]{2,1,0:T(8,128)(2,1)}, bf16[256,768]{1,0:T(8,128)(2,1)}, f32[25...) custom-call(bf16[256,768]{1,0:T(8,128)(2,1)} %get-tuple-element.57.x, ...), custom_call_target="tpu_custom_call" | custom-call | flops 2147483648 | bytes 8388608 | tf_op jit(solution)/shard_map/pallas_call | solution.py:392
  270.8 30.0 %all-gather.12.cloned.1.call-done.w_in = bf16[768,2048]{1,0:T(8,128)(2,1)} async-done(((bf16[192,2048]{1,0:T(8,128)(2,1)}), bf16[768,2048]{1,0:T(8,128)(2,1)}) %all-gather.12.cloned.1.call-update) | async-done | bytes 3145744 | tf_op jit(solution)/shard_map/all_gather | solution.py:490
  301.5 8.6 %shard_map.242 = (bf16[320,768]{1,0:T(8,128)(2,1)}, bf16[320,768]{1,0:T(8,128)(2,1)}) custom-call(bf16[320,768]{1,0:T(8,128)(2,1)} %bitcast.137, bf16[320,768]{1,0:T(8,128)(2,1)} %copy-done.33, bf16[768,2048]{1,0:T(8,128)(2,1)} %all-gather.12.cloned.1.call-done.w_in, bf16[1024,768]{1,0:T(8,128)(2,1)} %all-gather.14.cloned.1.call-done.w_out), custom_call_target="tpu_custom_call" | custom-call | flops 3019898880 | bytes 8388608 | tf_op jit(solution)/shard_map/pallas_call | solution.py:410
  314.5 14.1 %shard_map.245 = (bf16[320,768]{1,0:T(8,128)(2,1)}, bf16[320,768]{1,0:T(8,128)(2,1)}, bf16[768,2048]{1,0:T(8,128)(2,1)}, bf16[1024,768]{1,0:T(8,128)(2,1)}) custom-call(bf16[320,768]{1,0:T(8,128)(2,1)} %bitcast.138, bf16[320,768]{1,0:T(8,128)(2,1)} %copy-done.33, bf16[320,768]{1,0:T(8,128)(2,1)} %bitcast.141, bf16[320,768]{1,0:T(8,128)(2,1)} %copy-done.34, ...), custom_call_target="tpu_custom_call" | custom-call | flops 8053063680 | bytes 16777216 | tf_op jit(solution)/shard_map/pallas_call | solution.py:425
  333.8 7.5 %all-to-all-done.7 = bf16[4,80,768]{2,1,0:T(8,128)(2,1)S(1)} async-done(((bf16[4,80,768]{2,1,0:T(8,128)(2,1)}), bf16[4,80,768]{2,1,0:T(8,128)(2,1)S(1)}, u32[]{:S(2)}, u32[]{:S(2)}) %all-to-all-start.7) | async-done | bytes 491552 | tf_op jit(solution)/shard_map/all_to_all | solution.py:533
  344.7 7.5 %all-to-all-done.5 = bf16[4,80,768]{2,1,0:T(8,128)(2,1)S(1)} async-done(((bf16[4,80,768]{2,1,0:T(8,128)(2,1)}), bf16[4,80,768]{2,1,0:T(8,128)(2,1)S(1)}, u32[]{:S(2)}, u32[]{:S(2)}) %all-to-all-start.5) | async-done | bytes 491552 | tf_op jit(solution)/shard_map/all_to_all | solution.py:533
  363.3 18.8 %shard_map.246 = (f32[256,768]{1,0:T(8,128)}, f32[256,128]{1,0:T(8,128)}, f32[128,128]{1,0:T(8,128)}, bf16[768,3200]{1,0:T(8,128)(2,1)}, bf16[256,2304]{1,0:T(8,128)(2,1)}) custom-call(f32[256,768]{1,0:T(8,128)} %dynamic-slice_bitcast_fusion.grad_y, f32[256,128]{1,0:T(8,128)} %broadcast_in_dim.46.grad_log, f32[256,768]{1,0:T(8,128)} %get-tuple-element.59.after, ...), custom_call_target="tpu_custom_call" | custom-call | flops 5368709120 | bytes 8388608 | tf_op jit(solution)/shard_map/pallas_call | solution.py:392
  386.7 10.7 %all_to_all.62 = bf16[4,80,768]{2,1,0:T(8,128)(2,1)S(1)} all-to-all(bf16[4,80,768]{2,1,0:T(8,128)(2,1)} %bitcast.127), channel_id=1, replica_groups=mesh['section'=2,'expert'=4,'shard'=4] {'expert'}, dimensions={0} | all-to-all | bytes 983040 | tf_op jit(solution)/shard_map/all_to_all | solution.py:533
  400.0 14.1 %shard_map.248 = (bf16[320,768]{1,0:T(8,128)(2,1)}, bf16[320,768]{1,0:T(8,128)(2,1)}, bf16[768,2048]{1,0:T(8,128)(2,1)}, bf16[1024,768]{1,0:T(8,128)(2,1)}) custom-call(bf16[320,768]{1,0:T(8,128)(2,1)} %bitcast.134, bf16[320,768]{1,0:T(8,128)(2,1)} %copy-done.32, bf16[320,768]{1,0:T(8,128)(2,1)} %bitcast.149, bf16[320,768]{1,0:T(8,128)(2,1)} %copy-done.36, ...), custom_call_target="tpu_custom_call" | custom-call | flops 8053063680 | bytes 16777216 | tf_op jit(solution)/shard_map/pallas_call | solution.py:425
  415.3 12.2 %all_to_all.63 = bf16[4,80,768]{2,1,0:T(8,128)(2,1)} all-to-all(bf16[4,80,768]{2,1,0:T(8,128)(2,1)S(1)} %bitcast.145), channel_id=1, replica_groups=mesh['section'=2,'expert'=4,'shard'=4] {'expert'}, dimensions={0} | all-to-all | bytes 983040 | tf_op jit(solution)/shard_map/all_to_all | solution.py:533
  439.1 18.8 %shard_map.249 = (f32[256,768]{1,0:T(8,128)}, f32[256,128]{1,0:T(8,128)}, f32[128,128]{1,0:T(8,128)}, bf16[768,3200]{1,0:T(8,128)(2,1)}, bf16[256,2304]{1,0:T(8,128)(2,1)}) custom-call(bf16[256,768]{1,0:T(8,128)(2,1)} %convert_element_type.65.grad_y, bf16[256,128]{1,0:T(8,128)(2,1)} %convert_element_type.66.grad_log, f32[256,768]{1,0:T(8,128)} %get-tuple-element.51.after, ...), custom_call_target="tpu_custom_call" | custom-call | flops 5368709120 | bytes 8388608 | tf_op jit(solution)/shard_map/pallas_call | solution.py:392
  467.7 8.1 %collective-permute-done.16 = bf16[768,3200]{1,0:T(8,128)(2,1)} collective-permute-done((bf16[768,3200]{1,0:T(8,128)(2,1)}, bf16[768,3200]{1,0:T(8,128)(2,1)}, u32[]{:S(2)}, u32[]{:S(2)}) %collective-permute-start.16) | collective-permute-done | bytes 4915232 | tf_op jit(solution)/shard_map/ppermute | solution.py:465
  475.7 8.0 %add_convert_fusion = bf16[768,3200]{1,0:T(8,128)(2,1)} fusion(bf16[768,3200]{1,0:T(8,128)(2,1)} %collective-permute-done.16, bf16[768,3200]{1,0:T(8,128)(2,1)} %dynamic_update_slice.6, bf16[768,3200]{1,0:T(8,128)(2,1)} %dynamic_update_slice.7, pred[]{:T(512)S(6)} %eq.3), kind=kLoop, calls=%fused_computation | loop fusion | flops 12288000 | bytes 19660800 | tf_op jit(solution)/shard_map/convert_element_type | solution.py:616
  491.8 17.1 %reduce-scatter.10.cloned.1.call-done = bf16[192,2048]{1,0:T(8,128)(2,1)} async-done(((bf16[768,2048]{1,0:T(8,128)(2,1)}), bf16[192,2048]{1,0:T(8,128)(2,1)}) %reduce-scatter.10.cloned.1.call-update) | async-done | bytes 786448 | tf_op jit(solution)/shard_map/reduce_scatter | solution.py:586
  508.9 62.6 %reduce-scatter.8.cloned.1.call-done = bf16[192,2048]{1,0:T(8,128)(2,1)} async-done(((bf16[768,2048]{1,0:T(8,128)(2,1)}), bf16[192,2048]{1,0:T(8,128)(2,1)}) %reduce-scatter.8.cloned.1.call-update) | async-done | bytes 786448 | tf_op jit(solution)/shard_map/reduce_scatter | solution.py:586
  588.1 127.0 %reduce-scatter.6.cloned.1.call-done = bf16[48,3200]{1,0:T(8,128)(2,1)} async-done(((bf16[768,3200]{1,0:T(8,128)(2,1)}), bf16[48,3200]{1,0:T(8,128)(2,1)}) %reduce-scatter.6.cloned.1.call-update) | async-done | bytes 307216 | tf_op jit(solution)/shard_map/reduce_scatter | solution.py:617
  (243 shorter events, 156.8 us)
Async XLA Ops:
  7.2 90.1 %all-gather.6.cloned.1.call-start = ((), (), s32[]{:S(2)}) async-start(), calls=%async_computation.17 | async-start | bytes 5222400 | tf_op jit(solution)/shard_map/all_gather | solution.py:510
  12.3 126.9 %all-gather.10.cloned.1.call-start = ((), (), s32[]{:S(2)}) async-start(), calls=%async_computation.19 | async-start | bytes 1966080 | tf_op jit(solution)/shard_map/all_gather | solution.py:491
  17.2 181.9 %all-gather.8.cloned.1.call-start = ((), (), s32[]{:S(2)}) async-start(), calls=%async_computation.18 | async-start | bytes 3932160 | tf_op jit(solution)/shard_map/all_gather | solution.py:490
  36.4 234.3 %all-gather.14.cloned.1.call-start = ((), (), s32[]{:S(2)}) async-start(), calls=%async_computation.21 | async-start | bytes 1966080 | tf_op jit(solution)/shard_map/all_gather | solution.py:491
  97.3 203.4 %all-gather.12.cloned.1.call-start = ((), (), s32[]{:S(2)}) async-start(), calls=%async_computation.20 | async-start | bytes 3932160 | tf_op jit(solution)/shard_map/all_gather | solution.py:490
  139.2 59.9 %collective-permute-start.3 = (bf16[320,768]{1,0:T(8,128)(2,1)S(1)}, bf16[320,768]{1,0:T(8,128)(2,1)S(1)}, u32[]{:S(2)}, u32[]{:S(2)}) collective-permute-start(bf16[320,768]{1,0:T(8,128)(2,1)S(1)} %bitcast.132), channel_id=1, source_target_pairs={{0,16},{16,0},{1,17},{17,1},{2,18},{18,2},{3,19},{19,3},{4,20},{20... | collective-permute-start | bytes 1474568 | tf_op jit(solution)/shard_map/ppermute | solution.py:465
  208.5 13.4 %collective-permute-start.6 = (bf16[320,768]{1,0:T(8,128)(2,1)}, bf16[320,768]{1,0:T(8,128)(2,1)}, u32[]{:S(2)}, u32[]{:S(2)}) collective-permute-start(bf16[320,768]{1,0:T(8,128)(2,1)} %get-tuple-element.56), channel_id=1, source_target_pairs={{0,16},{16,0},{1,17},{17,1},{2,18},{18,2},{3,19},{19,3},{4,20},{20... | collective-permute-start | bytes 1474568 | tf_op jit(solution)/shard_map/ppermute | solution.py:465
  222.0 11.5 %all-to-all-start.2 = ((bf16[4,80,768]{2,1,0:T(8,128)(2,1)}), bf16[4,80,768]{2,1,0:T(8,128)(2,1)S(1)}, u32[]{:S(2)}, u32[]{:S(2)}) async-start(bf16[4,80,768]{2,1,0:T(8,128)(2,1)} %bitcast.27), calls=%async_computation.2 | async-start | bytes 983040 | tf_op jit(solution)/shard_map/all_to_all | solution.py:533
  264.4 36.3 %collective-permute-start.7 = (bf16[320,768]{1,0:T(8,128)(2,1)S(1)}, bf16[320,768]{1,0:T(8,128)(2,1)S(1)}, u32[]{:S(2)}, u32[]{:S(2)}) collective-permute-start(bf16[320,768]{1,0:T(8,128)(2,1)S(1)} %bitcast.136), channel_id=1, source_target_pairs={{0,16},{16,0},{1,17},{17,1},{2,18},{18,2},{3,19},{19,3},{4,20},{20... | collective-permute-start | bytes 1474568 | tf_op jit(solution)/shard_map/ppermute | solution.py:465
  270.8 43.0 %collective-permute-start.10 = (bf16[320,768]{1,0:T(8,128)(2,1)S(1)}, bf16[320,768]{1,0:T(8,128)(2,1)S(1)}, u32[]{:S(2)}, u32[]{:S(2)}) collective-permute-start(bf16[320,768]{1,0:T(8,128)(2,1)S(1)} %bitcast.140), channel_id=1, source_target_pairs={{0,16},{16,0},{1,17},{17,1},{2,18},{18,2},{3,19},{19,3},{4,20},{20... | collective-permute-start | bytes 1474568 | tf_op jit(solution)/shard_map/ppermute | solution.py:465
  310.1 18.6 %all-to-all-start.4 = ((bf16[4,80,768]{2,1,0:T(8,128)(2,1)}), bf16[4,80,768]{2,1,0:T(8,128)(2,1)S(1)}, u32[]{:S(2)}, u32[]{:S(2)}) async-start(bf16[4,80,768]{2,1,0:T(8,128)(2,1)} %bitcast.146), calls=%async_computation.4 | async-start | bytes 983040 | tf_op jit(solution)/shard_map/all_to_all | solution.py:533
  313.7 27.5 %collective-permute-start.8 = (bf16[320,768]{1,0:T(8,128)(2,1)}, bf16[320,768]{1,0:T(8,128)(2,1)}, u32[]{:S(2)}, u32[]{:S(2)}) collective-permute-start(bf16[320,768]{1,0:T(8,128)(2,1)} %get-tuple-element.64), channel_id=1, source_target_pairs={{0,16},{16,0},{1,17},{17,1},{2,18},{18,2},{3,19},{19,3},{4,20},{20... | collective-permute-start | bytes 1474568 | tf_op jit(solution)/shard_map/ppermute | solution.py:465
  328.7 12.5 %all-to-all-start.7 = ((bf16[4,80,768]{2,1,0:T(8,128)(2,1)}), bf16[4,80,768]{2,1,0:T(8,128)(2,1)S(1)}, u32[]{:S(2)}, u32[]{:S(2)}) async-start(bf16[4,80,768]{2,1,0:T(8,128)(2,1)} %bitcast.144), calls=%async_computation.7 | async-start | bytes 983040 | tf_op jit(solution)/shard_map/all_to_all | solution.py:533
  332.9 157.0 %reduce-scatter.14.cloned.1.call-start = ((), (), s32[]{:S(2)}) async-start(), calls=%async_computation.26 | async-start | bytes 1966080 | tf_op jit(solution)/shard_map/reduce_scatter | solution.py:587
  333.5 11.3 %collective-permute-start.11 = (bf16[320,768]{1,0:T(8,128)(2,1)}, bf16[320,768]{1,0:T(8,128)(2,1)}, u32[]{:S(2)}, u32[]{:S(2)}) collective-permute-start(bf16[320,768]{1,0:T(8,128)(2,1)} %get-tuple-element.68), channel_id=1, source_target_pairs={{0,16},{16,0},{1,17},{17,1},{2,18},{18,2},{3,19},{19,3},{4,20},{20... | collective-permute-start | bytes 1474568 | tf_op jit(solution)/shard_map/ppermute | solution.py:465
  341.3 11.0 %all-to-all-start.5 = ((bf16[4,80,768]{2,1,0:T(8,128)(2,1)}), bf16[4,80,768]{2,1,0:T(8,128)(2,1)S(1)}, u32[]{:S(2)}, u32[]{:S(2)}) async-start(bf16[4,80,768]{2,1,0:T(8,128)(2,1)} %bitcast.33), calls=%async_computation.5 | async-start | bytes 983040 | tf_op jit(solution)/shard_map/all_to_all | solution.py:533
  355.7 134.2 %reduce-scatter.12.cloned.1.call-start = ((), (), s32[]{:S(2)}) async-start(), calls=%async_computation.25 | async-start | bytes 1966080 | tf_op jit(solution)/shard_map/reduce_scatter | solution.py:587
  414.2 94.7 %reduce-scatter.10.cloned.1.call-start = ((), (), s32[]{:S(2)}) async-start(), calls=%async_computation.24 | async-start | bytes 3932160 | tf_op jit(solution)/shard_map/reduce_scatter | solution.py:586
  415.2 12.3 %collective-permute-start.13 = (bf16[320,768]{1,0:T(8,128)(2,1)S(1)}, bf16[320,768]{1,0:T(8,128)(2,1)}, u32[]{:S(2)}, u32[]{:S(2)}) collective-permute-start(bf16[320,768]{1,0:T(8,128)(2,1)S(1)} %copy-done.35), channel_id=1, source_target_pairs={{0,16},{16,0},{1,17},{17,1},{2,18},{18,2},{3,19},{19,3},{4,20},{20... | collective-permute-start | bytes 1474568 | tf_op jit(solution)/shard_map/ppermute | solution.py:465
  427.5 10.8 %all-to-all-start.11 = ((bf16[4,80,768]{2,1,0:T(8,128)(2,1)}), bf16[4,80,768]{2,1,0:T(8,128)(2,1)S(1)}, u32[]{:S(2)}, u32[]{:S(2)}) async-start(bf16[4,80,768]{2,1,0:T(8,128)(2,1)} %bitcast.50), calls=%async_computation.11 | async-start | bytes 983040 | tf_op jit(solution)/shard_map/all_to_all | solution.py:533
  430.9 140.6 %reduce-scatter.8.cloned.1.call-start = ((), (), s32[]{:S(2)}) async-start(), calls=%async_computation.23 | async-start | bytes 3932160 | tf_op jit(solution)/shard_map/reduce_scatter | solution.py:586
  467.2 247.9 %reduce-scatter.6.cloned.1.call-start = ((), (), s32[]{:S(2)}) async-start(), calls=%async_computation.22 | async-start | bytes 5222400 | tf_op jit(solution)/shard_map/reduce_scatter | solution.py:617
  488.0 84.9 %collective-permute-start.14 = (f32[256,768]{1,0:T(8,128)S(1)}, f32[256,768]{1,0:T(8,128)S(1)}, u32[]{:S(2)}, u32[]{:S(2)}) collective-permute-start(f32[256,768]{1,0:T(8,128)S(1)} %broadcast_select_fusion.13), channel_id=1, source_target_pairs={{0,16},{16,0},{1,17},{17,1},{2,18},{18,2},{3,19},{19,3},{4,20},{20... | collective-permute-start | bytes 2359304 | tf_op jit(solution)/shard_map/ppermute | solution.py:465
  491.7 82.6 %collective-permute-start.18 = (bf16[256,768]{1,0:T(8,128)(2,1)}, bf16[256,768]{1,0:T(8,128)(2,1)}, u32[]{:S(2)}, u32[]{:S(2)}) collective-permute-start(bf16[256,768]{1,0:T(8,128)(2,1)} %broadcast_select_fusion.11), channel_id=1, source_target_pairs={{0,16},{16,0},{1,17},{17,1},{2,18},{18,2},{3,19},{19,3},{4,20},{20... | collective-permute-start | bytes 1179656 | tf_op jit(solution)/shard_map/ppermute | solution.py:465
  (50 other events, 1249.8 us)
Sparse Core Ops, SparseCore 0:
  12.4 84.8 all-gather.5
  98.9 35.6 all-gather.9
  136.7 62.3 all-gather.7
  200.5 35.7 all-gather.13
  238.3 62.3 all-gather.11
  335.7 34.4 reduce-scatter.13
  414.3 32.4 reduce-scatter.11
  449.6 59.2 reduce-scatter.9
  511.2 60.2 reduce-scatter.7
  576.6 138.5 reduce-scatter.5

commit v3 on v2

--- a/solution.py
+++ b/solution.py
@@ -65,8 +65,8 @@
     return jnp.where(condition, 1.0, 0.0).astype(BF16)
 
 
-def small_rows_of(w, width):
-    rows = w[:, 4 * width :].astype(F32).T
+def small_rows_of(small):
+    rows = small[...].astype(F32).T
     return rows[AT_GAIN : AT_GAIN + 1], rows[AT_GAIN + 1 : AT_GAIN + 2], rows[AT_VEC:AT_GAIN]
 
 
@@ -151,13 +151,13 @@
     return gates, of(nffn + 1), [of(nffn + 2 + c) for c in range(nconst)], [mixes(c) for c in range(nconst)]
 
 
-def combine(after, packed, slot_pair, ints, parts, gain_second, vec_rows, dims, picked_ref):
+def combine(after, packed, slot_pair, ints, blocks, gain_second, vec_rows, dims, picked_ref):
     nffn, nexp, _, slots = dims
     nconst = nexp - nffn - 2
     rows = after.shape[0]
     second = after * inverse_norm(after) * gain_second
     gates, copied, const, mixes = extras(packed, ints, nffn, nconst)
-    made = (parts[0][...].astype(F32) + parts[1][...].astype(F32)).astype(BF16)
+    made = blocks[...]
     slot_lane = lane_of(rows, slots)
     coefficient = copied
     for c in range(nconst):
@@ -184,7 +184,7 @@
 
 
 def moe_back(
-    grad_y, grad_log_in, after, packed, slot_pair, ints, picked, parts, r, small, mix, gain_second, vec_rows, dims
+    grad_y, grad_log_in, after, packed, slot_pair, ints, picked, blocks, r, small, mix, gain_second, vec_rows, dims
 ):
     nffn, nexp, _, slots = dims
     nconst = nexp - nffn - 2
@@ -195,7 +195,7 @@
     second = unit * gain_second
     second_b = second.astype(BF16)
     gates, copied, const, mixes = extras(packed, ints, nffn, nconst)
-    grad_buffer = (parts[0][...].astype(F32) + parts[1][...].astype(F32)).astype(BF16)
+    grad_buffer = blocks[...]
     slot_lane = lane_of(rows, slots)
     dispatch = sum(jnp.where(slot_pair[:, k : k + 1] == slot_lane, 1.0, 0.0) for k in range(TOP))
     grad_second = mm(dispatch.astype(BF16), grad_buffer)
@@ -281,43 +281,62 @@
 
 
 def attend_kernel(
-    dims, x, r, w, mix, cosine, sine, seg_col, seg_row, ints, prio_row,
+    dims, x, r, w, small, mix, cosine, sine, seg_col, seg_row, ints, prio_row,
     after, qkv, probs_att, attended, packed, slot_pair, r_next, buffer,
 ):
-    width = x.shape[1]
-    gain_first, gain_second, _ = small_rows_of(w, width)
+    gain_first, gain_second, _ = small_rows_of(small)
     after_v = attention(
         x[...].astype(F32), w, gain_first, cosine[...], sine[...], seg_col[...], seg_row[...], qkv, probs_att, attended
     )
     after[...] = after_v
     gating(
-        after_v, r[...].astype(F32), w[:, 4 * width :], mix[...], gain_second, ints[...], prio_row[...], dims,
+        after_v, r[...].astype(F32), small[...], mix[...], gain_second, ints[...], prio_row[...], dims,
         packed, slot_pair, r_next, buffer,
     )
 
 
-def combine_kernel(dims, after, packed, slot_pair, ints, part_0, part_1, w, out, picked):
-    width = after.shape[1]
-    _, gain_second, vec_rows = small_rows_of(w, width)
+def middle_kernel(
+    dims, after_0, packed_0, slots_0, ints_0, blocks_0, small_0,
+    r, w, small, mix, cosine, sine, seg_col, seg_row, ints, prio_row, grad_y,
+    out, picked, after, qkv, probs_att, attended, packed, slot_pair, buffer, grad_buffer,
+):
+    _, gain_second, vec_rows = small_rows_of(small_0)
     out[...] = combine(
-        after[...], packed[...], slot_pair[...], ints[...], (part_0, part_1), gain_second, vec_rows, dims, picked
+        after_0[...], packed_0[...], slots_0[...], ints_0[...], blocks_0, gain_second, vec_rows, dims, picked
     ).astype(BF16)
-
-
-def give_back_kernel(dims, grad_y, packed, slot_pair, buffer):
-    give_back(grad_y[...].astype(F32), packed[...], slot_pair[...], dims, buffer)
+    attend_kernel(
+        dims, out, r, w, small, mix, cosine, sine, seg_col, seg_row, ints, prio_row,
+        after, qkv, probs_att, attended, packed, slot_pair, None, buffer,
+    )
+    give_back(grad_y[...], packed[...], slot_pair[...], dims, grad_buffer)
+
+
+def turn_kernel(
+    dims, grad_y, after, packed, slot_pair, ints, made, blocks, r, w, small, mix, x, qkv, probs_att, attended,
+    cosine, sine, packed_0, slots_0,
+    out, grad_x, grad_r, grad_mix, grads, buffer, grad_qkv, picked,
+):
+    _, gain_second, vec_rows = small_rows_of(small)
+    out[...] = combine(
+        after[...], packed[...], slot_pair[...], ints[...], made, gain_second, vec_rows, dims, picked
+    ).astype(BF16)
+    back_kernel(
+        dims, grad_y, None, after, packed, slot_pair, ints, picked, blocks, r, w, small, mix, x, qkv, probs_att, attended,
+        cosine, sine, grad_x, grad_r, grad_mix, grads, grad_qkv,
+    )
+    give_back(grad_x[...].astype(BF16).astype(F32), packed_0[...], slots_0[...], dims, buffer)
 
 
 def back_kernel(
-    dims, grad_y, grad_log, after, packed, slot_pair, ints, picked, part_0, part_1, r, w, mix,
-    x, qkv, probs_att, attended, cosine, sine,
-    grad_x, grad_r, grad_mix, grads, grad_qkv,
+    dims, grad_y, grad_log, after, packed, slot_pair, ints, picked, blocks, r, w, small, mix, x, qkv, probs_att, attended,
+    cosine, sine, grad_x, grad_r, grad_mix, grads, grad_qkv,
 ):
-    width = x.shape[1]
-    gain_first, gain_second, vec_rows = small_rows_of(w, width)
+    gain_first, gain_second, vec_rows = small_rows_of(small)
+    grad_log_v = 0.0 if grad_log is None else grad_log[...].astype(BF16).astype(F32)
+    grad_y_v = grad_y[...] if grad_log is None else grad_y[...].astype(BF16).astype(F32)
     grad_after, grad_r_v, grad_mix_v, small_rows = moe_back(
-        grad_y[...].astype(F32), grad_log[...].astype(F32), after[...], packed[...], slot_pair[...], ints[...], picked,
-        (part_0, part_1), r[...].astype(F32), w[:, 4 * width :], mix[...], gain_second, vec_rows, dims,
+        grad_y_v, grad_log_v, after[...], packed[...], slot_pair[...], ints[...], picked,
+        blocks, r[...].astype(F32), small[...], mix[...], gain_second, vec_rows, dims,
     )
     grad_r[...] = grad_r_v
     grad_mix[...] = grad_mix_v
@@ -327,111 +346,356 @@
     )
 
 
-def expert_kernel(arrived_0, arrived_1, w_in, w_out, made_0, made_1, total):
-    slots = arrived_0.shape[0]
-    step = pl.program_id(0)
-    for part, arrived in enumerate((arrived_0, arrived_1)):
-        at = part * slots
-        both = mm(arrived[...], w_in[...])
-        gate = both[:, :CHUNK]
-        hidden = (gate * jax.nn.sigmoid(gate) * both[:, CHUNK:]).astype(BF16)
-        more = mm(hidden, w_out[...])
-
-        @pl.when(step == 0)
-        def _():
-            total[at : at + slots] = more
-
-        @pl.when(step > 0)
-        def _():
-            total[at : at + slots] += more
-
-    @pl.when(step == pl.num_programs(0) - 1)
-    def _():
-        made_0[...] = total[:slots].astype(BF16)
-        made_1[...] = total[slots:].astype(BF16)
-
-
-def expert_back_kernel(
-    arrived_0, arrived_1, grad_0, grad_1, w_in, w_out, given_0, given_1, grad_in, grad_out, total
-):
-    slots = arrived_0.shape[0]
-    step = pl.program_id(0)
-    arrived = jnp.concatenate([arrived_0[...], arrived_1[...]], axis=0)
-    grad_made = jnp.concatenate([grad_0[...], grad_1[...]], axis=0)
-    both = mm(arrived, w_in[...])
-    gate, up = both[:, :CHUNK], both[:, CHUNK:]
-    sig = jax.nn.sigmoid(gate)
-    hidden = (gate * sig * up).astype(BF16)
-    grad_hidden = mm(grad_made, w_out[...], NT)
-    grad_out[...] = mm(hidden, grad_made, TN).astype(BF16)
-    grad_gate = grad_hidden * up * sig * (1.0 + gate * (1.0 - sig))
-    grad_up = grad_hidden * gate * sig
-    grad_both = jnp.concatenate([grad_gate, grad_up], axis=1).astype(BF16)
-    grad_in[...] = mm(arrived, grad_both, TN).astype(BF16)
-    more = mm(grad_both, w_in[...], NT)
-
-    @pl.when(step == 0)
-    def _():
-        total[...] = more
-
-    @pl.when(step > 0)
-    def _():
-        total[...] += more
-
-    @pl.when(step == pl.num_programs(0) - 1)
-    def _():
-        given_0[...] = total[:slots].astype(BF16)
-        given_1[...] = total[slots:].astype(BF16)
-
-
 def shaped(shape, dtype):
     return jax.ShapeDtypeStruct(shape, dtype)
 
 
-def run(kernel, out, args, flops=0):
+def run(kernel, out, args, flops=0, scratch=()):
     return pl.pallas_call(
         kernel,
         out_shape=out,
+        in_specs=[pl.BlockSpec(memory_space=pltpu.VMEM) for _ in args],
+        out_specs=[pl.BlockSpec(memory_space=pltpu.VMEM) for _ in out],
+        scratch_shapes=list(scratch),
         compiler_params=pltpu.CompilerParams(vmem_limit_bytes=VMEM_BYTES),
         cost_estimate=pl.CostEstimate(flops=flops, bytes_accessed=8 << 20, transcendentals=0),
     )(*args)
 
 
-def expert_specs(slots, width):
-    whole = pl.BlockSpec((slots, width), lambda i: (0, 0))
-    w_in = pl.BlockSpec((width, 2 * CHUNK), lambda i: (0, i))
-    w_out = pl.BlockSpec((CHUNK, width), lambda i: (i, 0))
-    return whole, w_in, w_out
-
-
-def expert_forward(arrived, w_in, w_out):
-    slots, width = arrived[0].shape
-    whole, in_spec, out_spec = expert_specs(slots, width)
+MESH = pl.DeviceIdType.MESH
+
+
+class Exchange:
+    def __init__(self, stream, sent, groups, partial, sibling_part, onward, pair_part, summed, result, sems):
+        self.stream, self.sent, self.groups = stream, sent, groups
+        self.partial, self.sibling_part, self.onward = partial, sibling_part, onward
+        self.pair_part, self.summed, self.result = pair_part, summed, result
+        (self.column_s, self.column_r, self.pair_s, self.pair_r, self.core_s, self.core_r, self.last_s, self.last_r,
+         self.local_sem, self.back_s, self.back_r, self.over_s, self.over_r, self.home_s, self.home_r) = sems
+        self.core, self.column, self.place = lax.axis_index("section"), lax.axis_index("expert"), lax.axis_index("shard")
+        self.owners = lax.axis_size("expert")
+        self.sibling = (1 - self.core, self.column, self.place)
+        self.pair = (self.core, self.column, self.place + 1 - 2 * lax.rem(self.place, 2))
+
+    def peer(self, column):
+        return (self.core, column, self.place)
+
+    def turn(self, by):
+        return lax.rem(self.column + by + self.owners, self.owners)
+
+    def to_column(self, by):
+        return pltpu.make_async_remote_copy(
+            self.sent.at[self.turn(by)], self.groups.at[0, self.column],
+            self.column_s.at[self.stream, by], self.column_r.at[self.stream, by],
+            device_id=self.peer(self.turn(by)), device_id_type=MESH,
+        )
+
+    def from_column(self, by):
+        source = self.turn(-by)
+        return pltpu.make_async_remote_copy(
+            self.sent.at[source], self.groups.at[0, source],
+            self.column_s.at[self.stream, by], self.column_r.at[self.stream, by],
+            device_id=self.peer(source), device_id_type=MESH,
+        )
+
+    def own_block(self):
+        return pltpu.make_async_copy(
+            self.sent.at[self.column], self.groups.at[0, self.column], self.local_sem.at[self.stream]
+        )
+
+    def forward(self, by, here, there, device, send, recv):
+        block = self.turn(-by)
+        return pltpu.make_async_remote_copy(
+            self.groups.at[here, block], self.groups.at[there, block],
+            send.at[self.stream, by], recv.at[self.stream, by], device_id=device, device_id_type=MESH,
+        )
+
+    def to_pair(self, by):
+        return self.forward(by, 0, 2, self.pair, self.pair_s, self.pair_r)
+
+    def to_core(self, by):
+        return self.forward(by, 0, 1, self.sibling, self.core_s, self.core_r)
+
+    def to_core_last(self, by):
+        return self.forward(by, 2, 3, self.sibling, self.last_s, self.last_r)
+
+    def start(self):
+        for by in range(1, self.owners):
+            self.to_column(by).start()
+        self.own_block().start()
+
+    def spread(self):
+        for by in range(self.owners):
+            if by:
+                self.from_column(by).wait_recv()
+            else:
+                self.own_block().wait()
+            self.to_pair(by).start()
+            self.to_core(by).start()
+
+    def near_ready(self):
+        for by in range(self.owners):
+            self.to_core(by).wait_recv()
+
+    def spread_far(self):
+        for by in range(self.owners):
+            self.to_pair(by).wait_recv()
+            self.to_core_last(by).start()
+
+    def far_ready(self):
+        for by in range(self.owners):
+            self.to_core_last(by).wait_recv()
+
+    def finish_dispatch(self):
+        for by in range(self.owners):
+            if by:
+                self.to_column(by).wait_send()
+            self.to_pair(by).wait_send()
+            self.to_core(by).wait_send()
+            self.to_core_last(by).wait_send()
+
+    def to_sibling(self, half):
+        return pltpu.make_async_remote_copy(
+            self.partial.at[2 * half + 1], self.sibling_part.at[half],
+            self.back_s.at[self.stream, half], self.back_r.at[self.stream, half],
+            device_id=self.sibling, device_id_type=MESH,
+        )
+
+    def over_pair(self):
+        return pltpu.make_async_remote_copy(
+            self.onward, self.pair_part, self.over_s.at[self.stream], self.over_r.at[self.stream],
+            device_id=self.pair, device_id_type=MESH,
+        )
+
+    def home(self, by):
+        return pltpu.make_async_remote_copy(
+            self.summed.at[self.turn(by)], self.result.at[self.column],
+            self.home_s.at[self.stream, by], self.home_r.at[self.stream, by],
+            device_id=self.peer(self.turn(by)), device_id_type=MESH,
+        )
+
+    def home_here(self, by):
+        source = self.turn(-by)
+        return pltpu.make_async_remote_copy(
+            self.summed.at[source], self.result.at[source],
+            self.home_s.at[self.stream, by], self.home_r.at[self.stream, by],
+            device_id=self.peer(source), device_id_type=MESH,
+        )
+
+    def return_far(self):
+        self.to_sibling(1).wait_recv()
+        self.onward[...] = (self.partial[2].astype(F32) + self.sibling_part[1].astype(F32)).astype(BF16)
+        self.over_pair().start()
+
+    def return_home(self):
+        self.to_sibling(0).wait_recv()
+        near = self.partial[0].astype(F32) + self.sibling_part[0].astype(F32)
+        self.over_pair().wait_recv()
+        self.summed[...] = (near + self.pair_part[...].astype(F32)).astype(BF16)
+        for by in range(1, self.owners):
+            self.home(by).start()
+        self.result[self.column] = self.summed[self.column]
+
+    def finish(self):
+        for by in range(1, self.owners):
+            self.home_here(by).wait_recv()
+            self.home(by).wait_send()
+        self.over_pair().wait_send()
+        self.to_sibling(0).wait_send()
+        self.to_sibling(1).wait_send()
+
+
+def greet(exchange):
+    barrier = pltpu.get_barrier_semaphore()
+    owners = exchange.owners
+    for by in range(1, owners):
+        pl.semaphore_signal(barrier, inc=1, device_id=exchange.peer(exchange.turn(by)), device_id_type=MESH)
+    pl.semaphore_signal(barrier, inc=1, device_id=exchange.sibling, device_id_type=MESH)
+    pl.semaphore_signal(barrier, inc=1, device_id=exchange.pair, device_id_type=MESH)
+    pl.semaphore_wait(barrier, owners + 1)
+
+
+def exchange_scratch(streams, owners, room, width):
+    block = (owners, room, width)
+    shapes = []
+    for _ in range(streams):
+        shapes += [
+            pltpu.VMEM((4,) + block, BF16),
+            pltpu.VMEM((4,) + block, BF16),
+            pltpu.VMEM((2,) + block, BF16),
+            pltpu.VMEM(block, BF16),
+            pltpu.VMEM(block, BF16),
+            pltpu.VMEM(block, BF16),
+            pltpu.VMEM(block, BF16),
+        ]
+    dma = pltpu.SemaphoreType.DMA
+    shapes += [dma((streams, owners)) for _ in range(8)] + [dma((streams,))]
+    shapes += [dma((streams, 2)) for _ in range(2)] + [dma((streams,)) for _ in range(2)] + [dma((streams, owners)) for _ in range(2)]
+    return shapes
+
+
+def exchanges(streams, sent, scratch):
+    sems = scratch[7 * streams :]
+    return [Exchange(i, sent[i], *scratch[7 * i : 7 * i + 7], sems) for i in range(streams)]
+
+
+def half_rows(ref, half):
+    groups, owners, room, width = ref.shape
+    return ref[2 * half : 2 * half + 2].reshape(2 * owners * room, width)
+
+
+def set_half(ref, half, value):
+    groups, owners, room, width = ref.shape
+    ref[2 * half : 2 * half + 2] = value.astype(BF16).reshape(2, owners, room, width)
+
+
+def experts_forward_half(rows, w_in, w_out):
+    total = 0.0
+    for chunk in range(w_out.shape[0] // CHUNK):
+        both = mm(rows, w_in[:, 2 * CHUNK * chunk : 2 * CHUNK * (chunk + 1)])
+        gate = both[:, :CHUNK]
+        hidden = (gate * jax.nn.sigmoid(gate) * both[:, CHUNK:]).astype(BF16)
+        total = total + mm(hidden, w_out[CHUNK * chunk : CHUNK * (chunk + 1)])
+    return total
+
+
+def experts_kernel(buffer, w_in, w_out, returned, arrived, *scratch):
+    (tokens,) = exchanges(1, [buffer], scratch)
+    greet(tokens)
+    tokens.start()
+    tokens.spread()
+    tokens.near_ready()
+    set_half(tokens.partial, 0, experts_forward_half(half_rows(tokens.groups, 0), w_in, w_out))
+    tokens.to_sibling(0).start()
+    tokens.spread_far()
+    tokens.far_ready()
+    set_half(tokens.partial, 1, experts_forward_half(half_rows(tokens.groups, 1), w_in, w_out))
+    tokens.to_sibling(1).start()
+    tokens.return_far()
+    arrived[...] = tokens.groups[...]
+    tokens.return_home()
+    tokens.finish_dispatch()
+    tokens.finish()
+    returned[...] = tokens.result[...]
+
+
+def keep_forward(half, rows, w_in, both_ref, hidden_ref):
+    count = rows.shape[0]
+    at = half * count
+    for chunk in range(hidden_ref.shape[1] // CHUNK):
+        columns = slice(2 * CHUNK * chunk, 2 * CHUNK * (chunk + 1))
+        both = mm(rows, w_in[:, columns])
+        gate = both[:, :CHUNK]
+        both_ref[at : at + count, columns] = both
+        hidden_ref[at : at + count, CHUNK * chunk : CHUNK * (chunk + 1)] = (
+            gate * jax.nn.sigmoid(gate) * both[:, CHUNK:]
+        ).astype(BF16)
+
+
+def made_half(half, count, hidden_ref, w_out):
+    return mm(hidden_ref[half * count : (half + 1) * count], w_out[...])
+
+
+def back_half(half, grad_rows, w_in, w_out, both_ref, grad_ref):
+    count = grad_rows.shape[0]
+    at = half * count
+    total = 0.0
+    for chunk in range(w_out.shape[0] // CHUNK):
+        columns = slice(2 * CHUNK * chunk, 2 * CHUNK * (chunk + 1))
+        both = both_ref[at : at + count, columns]
+        gate, up = both[:, :CHUNK], both[:, CHUNK:]
+        sig = jax.nn.sigmoid(gate)
+        grad_hidden = mm(grad_rows, w_out[CHUNK * chunk : CHUNK * (chunk + 1)], NT)
+        grad_gate = grad_hidden * up * sig * (1.0 + gate * (1.0 - sig))
+        grad_both = jnp.concatenate([grad_gate, grad_hidden * gate * sig], axis=1).astype(BF16)
+        grad_ref[at : at + count, columns] = grad_both
+        total = total + mm(grad_both, w_in[:, columns], NT)
+    return total
+
+
+def all_rows(ref):
+    groups, owners, room, width = ref.shape
+    return ref[...].reshape(groups * owners * room, width)
+
+
+def experts_both_kernel(buffer, grad_buffer, w_in, w_out, made, returned, grad_in, grad_out, both_ref, hidden_ref, grad_ref, *scratch):
+    tokens, grads = exchanges(2, [buffer, grad_buffer], scratch)
+    count = both_ref.shape[0] // 2
+    greet(tokens)
+    tokens.start()
+    grads.start()
+    tokens.spread()
+    grads.spread()
+    tokens.near_ready()
+    keep_forward(0, half_rows(tokens.groups, 0), w_in, both_ref, hidden_ref)
+    set_half(tokens.partial, 0, made_half(0, count, hidden_ref, w_out))
+    tokens.to_sibling(0).start()
+    grads.near_ready()
+    set_half(grads.partial, 0, back_half(0, half_rows(grads.groups, 0), w_in, w_out, both_ref, grad_ref))
+    grads.to_sibling(0).start()
+    tokens.spread_far()
+    grads.spread_far()
+    tokens.far_ready()
+    keep_forward(1, half_rows(tokens.groups, 1), w_in, both_ref, hidden_ref)
+    set_half(tokens.partial, 1, made_half(1, count, hidden_ref, w_out))
+    tokens.to_sibling(1).start()
+    grads.far_ready()
+    set_half(grads.partial, 1, back_half(1, half_rows(grads.groups, 1), w_in, w_out, both_ref, grad_ref))
+    grads.to_sibling(1).start()
+    tokens.return_far()
+    grads.return_far()
+    grad_out[...] = mm(hidden_ref[...], all_rows(grads.groups), TN).astype(BF16)
+    tokens.return_home()
+    grads.return_home()
+    for chunk in range(grad_in.shape[1] // (2 * CHUNK)):
+        columns = slice(2 * CHUNK * chunk, 2 * CHUNK * (chunk + 1))
+        grad_in[:, columns] = mm(all_rows(tokens.groups), grad_ref[:, columns], TN).astype(BF16)
+    for one in (tokens, grads):
+        one.finish_dispatch()
+        one.finish()
+    made[...] = tokens.result[...]
+    returned[...] = grads.result[...]
+
+
+def experts_back_kernel(grad_buffer, arrived, w_in, w_out, returned, grad_in, grad_out, both_ref, hidden_ref, grad_ref, *scratch):
+    (grads,) = exchanges(1, [grad_buffer], scratch)
+    greet(grads)
+    grads.start()
+    grads.spread()
+    keep_forward(0, half_rows(arrived, 0), w_in, both_ref, hidden_ref)
+    grads.near_ready()
+    set_half(grads.partial, 0, back_half(0, half_rows(grads.groups, 0), w_in, w_out, both_ref, grad_ref))
+    grads.to_sibling(0).start()
+    grads.spread_far()
+    keep_forward(1, half_rows(arrived, 1), w_in, both_ref, hidden_ref)
+    grads.far_ready()
+    set_half(grads.partial, 1, back_half(1, half_rows(grads.groups, 1), w_in, w_out, both_ref, grad_ref))
+    grads.to_sibling(1).start()
+    grads.return_far()
+    grad_out[...] = mm(hidden_ref[...], all_rows(grads.groups), TN).astype(BF16)
+    grads.return_home()
+    for chunk in range(grad_in.shape[1] // (2 * CHUNK)):
+        columns = slice(2 * CHUNK * chunk, 2 * CHUNK * (chunk + 1))
+        grad_in[:, columns] = mm(all_rows(arrived), grad_ref[:, columns], TN).astype(BF16)
+    grads.finish_dispatch()
+    grads.finish()
+    returned[...] = grads.result[...]
+
+
+def run_experts(kernel, identity, streams, blocks, args, out, kept=(), flops=0):
+    owners, room, width = blocks
     return pl.pallas_call(
-        expert_kernel,
-        grid=(w_out.shape[0] // CHUNK,),
-        in_specs=[whole, whole, in_spec, out_spec],
-        out_specs=[whole, whole],
-        out_shape=[shaped((slots, width), BF16)] * 2,
-        scratch_shapes=[pltpu.VMEM((2 * slots, width), F32)],
-        compiler_params=pltpu.CompilerParams(vmem_limit_bytes=VMEM_BYTES),
-        cost_estimate=pl.CostEstimate(flops=12 * slots * width * w_out.shape[0], bytes_accessed=8 << 20, transcendentals=0),
-    )(*arrived, w_in, w_out)
-
-
-def expert_backward(grad_made, arrived, w_in, w_out):
-    slots, width = arrived[0].shape
-    whole, in_spec, out_spec = expert_specs(slots, width)
-    return pl.pallas_call(
-        expert_back_kernel,
-        grid=(w_out.shape[0] // CHUNK,),
-        in_specs=[whole, whole, whole, whole, in_spec, out_spec],
-        out_specs=[whole, whole, in_spec, out_spec],
-        out_shape=[shaped((slots, width), BF16)] * 2 + [shaped(w_in.shape, BF16), shaped(w_out.shape, BF16)],
-        scratch_shapes=[pltpu.VMEM((2 * slots, width), F32)],
-        compiler_params=pltpu.CompilerParams(vmem_limit_bytes=VMEM_BYTES),
-        cost_estimate=pl.CostEstimate(flops=32 * slots * width * w_out.shape[0], bytes_accessed=16 << 20, transcendentals=0),
-    )(*arrived, *grad_made, w_in, w_out)
+        kernel,
+        out_shape=out,
+        in_specs=[pl.BlockSpec(memory_space=pltpu.VMEM) for _ in args],
+        out_specs=[pl.BlockSpec(memory_space=pltpu.VMEM) for _ in out],
+        scratch_shapes=list(kept) + exchange_scratch(streams, owners, room, width),
+        compiler_params=pltpu.CompilerParams(
+            vmem_limit_bytes=VMEM_BYTES, collective_id=identity, has_side_effects=True
+        ),
+        cost_estimate=pl.CostEstimate(flops=flops, bytes_accessed=16 << 20, transcendentals=0),
+    )(*args)
+
 
 def local(
     x_in,
@@ -475,23 +739,48 @@
 
     in_rows, columns = expert_in.shape[2:]
     hidden_here = expert_out.shape[2] // 2
-    chunks = pieces * hidden_here // CHUNK
-    w_in = expert_in[0, 0].reshape(in_rows, 2, pieces, 2, hidden_here)
+    pairs = pieces // 2
+    quarter = pairs * hidden_here
+    chunks = quarter // CHUNK
+    pair_index = lax.axis_index("shard") // 2
+    w_in = expert_in[0, 0].reshape(in_rows, 2, pairs, 2, 2, hidden_here)
 
     def as_chunks(half):
-        half = half.reshape(in_rows, 2, chunks, CHUNK)
-        return jnp.swapaxes(half, 1, 2).reshape(in_rows, columns // 2)
+        half = jnp.moveaxis(half, 3, 0).reshape(2, in_rows, 2, chunks, CHUNK)
+        return jnp.swapaxes(half, 2, 3).reshape(2, in_rows, 2 * quarter)
 
     w_out = expert_out[0, 0].reshape(2, hidden_here, width)
-    ins = by_section(as_chunks(mine(w_in, 3)), swap(as_chunks(others(w_in, 3))))
+    ins = by_section(as_chunks(mine(w_in, 4)), swap(as_chunks(others(w_in, 4))))
     outs = by_section(mine(w_out), swap(others(w_out)))
-    experts = [
-        (
-            lax.all_gather(ins[s], "shard", axis=0, tiled=True),
-            lax.all_gather(outs[s], "shard", axis=0, tiled=True),
+
+    def across(piece, hops):
+        return lax.ppermute(piece, "shard", [(i, (i + 2 * hops) % pieces) for i in range(pieces)])
+
+    def whole_experts(in_pieces, out_piece):
+        sent = jnp.tile(in_pieces, (pairs, 1, 1))
+        got = lax.all_to_all(sent, "shard", split_axis=0, concat_axis=0, tiled=True)
+        parts = jnp.stack([out_piece] + [across(out_piece, hops) for hops in range(1, pairs)])
+        parts = jnp.stack(
+            [lax.dynamic_index_in_dim(parts, (pair_index - i) % pairs, 0, False) for i in range(pairs)]
         )
-        for s in range(2)
-    ]
+        return got.reshape(pieces * in_rows, 2 * quarter), parts.reshape(quarter, width)
+
+    def split_grads(grad_in, grad_out):
+        got = lax.all_to_all(
+            grad_in.reshape(pieces, in_rows, 2 * quarter), "shard", split_axis=0, concat_axis=0, tiled=True
+        )
+        in_sum = jnp.sum(got.reshape(pairs, 2, in_rows, 2 * quarter).astype(F32), axis=0).astype(BF16)
+        grad_out = grad_out.reshape(pairs, hidden_here, width)
+
+        def piece(hops):
+            return lax.dynamic_index_in_dim(grad_out, (pair_index + hops) % pairs, 0, False)
+
+        out_sum = piece(0).astype(F32)
+        for hops in range(1, pairs):
+            out_sum = out_sum + across(piece(hops), hops).astype(F32)
+        return in_sum, out_sum.astype(BF16)
+
+    experts = [whole_experts(ins[s], outs[s]) for s in range(2)]
     rows = attn_qkv.shape[1]
 
     def lanes(array, upto):
@@ -528,89 +817,94 @@
 
     dims = (nffn, nexp, capacity, slots)
     heads = width // HEAD
-
-    def exchanged(blocks):
-        return lax.all_to_all(
-            blocks.reshape(owners, room, width), "expert", split_axis=0, concat_axis=0, tiled=True
-        ).reshape(slots, width)
-
-    def to_owners(blocks):
-        blocks = exchanged(blocks)
-        return blocks, swap(blocks)
-
-    def to_tokens(parts):
-        return exchanged(parts[0]), exchanged(swap(parts[1]))
-
-    kept = []
-    x, r = x_first, r_first
-    results = []
+    blocks = (owners, room, width)
     seg_col, seg_row = seg[:, None], seg[None, :]
-    for s in range(2):
-        w, ints = shared[s], ints_all[s]
-        after, qkv, probs_att, attended, packed, slot_pair, r_next, buffer = run(
-            functools.partial(attend_kernel, dims),
-            [
-                shaped((seq_len, width), F32),
-                shaped((seq_len, 3 * width), BF16),
-                shaped((heads, seq_len, seq_len), BF16),
-                shaped((seq_len, width), BF16),
-                shaped((seq_len, LANES), F32),
-                shaped((seq_len, LANES), jnp.int32),
-                shaped((seq_len, LANES), BF16),
-                shaped((slots, width), BF16),
-            ],
-            (x, r, w, mix_all[s], cosine, sine, seg_col, seg_row, ints, ints[:, 2][None]),
-            flops=2 << 30,
-        )
-        arrived = to_owners(buffer)
-        parts = to_tokens(expert_forward(arrived, *experts[s]))
-        out, picked = run(
-            functools.partial(combine_kernel, dims),
-            [shaped((seq_len, width), BF16), shaped((TOP, seq_len, width), BF16)],
-            (after, packed, slot_pair, ints, *parts, w),
-        )
-        kept.append((x, r, w, ints, after, qkv, probs_att, attended, packed, slot_pair, arrived, picked))
-        results.append(out)
-        x, r = out, r_next
-    grad_y = upstream
-    grad_log = jnp.zeros((seq_len, LANES), F32)
-    x_grads, r_grads, sums = [None, None], [None, None], [None, None]
-    for s in (1, 0):
-        x, r, w, ints, after, qkv, probs_att, attended, packed, slot_pair, arrived, picked = kept[s]
-        (buffer,) = run(
-            functools.partial(give_back_kernel, dims),
-            [shaped((slots, width), BF16)],
-            (grad_y, packed, slot_pair),
-        )
-        given_0, given_1, grad_in, grad_out = expert_backward(to_owners(buffer), arrived, *experts[s])
-        in_sum = lax.psum_scatter(grad_in, "shard", scatter_dimension=0, tiled=True)
-        out_sum = lax.psum_scatter(grad_out, "shard", scatter_dimension=0, tiled=True)
-        parts = to_tokens((given_0, given_1))
-        grad_x, grad_r, grad_mix, grads, _ = run(
-            functools.partial(back_kernel, dims),
-            [
-                shaped((seq_len, width), F32),
-                shaped((seq_len, LANES), F32),
-                shaped((LANES, LANES), F32),
-                shaped(w.shape, BF16),
-                shaped((seq_len, 3 * width), BF16),
-            ],
-            (
-                grad_y, grad_log, after, packed, slot_pair, ints, picked, *parts, r, w, mix_all[s],
-                x, qkv, probs_att, attended, cosine, sine,
-            ),
-            flops=5 << 30,
-        )
-        x_grads[s] = grad_x
-        r_grads[s] = grad_r[:, :nexp]
+    smalls = [w[:, 4 * width :] for w in shared]
+    token_f32 = shaped((seq_len, width), F32)
+    token_b16 = shaped((seq_len, width), BF16)
+    lanes_f32 = shaped((seq_len, LANES), F32)
+    slot_shape = shaped((slots, width), BF16)
+    block_shape = shaped(blocks, BF16)
+    attend_out = [
+        token_f32,
+        shaped((seq_len, 3 * width), BF16),
+        shaped((heads, seq_len, seq_len), BF16),
+        token_b16,
+        lanes_f32,
+        shaped((seq_len, LANES), jnp.int32),
+    ]
+    back_out = [token_f32, lanes_f32, shaped((LANES, LANES), F32), shaped(shared[0].shape, BF16)]
+    grad_qkv = pltpu.VMEM((seq_len, 3 * width), BF16)
+    prio = [ints[:, 2][None] for ints in ints_all]
+    rows_there = 4 * slots
+    kept = [
+        pltpu.VMEM((rows_there, 2 * quarter), F32),
+        pltpu.VMEM((rows_there, quarter), BF16),
+        pltpu.VMEM((rows_there, 2 * quarter), BF16),
+    ]
+    grad_shapes = [shaped((width, 2 * quarter), BF16), shaped((quarter, width), BF16)]
+    work = 2 * rows_there * width * quarter
+
+    w, ints = shared[0], ints_all[0]
+    after_0, qkv_0, probs_0, attended_0, packed_0, slots_0, r_next, buffer = run(
+        functools.partial(attend_kernel, dims),
+        attend_out + [shaped((seq_len, LANES), BF16), slot_shape],
+        (x_first, r_first, w, smalls[0], mix_all[0], cosine, sine, seg_col, seg_row, ints, prio[0]),
+        flops=2 << 30,
+    )
+    returned, arrived = run_experts(
+        experts_kernel, 0, 1, blocks, (buffer.reshape(blocks), *experts[0]),
+        [block_shape, shaped((4,) + blocks, BF16)], flops=3 * work,
+    )
+    out_0, picked_0, after_1, qkv_1, probs_1, attended_1, packed_1, slots_1, buffer, grad_buffer = run(
+        functools.partial(middle_kernel, dims),
+        [token_b16, shaped((TOP, seq_len, width), BF16)] + attend_out + [slot_shape, slot_shape],
+        (
+            after_0, packed_0, slots_0, ints, returned.reshape(slots, width), smalls[0],
+            r_next, shared[1], smalls[1], mix_all[1], cosine, sine, seg_col, seg_row, ints_all[1], prio[1], upstream,
+        ),
+        flops=3 << 30,
+    )
+    made, returned, grad_in_1, grad_out_1 = run_experts(
+        experts_both_kernel, 1, 2, blocks, (buffer.reshape(blocks), grad_buffer.reshape(blocks), *experts[1]),
+        [block_shape, block_shape] + grad_shapes, kept, flops=9 * work,
+    )
+    sums_1 = split_grads(grad_in_1, grad_out_1)
+    out_1, grad_x_1, grad_r_1, grad_mix_1, grads_1, buffer = run(
+        functools.partial(turn_kernel, dims),
+        [token_b16] + back_out + [slot_shape],
+        (
+            upstream, after_1, packed_1, slots_1, ints_all[1], made.reshape(slots, width), returned.reshape(slots, width),
+            r_next, shared[1], smalls[1], mix_all[1], out_0, qkv_1, probs_1, attended_1, cosine, sine, packed_0, slots_0,
+        ),
+        flops=5 << 30,
+        scratch=[grad_qkv, pltpu.VMEM((TOP, seq_len, width), BF16)],
+    )
+    returned, grad_in_0, grad_out_0 = run_experts(
+        experts_back_kernel, 2, 1, blocks, (buffer.reshape(blocks), arrived, *experts[0]),
+        [block_shape] + grad_shapes, kept, flops=9 * work,
+    )
+    sums_0 = split_grads(grad_in_0, grad_out_0)
+    grad_x_0, grad_r_0, grad_mix_0, grads_0 = run(
+        functools.partial(back_kernel, dims),
+        back_out,
+        (
+            grad_x_1, grad_r_1, after_0, packed_0, slots_0, ints, picked_0, returned.reshape(slots, width),
+            r_first, w, smalls[0], mix_all[0], x_first, qkv_0, probs_0, attended_0, cosine, sine,
+        ),
+        flops=5 << 30,
+        scratch=[grad_qkv],
+    )
+    results, x_grads = (out_0, out_1), (grad_x_0, grad_x_1)
+    r_grads = (grad_r_0[:, :nexp], grad_r_1[:, :nexp])
+    sums = []
+    for grads, grad_mix, expert_sums in ((grads_0, grad_mix_0, sums_0), (grads_1, grad_mix_1, sums_1)):
         mix_lanes = -(-nexp * nexp // rows)
         mix_flat = jnp.pad(grad_mix[:nexp, :nexp].reshape(-1), (0, rows * mix_lanes - nexp * nexp)).reshape(rows, mix_lanes)
         mix_tile = jnp.tile(mix_flat, (owners * pieces, 1)).astype(BF16)
         at = 4 * width + AT_MIX
         grads = lax.dynamic_update_slice(grads, mix_tile, (0, at))
-        sums[s] = (grads, in_sum, out_sum)
-        grad_y = grad_x.astype(BF16)
-        grad_log = grad_r.astype(BF16)
+        sums.append((grads, *expert_sums))
     shared_own = jnp.where(first_core, sums[0][0], sums[1][0])
     shared_other = jnp.where(first_core, sums[1][0], sums[0][0])
     shared_sum = (shared_own.astype(F32) + swap(shared_other).astype(F32)).astype(BF16)
@@ -621,11 +915,11 @@
         got = swap(jnp.where(first_core, sums[1][index], sums[0][index]))
         return jnp.where(first_core, own, got).astype(F32), jnp.where(first_core, got, own).astype(F32)
 
-    in_halves = [
-        jnp.swapaxes(half.reshape(in_rows, chunks, 2, CHUNK), 1, 2).reshape(in_rows, 2, pieces, hidden_here)
-        for half in halves(1)
-    ]
-    in_grad = jnp.stack(in_halves, axis=3).reshape(in_rows, columns)
+    def from_chunks(half):
+        half = jnp.swapaxes(half.reshape(2, in_rows, chunks, 2, CHUNK), 2, 3)
+        return jnp.moveaxis(half.reshape(2, in_rows, 2, pairs, hidden_here), 0, 3)
+
+    in_grad = jnp.stack([from_chunks(half) for half in halves(1)], axis=4).reshape(in_rows, columns)
     out_grad = jnp.concatenate(halves(2), axis=0)
 
     def both_batches(pair):

time: 738 us -> 668 us (0.905)
  waiting for transfers between devices: 410 us -> 228 us
  Pallas kernels: 121 us -> 220 us
  blocking collectives: 48.8 us -> 67.8 us
  starting transfers between devices: 33.5 us -> 20.7 us
    ppermute x0 -> x4, waiting for transfers between devices: none -> 135 us  [across(): lax.ppermute(piece, 'shard', [(i, (i + 2 * hops) % pieces) for i in range...]
    reduce_scatter x1, waiting for transfers between devices: 127 us -> 0.01 us  [local(): lax.psum_scatter(shared_sum, ('expert', 'shard'), scatter_dimension=0, ti...]
    pallas_call x12 -> x7, Pallas kernels: 121 us -> 220 us  [the longest x3 155 us: run_experts(): pl.pallas_call(kernel, out_shape=out, in_specs=[pl.BlockSpec(memory_space...]
    all_gather x4 -> x0, waiting for transfers between devices: 89.9 us -> none  [the longest x2 89.8 us: local(): lax.all_gather(ins[s], 'shard', axis=0, tiled=True)]
    reduce_scatter x4 -> x0, waiting for transfers between devices: 79.7 us -> none  [the longest x2 79.7 us: local(): in_sum = lax.psum_scatter(grad_in, 'shard', scatter_dimension=0, tiled=True)]
    all_to_all x8 -> x3, waiting for transfers between devices: 35 us -> 0.01 us  [the longest x2 0.01 us: whole_experts(): got = lax.all_to_all(sent, 'shard', split_axis=0, concat_axis=0, tiled=True)]
    all_gather x1, waiting for transfers between devices: 60.8 us -> 85 us  [local(): shared = lax.all_gather(shared, ('expert', 'shard'), axis=0, tiled=True)]
    all_to_all x4 -> x1, blocking collectives: 48.8 us -> 67.8 us  [split_grads(): lax.all_to_all(grad_in.reshape(pieces, in_rows, 2 * quarter), 'shard', sp...]
  transfers between devices with their start and end apart: 37 -> 20, of which waited for: 19 -> 6; matrix products, arithmetic and copies ran while one was open for 11% -> 11% of each run, Pallas kernels for 17% -> 10%
where the time goes in v3:
time: 668 us; the launch traced here: 658 us
  waiting for transfers between devices  228 us (34%)
  Pallas kernels  220 us (33%)
  blocking collectives  67.8 us (10%)
  local copies, waits for them, and re-layouts  62.8 us (9%)
  other arithmetic  43.7 us (7%)
  starting transfers between devices  20.7 us (3%)
  between operations  15.1 us (2%)
    pallas_call x3, Pallas kernels, run_experts(): pl.pallas_call(kernel, out_shape=out, in_specs=[pl.BlockSpec(memory_space...  155 us
    ppermute x4, waiting for transfers between devices, across(): lax.ppermute(piece, 'shard', [(i, (i + 2 * hops) % pieces) for i in range...  135 us
    all_gather x1, waiting for transfers between devices, local(): shared = lax.all_gather(shared, ('expert', 'shard'), axis=0, tiled=True)  85 us
    all_to_all x1, blocking collectives, split_grads(): lax.all_to_all(grad_in.reshape(pieces, in_rows, 2 * quarter), 'shard', sp...  67.8 us
    pallas_call x4, Pallas kernels, run(): pl.pallas_call(kernel, out_shape=out, in_specs=[pl.BlockSpec(memory_space...  64.7 us
  transfers between devices with their start and end apart: 20, of which 6 were waited for; matrix products, arithmetic and copies ran while one was open for 11% of the time, Pallas kernels for 10%

profile of v3, /device:TPU:0, one launch (start us, length us, event | category | flops | bytes accessed | tf_op | source)
XLA Modules:
  0.0 658.4 jit_solution(8945780818884199599)
XLA Ops:
  12.3 85.0 %all-gather.2.cloned.1.call-done = bf16[768,3200]{1,0:T(8,128)(2,1)} async-done(((bf16[48,3200]{1,0:T(8,128)(2,1)}), bf16[768,3200]{1,0:T(8,128)(2,1)}) %all-gather.2.cloned.1.call-update) | async-done | bytes 4915216 | tf_op jit(solution)/shard_map/all_gather | solution.py:799
  100.2 3.2 constant_dynamic-slice_fusion
  115.5 4.5 all-to-all-start
  134.2 49.3 %collective-permute-done.6 = bf16[256,768]{1,0:T(8,128)(2,1)S(1)} collective-permute-done((bf16[256,768]{1,0:T(8,128)(2,1)S(1)}, bf16[256,768]{1,0:T(8,128)(2,1)S(1)}, u32[]{:S(2)}, u32[]{:S(2)}) %collective-permute-start.6) | collective-permute-done | bytes 393248 | tf_op jit(solution)/shard_map/ppermute | solution.py:757
  183.5 8.0 %collective-permute-done.5 = bf16[256,768]{1,0:T(8,128)(2,1)S(1)} collective-permute-done((bf16[256,768]{1,0:T(8,128)(2,1)S(1)}, bf16[256,768]{1,0:T(8,128)(2,1)S(1)}, u32[]{:S(2)}, u32[]{:S(2)}) %collective-permute-start.5) | collective-permute-done | bytes 393248 | tf_op jit(solution)/shard_map/ppermute | solution.py:757
  194.5 3.6 all-to-all-start.1
  199.5 7.0 %broadcast_select_fusion.1 = (bf16[768,3200]{1,0:T(8,128)(2,1)}, bf16[768,3200]{1,0:T(8,128)(2,1)S(1)}) fusion(bf16[768,3200]{1,0:T(8,128)(2,1)} %collective-permute-done, bf16[768,3200]{1,0:T(8,128)(2,1)} %all-gather.2.cloned.1.call-done, pred[]{:T(512)S(6)} %eq.12), kind=kLoop, calls=%fused_computation.2 | loop fusion | flops 4915200 | bytes 19660800 | tf_op jit(solution)/shard_map/jit(_where)/select_n | solution.py:738
  209.1 11.3 %shard_map.238 = (f32[256,768]{1,0:T(8,128)}, bf16[256,2304]{1,0:T(8,128)(2,1)}, bf16[12,256,256]{2,1,0:T(8,128)(2,1)}, bf16[256,768]{1,0:T(8,128)(2,1)}, f32[25...) custom-call(bf16[256,768]{1,0:T(8,128)(2,1)} %dynamic-slice_bitcast_fusion.4.x, ...), custom_call_target="tpu_custom_call" | custom-call | flops 2147483648 | bytes 8388608 | tf_op jit(solution)/shard_map/pallas_call | solution.py:354
  220.5 42.9 %shard_map.239 = (bf16[4,80,768]{2,1,0:T(8,128)(2,1)}, bf16[4,4,80,768]{3,2,1,0:T(8,128)(2,1)}) custom-call(bf16[4,80,768]{2,1,0:T(8,128)(2,1)} %bitcast.172, bf16[768,1024]{1,0:T(8,128)(2,1)} %bitcast.22.w_in, bf16[512,768]{1,0:T(8,128)(2,1)} %bitcast.140), custom_call_target="tpu_custom_call" | custom-call | flops 3019898880 | bytes 16777216 | tf_op jit(solution)/shard_map/pallas_call | solution.py:687
  263.3 14.7 %shard_map.240 = (bf16[256,768]{1,0:T(8,128)(2,1)}, bf16[2,256,768]{2,1,0:T(8,128)(2,1)}, f32[256,768]{1,0:T(8,128)}, bf16[256,2304]{1,0:T(8,128)(2,1)}, bf16[12...) custom-call(f32[256,768]{1,0:T(8,128)} %get-tuple-element.49.after_0, ...), custom_call_target="tpu_custom_call" | custom-call | flops 3221225472 | bytes 8388608 | tf_op jit(solution)/shard_map/pallas_call | solution.py:354
  279.2 67.6 %shard_map.241 = (bf16[4,80,768]{2,1,0:T(8,128)(2,1)}, bf16[4,80,768]{2,1,0:T(8,128)(2,1)}, bf16[768,1024]{1,0:T(8,128)(2,1)}, bf16[512,768]{1,0:T(8,128)(2,1)}) custom-call(bf16[4,80,768]{2,1,0:T(8,128)(2,1)} %bitcast.169, bf16[4,80,768]{2,1,0:T(8,128)(2,1)} %bitcast.170, bf16[768,1024]{1,0:T(8,128)(2,1)} %bitcast.133, bf16[512,768]{1,0:T(8,128)(2,1)} %bitcast.142), custom_call_target="tpu_custom_call" | custom-call | flops 9059696640 | bytes 16777216 | tf_op jit(solution)/shard_map/pallas_call | solution.py:687
  346.8 20.2 %shard_map.242 = (bf16[256,768]{1,0:T(8,128)(2,1)}, f32[256,768]{1,0:T(8,128)}, f32[256,128]{1,0:T(8,128)}, f32[128,128]{1,0:T(8,128)}, bf16[768,3200]{1,0:T(8,128)(2,1)}, /*index=5*/bf16[320,768]{1,0:T(8,128)(2,1)}) custom-call(f32[256,768]{1,0:T(8,128)} %dynamic-slice_bitcast_fusion.grad_y, f32[256,768]{1,0:T(8,128)} %get-tuple-element.56.after, ...), custom_call_target="tpu_custom_call" | custom-call | flops 5368709120 | bytes 8388608 | tf_op jit(solution)/shard_map/pallas_call | solution.py:354
  367.0 44.6 %shard_map.243 = (bf16[4,80,768]{2,1,0:T(8,128)(2,1)}, bf16[768,1024]{1,0:T(8,128)(2,1)}, bf16[512,768]{1,0:T(8,128)(2,1)}) custom-call(bf16[4,80,768]{2,1,0:T(8,128)(2,1)} %bitcast.166, bf16[4,4,80,768]{3,2,1,0:T(8,128)(2,1)} %get-tuple-element.71.arrived, bf16[768,1024]{1,0:T(8,128)(2,1)} %bitcast.22.w_in, bf16[512,768]{1,0:T(8,128)(2,1)} %bitcast.141), custom_call_target="tpu_custom_call" | custom-call | flops 9059696640 | bytes 16777216 | tf_op jit(solution)/shard_map/pallas_call | solution.py:687
  411.5 18.5 %shard_map.244 = (f32[256,768]{1,0:T(8,128)}, f32[256,128]{1,0:T(8,128)}, f32[128,128]{1,0:T(8,128)}, bf16[768,3200]{1,0:T(8,128)(2,1)}) custom-call(f32[256,768]{1,0:T(8,128)} %get-tuple-element.67.grad_y, f32[256,128]{1,0:T(8,128)} %get-tuple-element.68.grad_log, f32[256,768]{1,0:T(8,128)} %get-tuple-element.49.after_0.after, ...), custom_call_target="tpu_custom_call" | custom-call | flops 5368709120 | bytes 8388608 | tf_op jit(solution)/shard_map/pallas_call | solution.py:354
  431.9 3.1 dynamic_update_slice.6
  435.1 3.1 dynamic_update_slice.7
  441.4 8.3 %collective-permute-done.10 = bf16[768,3200]{1,0:T(8,128)(2,1)} collective-permute-done((bf16[768,3200]{1,0:T(8,128)(2,1)S(1)}, bf16[768,3200]{1,0:T(8,128)(2,1)}, u32[]{:S(2)}, u32[]{:S(2)}) %collective-permute-start.10) | collective-permute-done | bytes 4915232 | tf_op jit(solution)/shard_map/ppermute | solution.py:729
  449.7 7.9 %add_convert_fusion = bf16[768,3200]{1,0:T(8,128)(2,1)} fusion(bf16[768,3200]{1,0:T(8,128)(2,1)} %collective-permute-done.10, bf16[768,3200]{1,0:T(8,128)(2,1)} %dynamic_update_slice.6, bf16[768,3200]{1,0:T(8,128)(2,1)S(1)} %copy-done.2, pred[]{:T(512)S(6)} %eq.12), kind=kLoop, calls=%fused_computation | loop fusion | flops 12288000 | bytes 19660800 | tf_op jit(solution)/shard_map/convert_element_type | solution.py:910
  459.0 67.8 %all_to_all.20 = bf16[4,192,1024]{2,1,0:T(8,128)(2,1)} all-to-all(bf16[4,192,1024]{2,1,0:T(8,128)(2,1)S(1)} %bitcast.132), channel_id=1, replica_groups=mesh['section'=2,'expert'=4,'shard'=4] {'shard'}, dimensions={0} | all-to-all | bytes 3145728 | tf_op jit(solution)/shard_map/all_to_all | solution.py:769
  526.8 4.0 all-to-all-start.3
  540.1 65.4 %collective-permute-done.13 = bf16[256,768]{1,0:T(8,128)(2,1)} collective-permute-done((bf16[256,768]{1,0:T(8,128)(2,1)}, bf16[256,768]{1,0:T(8,128)(2,1)}, u32[]{:S(2)}, u32[]{:S(2)}) %collective-permute-start.13) | collective-permute-done | bytes 393248 | tf_op jit(solution)/shard_map/ppermute | solution.py:757
  605.4 12.4 %collective-permute-done.12 = bf16[256,768]{1,0:T(8,128)(2,1)} collective-permute-done((bf16[256,768]{1,0:T(8,128)(2,1)}, bf16[256,768]{1,0:T(8,128)(2,1)}, u32[]{:S(2)}, u32[]{:S(2)}) %collective-permute-start.12) | collective-permute-done | bytes 393248 | tf_op jit(solution)/shard_map/ppermute | solution.py:757
  634.0 4.0 copy.154
  638.0 5.6 reshape.174
  (181 shorter events, 81.3 us)
Async XLA Ops:
  7.2 118.7 %copy-start = (f32[2,1,256,768]{3,2,1,0:T(8,128)S(1)}, f32[2,1,256,768]{3,2,1,0:T(8,128)}, u32[]{:S(2)}) copy-start(f32[2,1,256,768]{3,2,1,0:T(8,128)} %param.16) | copy-start | bytes 4718596
  7.2 90.1 %all-gather.2.cloned.1.call-start = ((), (), s32[]{:S(2)}) async-start(), calls=%async_computation.5 | async-start | bytes 5222400 | tf_op jit(solution)/shard_map/all_gather | solution.py:799
  97.3 102.2 %collective-permute-start = (bf16[768,3200]{1,0:T(8,128)(2,1)}, bf16[768,3200]{1,0:T(8,128)(2,1)}, u32[]{:S(2)}, u32[]{:S(2)}) collective-permute-start(bf16[768,3200]{1,0:T(8,128)(2,1)} %all-gather.2.cloned.1.call-done), channel_id=1, source_target_pairs={{0,16},{16,0},{1,17},{17,1},{2,18},{18,2},{3,19},{19,3},{4,20},{20... | collective-permute-start | bytes 14745608 | tf_op jit(solution)/shard_map/ppermute | solution.py:729
  106.6 6.2 collective-permute-start.3
  107.8 24.9 %collective-permute-start.1 = (f32[128,128]{1,0:T(8,128)}, f32[128,128]{1,0:T(8,128)}, u32[]{:S(2)}, u32[]{:S(2)}) collective-permute-start(f32[128,128]{1,0:T(8,128)} %pad.38), channel_id=1, source_target_pairs={{0,16},{16,0},{1,17},{17,1},{2,18},{18,2},{3,19},{19,3},{4,20},{20... | collective-permute-start | bytes 196616 | tf_op jit(solution)/shard_map/ppermute | solution.py:729
  108.6 22.3 %collective-permute-start.2 = (s32[256,3]{1,0:T(8,128)}, s32[256,3]{1,0:T(8,128)}, u32[]{:S(2)}, u32[]{:S(2)}) collective-permute-start(s32[256,3]{1,0:T(8,128)} %bitcast.15), channel_id=1, source_target_pairs={{0,16},{16,0},{1,17},{17,1},{2,18},{18,2},{3,19},{19,3},{4,20},{20... | collective-permute-start | bytes 9224 | tf_op jit(solution)/shard_map/ppermute | solution.py:729
  110.9 16.0 %collective-permute-start.4 = (bf16[256,768]{1,0:T(8,128)(2,1)}, bf16[256,768]{1,0:T(8,128)(2,1)}, u32[]{:S(2)}, u32[]{:S(2)}) collective-permute-start(bf16[256,768]{1,0:T(8,128)(2,1)} %dynamic-slice_bitcast_fusion.3), channel_id=1, source_target_pairs={{0,16},{16,0},{1,17},{17,1},{2,18},{18,2},{3,19},{19,3},{4,20},{20... | collective-permute-start | bytes 1179656 | tf_op jit(solution)/shard_map/ppermute | solution.py:729
  115.5 77.6 %all-to-all-start = ((bf16[4,192,1024]{2,1,0:T(8,128)(2,1)}), bf16[4,192,1024]{2,1,0:T(8,128)(2,1)}, u32[]{:S(2)}, u32[]{:S(2)}) async-start(bf16[4,192,1024]{2,1,0:T(8,128)(2,1)} %bitcast.21), calls=%async_computation | async-start | bytes 3145728 | tf_op jit(solution)/shard_map/all_to_all | solution.py:761
  127.9 55.6 %collective-permute-start.6 = (bf16[256,768]{1,0:T(8,128)(2,1)S(1)}, bf16[256,768]{1,0:T(8,128)(2,1)S(1)}, u32[]{:S(2)}, u32[]{:S(2)}) collective-permute-start(bf16[256,768]{1,0:T(8,128)(2,1)S(1)} %get-tuple-element.175), channel_id=1, source_target_pairs={{0,2},{1,3},{2,0},{3,1},{4,6},{5,7},{6,4},{7,5},{8,10},{9,11},{10,... | collective-permute-start | bytes 1179656 | tf_op jit(solution)/shard_map/ppermute | solution.py:757
  130.8 60.7 %collective-permute-start.5 = (bf16[256,768]{1,0:T(8,128)(2,1)S(1)}, bf16[256,768]{1,0:T(8,128)(2,1)S(1)}, u32[]{:S(2)}, u32[]{:S(2)}) collective-permute-start(bf16[256,768]{1,0:T(8,128)(2,1)S(1)} %get-tuple-element.176), channel_id=1, source_target_pairs={{0,2},{1,3},{2,0},{3,1},{4,6},{5,7},{6,4},{7,5},{8,10},{9,11},{10,... | collective-permute-start | bytes 1179656 | tf_op jit(solution)/shard_map/ppermute | solution.py:757
  131.9 60.3 %copy-start.17 = (s32[256,3]{1,0:T(8,128)}, s32[256,3]{1,0:T(8,128)S(1)}, u32[]{:S(2)}) copy-start(s32[256,3]{1,0:T(8,128)S(1)} %get-tuple-element.186.ints.ints_0) | copy-start | bytes 9220
  131.9 60.3 %copy-start.18 = (s32[256,3]{1,0:T(8,128)}, s32[256,3]{1,0:T(8,128)S(1)}, u32[]{:S(2)}) copy-start(s32[256,3]{1,0:T(8,128)S(1)} %get-tuple-element.185.ints) | copy-start | bytes 9220
  194.5 83.6 %all-to-all-start.1 = ((bf16[4,192,1024]{2,1,0:T(8,128)(2,1)}), bf16[4,192,1024]{2,1,0:T(8,128)(2,1)S(1)}, u32[]{:S(2)}, u32[]{:S(2)}) async-start(bf16[4,192,1024]{2,1,0:T(8,128)(2,1)} %bitcast.33), calls=%async_computation.1 | async-start | bytes 3145728 | tf_op jit(solution)/shard_map/all_to_all | solution.py:761
  198.0 445.6 %reduce-scatter.2.cloned.1.call-start = ((), (), s32[]{:S(2)}) async-start(), calls=%async_computation.6 | async-start | bytes 5222400 | tf_op jit(solution)/shard_map/reduce_scatter | solution.py:911
  441.3 8.4 %collective-permute-start.10 = (bf16[768,3200]{1,0:T(8,128)(2,1)S(1)}, bf16[768,3200]{1,0:T(8,128)(2,1)}, u32[]{:S(2)}, u32[]{:S(2)}) collective-permute-start(bf16[768,3200]{1,0:T(8,128)(2,1)S(1)} %broadcast_select_fusion), channel_id=1, source_target_pairs={{0,16},{16,0},{1,17},{17,1},{2,18},{18,2},{3,19},{19,3},{4,20},{20... | collective-permute-start | bytes 14745608 | tf_op jit(solution)/shard_map/ppermute | solution.py:729
  526.8 97.2 %all-to-all-start.3 = ((bf16[4,192,1024]{2,1,0:T(8,128)(2,1)}), bf16[4,192,1024]{2,1,0:T(8,128)(2,1)S(1)}, u32[]{:S(2)}, u32[]{:S(2)}) async-start(bf16[4,192,1024]{2,1,0:T(8,128)(2,1)} %bitcast.64), calls=%async_computation.4 | async-start | bytes 3145728 | tf_op jit(solution)/shard_map/all_to_all | solution.py:769
  530.9 6.8 %collective-permute-start.9 = (f32[256,8]{1,0:T(8,128)S(1)}, f32[256,8]{1,0:T(8,128)S(1)}, u32[]{:S(2)}, u32[]{:S(2)}) collective-permute-start(f32[256,8]{1,0:T(8,128)S(1)} %slice_select_fusion), channel_id=1, source_target_pairs={{0,16},{16,0},{1,17},{17,1},{2,18},{18,2},{3,19},{19,3},{4,20},{20... | collective-permute-start | bytes 24584 | tf_op jit(solution)/shard_map/ppermute | solution.py:729
  531.8 88.3 %collective-permute-start.7 = (bf16[256,768]{1,0:T(8,128)(2,1)}, bf16[256,768]{1,0:T(8,128)(2,1)}, u32[]{:S(2)}, u32[]{:S(2)}) collective-permute-start(bf16[256,768]{1,0:T(8,128)(2,1)} %broadcast_select_fusion.15), channel_id=1, source_target_pairs={{0,16},{16,0},{1,17},{17,1},{2,18},{18,2},{3,19},{19,3},{4,20},{20... | collective-permute-start | bytes 1179656 | tf_op jit(solution)/shard_map/ppermute | solution.py:729
  533.1 72.4 %collective-permute-start.13 = (bf16[256,768]{1,0:T(8,128)(2,1)}, bf16[256,768]{1,0:T(8,128)(2,1)}, u32[]{:S(2)}, u32[]{:S(2)}) collective-permute-start(bf16[256,768]{1,0:T(8,128)(2,1)} %dynamic-slice_bitcast_fusion.1), channel_id=1, source_target_pairs={{0,2},{1,3},{2,0},{3,1},{4,6},{5,7},{6,4},{7,5},{8,10},{9,11},{10,... | collective-permute-start | bytes 1179656 | tf_op jit(solution)/shard_map/ppermute | solution.py:757
  536.7 81.1 %collective-permute-start.12 = (bf16[256,768]{1,0:T(8,128)(2,1)}, bf16[256,768]{1,0:T(8,128)(2,1)}, u32[]{:S(2)}, u32[]{:S(2)}) collective-permute-start(bf16[256,768]{1,0:T(8,128)(2,1)} %dynamic-slice_bitcast_fusion.2), channel_id=1, source_target_pairs={{0,2},{1,3},{2,0},{3,1},{4,6},{5,7},{6,4},{7,5},{8,10},{9,11},{10,... | collective-permute-start | bytes 1179656 | tf_op jit(solution)/shard_map/ppermute | solution.py:757
  537.7 90.0 %collective-permute-start.8 = (f32[256,768]{1,0:T(8,128)}, f32[256,768]{1,0:T(8,128)}, u32[]{:S(2)}, u32[]{:S(2)}) collective-permute-start(f32[256,768]{1,0:T(8,128)} %broadcast_select_fusion.13), channel_id=1, source_target_pairs={{0,16},{16,0},{1,17},{17,1},{2,18},{18,2},{3,19},{19,3},{4,20},{20... | collective-permute-start | bytes 2359304 | tf_op jit(solution)/shard_map/ppermute | solution.py:729
  620.1 4.9 collective-permute-start.14
  624.5 6.4 collective-permute-start.11
  638.0 13.0 %copy-start.1 = (f32[2,1,256,768]{3,2,1,0:T(8,128)S(1)}, f32[2,1,256,768]{3,2,1,0:T(8,128)}, u32[]{:S(2)}) copy-start(f32[2,1,256,768]{3,2,1,0:T(8,128)} %param.16) | copy-start | bytes 4718596
  (23 other events, 81.9 us)
Sparse Core Ops, SparseCore 0:
  12.4 84.8 all-gather.1
  457.7 158.5 reduce-scatter.1

commit v4 on v3

--- a/solution.py
+++ b/solution.py
@@ -129,7 +129,7 @@
         kept = (route[k] < nffn) & (rank_k < capacity)
         places.append(jnp.where(kept, route[k] * stride + rank_k, -1))
         dispatch = dispatch + jnp.where(places[k] == lane_of(rows, slots), 1.0, 0.0)
-    buffer[...] = mm(dispatch.astype(BF16), second_b, TN).astype(BF16)
+    buffer[...] = mm(dispatch.astype(BF16), second_b, TN).astype(BF16).reshape(buffer.shape)
     packed = jnp.where(inside, probs, jnp.where((lane >= AT_PROJ) & (lane < AT_VEC), mixes, 0.0))
     packed = jnp.where(lane == AT_VEC, gates[0], packed)
     packed_ref[...] = jnp.where(lane == AT_VEC + 1, gates[1], packed)
@@ -157,7 +157,7 @@
     rows = after.shape[0]
     second = after * inverse_norm(after) * gain_second
     gates, copied, const, mixes = extras(packed, ints, nffn, nconst)
-    made = blocks[...]
+    made = blocks[...].reshape(slots, after.shape[1])
     slot_lane = lane_of(rows, slots)
     coefficient = copied
     for c in range(nconst):
@@ -180,7 +180,7 @@
         gate = packed[:, AT_VEC + k : AT_VEC + k + 1]
         table = ones_where(slot_pair[:, k : k + 1] == slot_lane)
         total = total + mm(table, (gate * grad_y).astype(BF16), TN)
-    buffer[...] = total.astype(BF16)
+    buffer[...] = total.astype(BF16).reshape(buffer.shape)
 
 
 def moe_back(
@@ -195,7 +195,7 @@
     second = unit * gain_second
     second_b = second.astype(BF16)
     gates, copied, const, mixes = extras(packed, ints, nffn, nconst)
-    grad_buffer = blocks[...]
+    grad_buffer = blocks[...].reshape(slots, after.shape[1])
     slot_lane = lane_of(rows, slots)
     dispatch = sum(jnp.where(slot_pair[:, k : k + 1] == slot_lane, 1.0, 0.0) for k in range(TOP))
     grad_second = mm(dispatch.astype(BF16), grad_buffer)
@@ -697,6 +697,315 @@
     )(*args)
 
 
+class Spread:
+    def __init__(self, packed, in_pieces, out_pieces, attn, w_in, w_out, sems):
+        self.packed, self.in_pieces, self.out_pieces = packed, in_pieces, out_pieces
+        self.attn, self.w_in, self.w_out = attn, w_in, w_out
+        (self.own_sem, self.z_s, self.z_r, self.plane_s, self.plane_r, self.core_s, self.core_r,
+         self.in_s, self.in_r, self.out_s, self.out_r, self.own_in, self.own_out) = sems
+        self.core, self.column, self.place = lax.axis_index("section"), lax.axis_index("expert"), lax.axis_index("shard")
+        self.owners, self.pieces = lax.axis_size("expert"), lax.axis_size("shard")
+
+    def spot(self, column, place):
+        rows = self.packed.shape[0]
+        return pl.ds(pl.multiple_of((column * self.pieces + place) * rows, rows), rows)
+
+    def column_by(self, by):
+        return lax.rem(self.column + by + self.owners, self.owners)
+
+    def place_by(self, by):
+        return lax.rem(self.place + by + self.pieces, self.pieces)
+
+    def copy(self, source, target, send, recv, device):
+        return pltpu.make_async_remote_copy(source, target, send, recv, device_id=device, device_id_type=MESH)
+
+    def own(self):
+        return pltpu.make_async_copy(self.packed, self.attn.at[self.core, self.spot(self.column, self.place)], self.own_sem)
+
+    def along(self, by):
+        block = self.attn.at[self.core, self.spot(self.column, self.place)]
+        return self.copy(self.packed, block, self.z_s.at[by], self.z_r.at[by], (self.core, self.column, self.place_by(by)))
+
+    def along_in(self, by):
+        block = self.attn.at[self.core, self.spot(self.column, self.place_by(-by))]
+        return self.copy(self.packed, block, self.z_s.at[by], self.z_r.at[by], (self.core, self.column, self.place_by(-by)))
+
+    def plane(self, back, by):
+        block = self.attn.at[self.core, self.spot(self.column, self.place_by(-back))]
+        source = self.packed if back == 0 else block
+        return self.copy(
+            source, block, self.plane_s.at[back, by], self.plane_r.at[back, by], (self.core, self.column_by(by), self.place)
+        )
+
+    def plane_in(self, back, by):
+        block = self.attn.at[self.core, self.spot(self.column_by(-by), self.place_by(-back))]
+        return self.copy(
+            block, block, self.plane_s.at[back, by], self.plane_r.at[back, by], (self.core, self.column_by(-by), self.place)
+        )
+
+    def over(self, back, by, section):
+        block = self.attn.at[section, self.spot(self.column_by(-by), self.place_by(-back))]
+        source = self.packed if back == 0 and by == 0 else block
+        return self.copy(
+            source, block, self.core_s.at[back, by], self.core_r.at[back, by], (1 - self.core, self.column, self.place)
+        )
+
+    def begin(self):
+        self.own().start()
+        for by in range(1, self.pieces):
+            self.along(by).start()
+        for by in range(1, self.owners):
+            self.plane(0, by).start()
+        self.over(0, 0, self.core).start()
+
+    def pass_on(self):
+        for back in range(1, self.pieces):
+            self.along_in(back).wait_recv()
+            for by in range(1, self.owners):
+                self.plane(back, by).start()
+            self.over(back, 0, self.core).start()
+
+    def pass_over(self):
+        for back in range(self.pieces):
+            for by in range(1, self.owners):
+                self.plane_in(back, by).wait_recv()
+                self.over(back, by, self.core).start()
+        self.own().wait()
+
+    def over_ready(self):
+        for back in range(self.pieces):
+            for by in range(self.owners):
+                self.over(back, by, 1 - self.core).wait_recv()
+
+    def finish_attn(self):
+        for by in range(1, self.pieces):
+            self.along(by).wait_send()
+        for back in range(self.pieces):
+            for by in range(1, self.owners):
+                self.plane(back, by).wait_send()
+            for by in range(self.owners):
+                self.over(back, by, self.core).wait_send()
+
+    def in_rows(self, place):
+        rows = self.in_pieces.shape[2]
+        return pl.ds(pl.multiple_of(place * rows, rows), rows)
+
+    def out_rows(self, place):
+        rows = self.out_pieces.shape[1]
+        return pl.ds(pl.multiple_of(lax.div(place, 2) * rows, rows), rows)
+
+    def in_copy(self, cross, by):
+        core = 1 - self.core if cross else self.core
+        place = self.place_by(by)
+        return self.copy(
+            self.in_pieces.at[core, lax.rem(place, 2)], self.w_in.at[self.core, self.in_rows(self.place)],
+            self.in_s.at[cross, by], self.in_r.at[cross, by], (core, self.column, place),
+        )
+
+    def in_here(self, cross, by):
+        core = 1 - self.core if cross else self.core
+        place = self.place_by(-by)
+        return self.copy(
+            self.in_pieces.at[core, lax.rem(place, 2)], self.w_in.at[core, self.in_rows(place)],
+            self.in_s.at[cross, by], self.in_r.at[cross, by], (core, self.column, place),
+        )
+
+    def out_copy(self, cross, by):
+        core = 1 - self.core if cross else self.core
+        return self.copy(
+            self.out_pieces.at[core], self.w_out.at[self.core, self.out_rows(self.place)],
+            self.out_s.at[cross, by // 2], self.out_r.at[cross, by // 2], (core, self.column, self.place_by(by)),
+        )
+
+    def out_here(self, cross, by):
+        core = 1 - self.core if cross else self.core
+        place = self.place_by(-by)
+        return self.copy(
+            self.out_pieces.at[core], self.w_out.at[core, self.out_rows(place)],
+            self.out_s.at[cross, by // 2], self.out_r.at[cross, by // 2], (core, self.column, place),
+        )
+
+    def own_pieces(self):
+        return (
+            pltpu.make_async_copy(
+                self.in_pieces.at[self.core, lax.rem(self.place, 2)],
+                self.w_in.at[self.core, self.in_rows(self.place)], self.own_in,
+            ),
+            pltpu.make_async_copy(
+                self.out_pieces.at[self.core], self.w_out.at[self.core, self.out_rows(self.place)], self.own_out
+            ),
+        )
+
+    def expert_routes(self):
+        for by in range(self.pieces):
+            for cross in (0, 1):
+                if by or cross:
+                    yield cross, by
+
+    def begin_experts(self):
+        for one in self.own_pieces():
+            one.start()
+        for cross, by in self.expert_routes():
+            self.in_copy(cross, by).start()
+            if by % 2 == 0:
+                self.out_copy(cross, by).start()
+
+    def experts_ready(self, cross):
+        for way, by in self.expert_routes():
+            if way == cross:
+                self.in_here(cross, by).wait_recv()
+                if by % 2 == 0:
+                    self.out_here(cross, by).wait_recv()
+        if not cross:
+            for one in self.own_pieces():
+                one.wait()
+
+    def finish_experts(self):
+        for cross, by in self.expert_routes():
+            self.in_copy(cross, by).wait_send()
+            if by % 2 == 0:
+                self.out_copy(cross, by).wait_send()
+
+
+def spread_scratch(owners, pieces):
+    dma = pltpu.SemaphoreType.DMA
+    return [
+        dma, dma((pieces,)), dma((pieces,)), dma((pieces, owners)), dma((pieces, owners)), dma((pieces, owners)),
+        dma((pieces, owners)), dma((2, pieces)), dma((2, pieces)), dma((2, pieces // 2)), dma((2, pieces // 2)), dma, dma,
+    ]
+
+
+SPREAD_SEMS = 13
+
+
+def greet_all(spread):
+    barrier = pltpu.get_barrier_semaphore()
+    for by in range(1, spread.owners):
+        pl.semaphore_signal(
+            barrier, inc=1, device_id=(spread.core, spread.column_by(by), spread.place), device_id_type=MESH
+        )
+    for cross, by in spread.expert_routes():
+        core = 1 - spread.core if cross else spread.core
+        pl.semaphore_signal(barrier, inc=1, device_id=(core, spread.column, spread.place_by(by)), device_id_type=MESH)
+    pl.semaphore_wait(barrier, spread.owners - 1 + 2 * spread.pieces - 1)
+
+
+def front_kernel(
+    dims, inside,
+    packed, in_pieces, out_pieces, x, r, mix, cosine, sine, seg_col, seg_row, ints, prio_row, grad_y, *rest,
+):
+    if inside:
+        attn, *rest = rest
+    else:
+        attn, *rest = rest
+    (w_in, w_out, arrived, after_0, qkv_0, probs_0, attended_0, packed_0, slots_0, r_next,
+     out, picked, after_1, qkv_1, probs_1, attended_1, packed_1, slots_1, buffer, grad_buffer, *scratch) = rest
+    small, first_buffer = scratch[:2]
+    width = x.shape[1]
+    spread = Spread(packed, in_pieces, out_pieces, attn, w_in, w_out, scratch[2 : 2 + SPREAD_SEMS])
+    (tokens,) = exchanges(1, [first_buffer], scratch[2 + SPREAD_SEMS :])
+    first, second = spread.core == 0, spread.core == 1
+    greet_all(spread)
+
+    @pl.when(first)
+    def _():
+        if inside:
+            spread.begin()
+            spread.pass_on()
+            spread.pass_over()
+        spread.begin_experts()
+
+    @pl.when(second)
+    def _():
+        if inside:
+            spread.over_ready()
+            spread.begin()
+
+    small[0] = attn[0, :, 4 * width :]
+    attend_kernel(
+        dims, x, r, attn.at[0], small.at[0], mix.at[0], cosine, sine, seg_col, seg_row, ints.at[0], prio_row.at[0],
+        after_0, qkv_0, probs_0, attended_0, packed_0, slots_0, r_next, first_buffer,
+    )
+    tokens.start()
+
+    @pl.when(second)
+    def _():
+        if inside:
+            spread.pass_on()
+
+    tokens.spread()
+
+    @pl.when(second)
+    def _():
+        if inside:
+            spread.pass_over()
+        spread.begin_experts()
+
+    @pl.when(first)
+    def _():
+        spread.experts_ready(0)
+
+    @pl.when(second)
+    def _():
+        spread.experts_ready(1)
+
+    tokens.near_ready()
+    set_half(tokens.partial, 0, experts_forward_half(half_rows(tokens.groups, 0), w_in.at[0], w_out.at[0]))
+    tokens.to_sibling(0).start()
+    tokens.spread_far()
+    tokens.far_ready()
+    set_half(tokens.partial, 1, experts_forward_half(half_rows(tokens.groups, 1), w_in.at[0], w_out.at[0]))
+    tokens.to_sibling(1).start()
+    tokens.return_far()
+    arrived[...] = tokens.groups[...]
+    tokens.return_home()
+    tokens.finish_dispatch()
+    tokens.finish()
+    if inside:
+
+        @pl.when(first)
+        def _():
+            spread.over_ready()
+
+    small[1] = attn[1, :, 4 * width :]
+    middle_kernel(
+        dims, after_0, packed_0, slots_0, ints.at[0], tokens.result, small.at[0],
+        r_next, attn.at[1], small.at[1], mix.at[1], cosine, sine, seg_col, seg_row, ints.at[1], prio_row.at[1], grad_y,
+        out, picked, after_1, qkv_1, probs_1, attended_1, packed_1, slots_1, buffer, grad_buffer,
+    )
+
+    @pl.when(first)
+    def _():
+        spread.experts_ready(1)
+
+    @pl.when(second)
+    def _():
+        spread.experts_ready(0)
+
+    if inside:
+        spread.finish_attn()
+    spread.finish_experts()
+
+
+def run_front(dims, inside, args, out, owners, pieces, blocks, width):
+    vmem, anywhere = pl.BlockSpec(memory_space=pltpu.VMEM), pl.BlockSpec(memory_space=pl.ANY)
+    in_specs = [vmem] * len(args)
+    in_specs[1] = in_specs[2] = anywhere
+    return pl.pallas_call(
+        functools.partial(front_kernel, dims, inside),
+        out_shape=out,
+        in_specs=in_specs,
+        out_specs=[vmem] * len(out),
+        scratch_shapes=[pltpu.VMEM((2, width, LANES), BF16), pltpu.VMEM(blocks, BF16)]
+        + spread_scratch(owners, pieces)
+        + exchange_scratch(1, *blocks),
+        compiler_params=pltpu.CompilerParams(
+            vmem_limit_bytes=VMEM_BYTES, collective_id=0, has_side_effects=True
+        ),
+        cost_estimate=pl.CostEstimate(flops=8 << 30, bytes_accessed=40 << 20, transcendentals=0),
+    )(*args)
+
+
 def local(
     x_in,
     cotangent,
@@ -750,20 +1059,10 @@
         return jnp.swapaxes(half, 2, 3).reshape(2, in_rows, 2 * quarter)
 
     w_out = expert_out[0, 0].reshape(2, hidden_here, width)
-    ins = by_section(as_chunks(mine(w_in, 4)), swap(as_chunks(others(w_in, 4))))
-    outs = by_section(mine(w_out), swap(others(w_out)))
+    in_pieces = jnp.stack([as_chunks(w_in[:, :, :, :, half]) for half in range(2)])
 
     def across(piece, hops):
         return lax.ppermute(piece, "shard", [(i, (i + 2 * hops) % pieces) for i in range(pieces)])
-
-    def whole_experts(in_pieces, out_piece):
-        sent = jnp.tile(in_pieces, (pairs, 1, 1))
-        got = lax.all_to_all(sent, "shard", split_axis=0, concat_axis=0, tiled=True)
-        parts = jnp.stack([out_piece] + [across(out_piece, hops) for hops in range(1, pairs)])
-        parts = jnp.stack(
-            [lax.dynamic_index_in_dim(parts, (pair_index - i) % pairs, 0, False) for i in range(pairs)]
-        )
-        return got.reshape(pieces * in_rows, 2 * quarter), parts.reshape(quarter, width)
 
     def split_grads(grad_in, grad_out):
         got = lax.all_to_all(
@@ -780,7 +1079,6 @@
             out_sum = out_sum + across(piece(hops), hops).astype(F32)
         return in_sum, out_sum.astype(BF16)
 
-    experts = [whole_experts(ins[s], outs[s]) for s in range(2)]
     rows = attn_qkv.shape[1]
 
     def lanes(array, upto):
@@ -795,13 +1093,16 @@
         ],
         axis=1,
     )
-    shared = jnp.concatenate([attn_qkv[0], attn_out[0], small], axis=1)
-    shared = lax.all_gather(shared, ("expert", "shard"), axis=0, tiled=True)
-    shared = by_section(shared, swap(shared))
+    packed = jnp.concatenate([attn_qkv[0], attn_out[0], small], axis=1)
+    inside = rows % 16 == 0
+    given = []
+    if not inside:
+        shared = lax.all_gather(packed, ("expert", "shard"), axis=0, tiled=True)
+        given = [jnp.stack(by_section(shared, swap(shared)))]
     mix_own = jnp.pad(gate_mix[0], ((0, LANES - nexp), (0, LANES - nexp)))
-    mix_all = by_section(mix_own, swap(mix_own))
+    mix_all = jnp.stack(by_section(mix_own, swap(mix_own)))
     ints_own = jnp.concatenate([routes[0, :, 0], priority[0, :, 0, :, None]], axis=-1)
-    ints_all = by_section(mine(ints_own), swap(others(ints_own)))
+    ints_all = jnp.stack(by_section(mine(ints_own), swap(others(ints_own))))
     x_first = mine(x_in[:, 0])
     r_first = jnp.pad(mine(gate_prev[:, 0]), ((0, 0), (0, LANES - nexp)))
     upstream = mine(cotangent[:, 0])
@@ -819,7 +1120,6 @@
     heads = width // HEAD
     blocks = (owners, room, width)
     seg_col, seg_row = seg[:, None], seg[None, :]
-    smalls = [w[:, 4 * width :] for w in shared]
     token_f32 = shaped((seq_len, width), F32)
     token_b16 = shaped((seq_len, width), BF16)
     lanes_f32 = shaped((seq_len, LANES), F32)
@@ -833,9 +1133,10 @@
         lanes_f32,
         shaped((seq_len, LANES), jnp.int32),
     ]
-    back_out = [token_f32, lanes_f32, shaped((LANES, LANES), F32), shaped(shared[0].shape, BF16)]
+    attn_shape = shaped((width, 4 * width + LANES), BF16)
+    back_out = [token_f32, lanes_f32, shaped((LANES, LANES), F32), attn_shape]
     grad_qkv = pltpu.VMEM((seq_len, 3 * width), BF16)
-    prio = [ints[:, 2][None] for ints in ints_all]
+    prio = ints_all[:, None, :, 2]
     rows_there = 4 * slots
     kept = [
         pltpu.VMEM((rows_there, 2 * quarter), F32),
@@ -845,26 +1146,22 @@
     grad_shapes = [shaped((width, 2 * quarter), BF16), shaped((quarter, width), BF16)]
     work = 2 * rows_there * width * quarter
 
+    middle_out = [token_b16, shaped((TOP, seq_len, width), BF16)] + attend_out + [slot_shape, slot_shape]
+    outs = [shaped((2, width, 2 * quarter), BF16), shaped((2, quarter, width), BF16), shaped((4,) + blocks, BF16)]
+    outs += attend_out + [shaped((seq_len, LANES), BF16)] + middle_out
+    if inside:
+        outs = [shaped((2,) + attn_shape.shape, BF16)] + outs
+    got = run_front(
+        dims, inside,
+        [packed, in_pieces, w_out, x_first, r_first, mix_all, cosine, sine, seg_col, seg_row, ints_all, prio, upstream] + given,
+        outs, owners, pieces, blocks, width,
+    )
+    (attn_all, w_in_all, w_out_all, arrived, after_0, qkv_0, probs_0, attended_0, packed_0, slots_0, r_next,
+     out_0, picked_0, after_1, qkv_1, probs_1, attended_1, packed_1, slots_1, buffer, grad_buffer) = given + list(got)
+    shared = (attn_all[0], attn_all[1])
+    smalls = [w[:, 4 * width :] for w in shared]
+    experts = [(w_in_all[s], w_out_all[s]) for s in range(2)]
     w, ints = shared[0], ints_all[0]
-    after_0, qkv_0, probs_0, attended_0, packed_0, slots_0, r_next, buffer = run(
-        functools.partial(attend_kernel, dims),
-        attend_out + [shaped((seq_len, LANES), BF16), slot_shape],
-        (x_first, r_first, w, smalls[0], mix_all[0], cosine, sine, seg_col, seg_row, ints, prio[0]),
-        flops=2 << 30,
-    )
-    returned, arrived = run_experts(
-        experts_kernel, 0, 1, blocks, (buffer.reshape(blocks), *experts[0]),
-        [block_shape, shaped((4,) + blocks, BF16)], flops=3 * work,
-    )
-    out_0, picked_0, after_1, qkv_1, probs_1, attended_1, packed_1, slots_1, buffer, grad_buffer = run(
-        functools.partial(middle_kernel, dims),
-        [token_b16, shaped((TOP, seq_len, width), BF16)] + attend_out + [slot_shape, slot_shape],
-        (
-            after_0, packed_0, slots_0, ints, returned.reshape(slots, width), smalls[0],
-            r_next, shared[1], smalls[1], mix_all[1], cosine, sine, seg_col, seg_row, ints_all[1], prio[1], upstream,
-        ),
-        flops=3 << 30,
-    )
     made, returned, grad_in_1, grad_out_1 = run_experts(
         experts_both_kernel, 1, 2, blocks, (buffer.reshape(blocks), grad_buffer.reshape(blocks), *experts[1]),
         [block_shape, block_shape] + grad_shapes, kept, flops=9 * work,

time: 668 us -> 617 us (0.924)
  waiting for transfers between devices: 228 us -> 85.7 us
  Pallas kernels: 220 us -> 339 us
  starting transfers between devices: 20.7 us -> 8.72 us
  other arithmetic: 43.7 us -> 34.3 us
    pallas_call x0 -> x1, Pallas kernels: none -> 192 us  [run_front(): pl.pallas_call(functools.partial(front_kernel, dims, inside), out_shape=o...]
    all_gather x1 -> x0, waiting for transfers between devices: 85 us -> none  [local(): shared = lax.all_gather(shared, ('expert', 'shard'), axis=0, tiled=True)]
    ppermute x4 -> x2, waiting for transfers between devices: 135 us -> 77.4 us  [across(): lax.ppermute(piece, 'shard', [(i, (i + 2 * hops) % pieces) for i in range...]
    pallas_call x3 -> x2, Pallas kernels: 155 us -> 109 us  [run_experts(): pl.pallas_call(kernel, out_shape=out, in_specs=[pl.BlockSpec(memory_space...]
    pallas_call x4 -> x2, Pallas kernels: 64.7 us -> 38.7 us  [run(): pl.pallas_call(kernel, out_shape=out, in_specs=[pl.BlockSpec(memory_space...]
    select_n x5 -> x2, other arithmetic: 11.8 us -> 0.03 us  [by_section(): jnp.where(first_core, own, other)]
    squeeze x1 -> x3, local copies, waits for them, and re-layouts: 1.77 us -> 11.5 us  [the longest x1 6.82 us: local(): shared = (attn_all[0], attn_all[1])]
    all_to_all x2 -> x0, starting transfers between devices: 8.05 us -> none  [whole_experts(): got = lax.all_to_all(sent, 'shard', split_axis=0, concat_axis=0, tiled=True)]
  transfers between devices with their start and end apart: 20 -> 12, of which waited for: 6 -> 3; matrix products, arithmetic and copies ran while one was open for 11% -> 8% of each run, Pallas kernels for 10% -> 0%
where the time goes in v4:
time: 617 us; the launch traced here: 610 us
  Pallas kernels  339 us (55%)
  waiting for transfers between devices  85.7 us (14%)
  blocking collectives  66.1 us (11%)
  local copies, waits for them, and re-layouts  61.4 us (10%)
  other arithmetic  34.3 us (6%)
  between operations  14.9 us (2%)
  starting transfers between devices  8.72 us (1%)
    pallas_call x1, Pallas kernels, run_front(): pl.pallas_call(functools.partial(front_kernel, dims, inside), out_shape=o...  192 us
    pallas_call x2, Pallas kernels, run_experts(): pl.pallas_call(kernel, out_shape=out, in_specs=[pl.BlockSpec(memory_space...  109 us
    ppermute x2, waiting for transfers between devices, across(): lax.ppermute(piece, 'shard', [(i, (i + 2 * hops) % pieces) for i in range...  77.4 us
    all_to_all x1, blocking collectives, split_grads(): lax.all_to_all(grad_in.reshape(pieces, in_rows, 2 * quarter), 'shard', sp...  66.1 us
    pallas_call x2, Pallas kernels, run(): pl.pallas_call(kernel, out_shape=out, in_specs=[pl.BlockSpec(memory_space...  38.7 us
  transfers between devices with their start and end apart: 12, of which 3 were waited for; matrix products, arithmetic and copies ran while one was open for 8% of the time, Pallas kernels for 0%

profile of v4, /device:TPU:0, one launch (start us, length us, event | category | flops | bytes accessed | tf_op | source)
XLA Modules:
  0.0 610.4 jit_solution(12789024864582145785)
XLA Ops:
  16.2 2.2 fusion.10
  30.0 191.5 %shard_map.238 = (bf16[2,768,3200]{2,1,0:T(8,128)(2,1)}, bf16[2,768,1024]{2,1,0:T(8,128)(2,1)}, bf16[2,512,768]{2,1,0:T(8,128)(2,1)}, bf16[4,4,80,768]{3,2,1,0:T...) custom-call(bf16[48,3200]{1,0:T(8,128)(2,1)} %concatenate.16.packed,, ...), custom_call_target="tpu_custom_call" | custom-call | flops 8589934592 | bytes 41943040 | tf_op jit(solution)/shard_map/pallas_call | solution.py:994
  221.6 2.8 slice_bitcast_fusion.4
  224.4 2.0 slice_bitcast_fusion.2
  226.3 6.8 %slice_bitcast_fusion = (bf16[768,3200]{1,0:T(8,128)(2,1)S(1)}, bf16[768,3200]{1,0:T(8,128)(2,1)}) fusion(bf16[2,768,3200]{2,1,0:T(8,128)(2,1)} %get-tuple-element.61), kind=kLoop, calls=%fused_computation.1 | loop fusion | bytes 19660800 | tf_op jit(solution)/shard_map/squeeze | solution.py:1161
  233.9 1.9 slice.103.small
  235.8 63.9 %shard_map.239 = (bf16[4,80,768]{2,1,0:T(8,128)(2,1)}, bf16[4,80,768]{2,1,0:T(8,128)(2,1)}, bf16[768,1024]{1,0:T(8,128)(2,1)}, bf16[512,768]{1,0:T(8,128)(2,1)}) custom-call(bf16[4,80,768]{2,1,0:T(8,128)(2,1)} %bitcast.158, bf16[4,80,768]{2,1,0:T(8,128)(2,1)} %bitcast.159, bf16[768,1024]{1,0:T(8,128)(2,1)} %get-tuple-element.166.w_in, ...), custom_call_target="tpu_custom_call" | custom-call | flops 9059696640 | bytes 16777216 | tf_op jit(solution)/shard_map/pallas_call | solution.py:687
  299.7 20.2 %shard_map.240 = (bf16[256,768]{1,0:T(8,128)(2,1)}, f32[256,768]{1,0:T(8,128)}, f32[256,128]{1,0:T(8,128)}, f32[128,128]{1,0:T(8,128)}, bf16[768,3200]{1,0:T(8,128)(2,1)}, /*index=5*/bf16[320,768]{1,0:T(8,128)(2,1)}) custom-call(f32[256,768]{1,0:T(8,128)} %dynamic-slice_bitcast_fusion.grad_y, f32[256,768]{1,0:T(8,128)} %get-tuple-element.51.after, ...), custom_call_target="tpu_custom_call" | custom-call | flops 5368709120 | bytes 8388608 | tf_op jit(solution)/shard_map/pallas_call | solution.py:354
  319.9 45.1 %shard_map.241 = (bf16[4,80,768]{2,1,0:T(8,128)(2,1)}, bf16[768,1024]{1,0:T(8,128)(2,1)}, bf16[512,768]{1,0:T(8,128)(2,1)}) custom-call(bf16[4,80,768]{2,1,0:T(8,128)(2,1)} %bitcast.160, bf16[4,4,80,768]{3,2,1,0:T(8,128)(2,1)} %get-tuple-element.73.arrived, bf16[768,1024]{1,0:T(8,128)(2,1)} %get-tuple-element.165.w_in, bf16[512,768]{1,0:T(8,128)(2,1)} %get-tuple-element.171.w_out), custom_call_target="tpu_custom_call" | custom-call | flops 9059696640 | bytes 16777216 | tf_op jit(solution)/shard_map/pallas_call | solution.py:687
  365.0 18.6 %shard_map.242 = (f32[256,768]{1,0:T(8,128)}, f32[256,128]{1,0:T(8,128)}, f32[128,128]{1,0:T(8,128)}, bf16[768,3200]{1,0:T(8,128)(2,1)}) custom-call(f32[256,768]{1,0:T(8,128)} %get-tuple-element.68.grad_y, f32[256,128]{1,0:T(8,128)} %get-tuple-element.69.grad_log, f32[256,768]{1,0:T(8,128)} %get-tuple-element.70.after, ...), custom_call_target="tpu_custom_call" | custom-call | flops 5368709120 | bytes 8388608 | tf_op jit(solution)/shard_map/pallas_call | solution.py:354
  385.4 3.2 dynamic_update_slice.6
  388.6 3.1 dynamic_update_slice.7
  391.8 3.1 broadcast_select_fusion
  394.9 8.3 %collective-permute-done.5 = bf16[768,3200]{1,0:T(8,128)(2,1)} collective-permute-done((bf16[768,3200]{1,0:T(8,128)(2,1)S(1)}, bf16[768,3200]{1,0:T(8,128)(2,1)}, u32[]{:S(2)}, u32[]{:S(2)}) %collective-permute-start.5) | collective-permute-done | bytes 4915232 | tf_op jit(solution)/shard_map/ppermute | solution.py:1038
  403.2 7.9 %add_convert_fusion = bf16[768,3200]{1,0:T(8,128)(2,1)} fusion(bf16[768,3200]{1,0:T(8,128)(2,1)} %collective-permute-done.5, bf16[768,3200]{1,0:T(8,128)(2,1)} %dynamic_update_slice.6, bf16[768,3200]{1,0:T(8,128)(2,1)S(1)} %copy-done.2, pred[]{:T(512)S(6)} %eq.8), kind=kLoop, calls=%fused_computation | loop fusion | flops 12288000 | bytes 19660800 | tf_op jit(solution)/shard_map/convert_element_type | solution.py:1207
  412.5 66.1 %all_to_all.10 = bf16[4,192,1024]{2,1,0:T(8,128)(2,1)} all-to-all(bf16[4,192,1024]{2,1,0:T(8,128)(2,1)S(1)} %bitcast.129), channel_id=1, replica_groups=mesh['section'=2,'expert'=4,'shard'=4] {'shard'}, dimensions={0} | all-to-all | bytes 3145728 | tf_op jit(solution)/shard_map/all_to_all | solution.py:1068
  478.7 3.9 all-to-all-start
  482.7 1.9 dynamic-slice_bitcast_fusion.1
  484.5 2.9 collective-permute-start.8
  493.8 67.6 %collective-permute-done.8 = bf16[256,768]{1,0:T(8,128)(2,1)} collective-permute-done((bf16[256,768]{1,0:T(8,128)(2,1)}, bf16[256,768]{1,0:T(8,128)(2,1)}, u32[]{:S(2)}, u32[]{:S(2)}) %collective-permute-start.8) | collective-permute-done | bytes 393248 | tf_op jit(solution)/shard_map/ppermute | solution.py:1065
  561.4 9.8 %collective-permute-done.7 = bf16[256,768]{1,0:T(8,128)(2,1)} collective-permute-done((bf16[256,768]{1,0:T(8,128)(2,1)S(1)}, bf16[256,768]{1,0:T(8,128)(2,1)}, u32[]{:S(2)}, u32[]{:S(2)}) %collective-permute-start.7) | collective-permute-done | bytes 393248 | tf_op jit(solution)/shard_map/ppermute | solution.py:1065
  571.2 2.4 broadcast_select_fusion.7
  586.2 4.1 copy.152
  590.3 5.6 reshape.134
  (164 shorter events, 50.7 us)
Async XLA Ops:
  7.2 588.7 %reduce-scatter.2.cloned.1.call-start = ((), (), s32[]{:S(2)}) async-start(), calls=%async_computation.3 | async-start | bytes 5222400 | tf_op jit(solution)/shard_map/reduce_scatter | solution.py:1208
  8.1 21.2 %collective-permute-start = (f32[128,128]{1,0:T(8,128)S(1)}, f32[128,128]{1,0:T(8,128)S(1)}, u32[]{:S(2)}, u32[]{:S(2)}) collective-permute-start(f32[128,128]{1,0:T(8,128)S(1)} %pad.38), channel_id=1, source_target_pairs={{0,16},{16,0},{1,17},{17,1},{2,18},{18,2},{3,19},{19,3},{4,20},{20... | collective-permute-start | bytes 196616 | tf_op jit(solution)/shard_map/ppermute | solution.py:1038
  9.4 18.3 %collective-permute-start.1 = (s32[256,3]{1,0:T(8,128)S(1)}, s32[256,3]{1,0:T(8,128)S(1)}, u32[]{:S(2)}, u32[]{:S(2)}) collective-permute-start(s32[256,3]{1,0:T(8,128)S(1)} %bitcast.144), channel_id=1, source_target_pairs={{0,16},{16,0},{1,17},{17,1},{2,18},{18,2},{3,19},{19,3},{4,20},{20... | collective-permute-start | bytes 9224 | tf_op jit(solution)/shard_map/ppermute | solution.py:1038
  27.7 193.8 %copy-start.15 = (s32[256,3]{1,0:T(8,128)}, s32[256,3]{1,0:T(8,128)S(1)}, u32[]{:S(2)}) copy-start(s32[256,3]{1,0:T(8,128)S(1)} %get-tuple-element.183.ints) | copy-start | bytes 9220
  27.7 193.8 %copy-start.16 = (s32[256,3]{1,0:T(8,128)}, s32[256,3]{1,0:T(8,128)S(1)}, u32[]{:S(2)}) copy-start(s32[256,3]{1,0:T(8,128)S(1)} %get-tuple-element.184.ints) | copy-start | bytes 9220
  29.3 192.3 %copy-start.19 = (f32[128,128]{1,0:T(8,128)}, f32[128,128]{1,0:T(8,128)S(1)}, u32[]{:S(2)}) copy-start(f32[128,128]{1,0:T(8,128)S(1)} %get-tuple-element.185.mix) | copy-start | bytes 196612
  29.4 192.3 %copy-start.20 = (f32[128,128]{1,0:T(8,128)}, f32[128,128]{1,0:T(8,128)S(1)}, u32[]{:S(2)}) copy-start(f32[128,128]{1,0:T(8,128)S(1)} %get-tuple-element.186.mix) | copy-start | bytes 196612
  233.2 66.5 %copy-start.3 = (bf16[768,3200]{1,0:T(8,128)(2,1)}, bf16[768,3200]{1,0:T(8,128)(2,1)S(1)}, u32[]{:S(2)}) copy-start(bf16[768,3200]{1,0:T(8,128)(2,1)S(1)} %get-tuple-element.163.w) | copy-start | bytes 14745604
  391.8 11.5 %copy-start.2 = (bf16[768,3200]{1,0:T(8,128)(2,1)S(1)}, bf16[768,3200]{1,0:T(8,128)(2,1)}, u32[]{:S(2)}) copy-start(bf16[768,3200]{1,0:T(8,128)(2,1)} %dynamic_update_slice.7) | copy-start | bytes 14745604
  394.8 8.4 %collective-permute-start.5 = (bf16[768,3200]{1,0:T(8,128)(2,1)S(1)}, bf16[768,3200]{1,0:T(8,128)(2,1)}, u32[]{:S(2)}, u32[]{:S(2)}) collective-permute-start(bf16[768,3200]{1,0:T(8,128)(2,1)S(1)} %broadcast_select_fusion), channel_id=1, source_target_pairs={{0,16},{16,0},{1,17},{17,1},{2,18},{18,2},{3,19},{19,3},{4,20},{20... | collective-permute-start | bytes 14745608 | tf_op jit(solution)/shard_map/ppermute | solution.py:1038
  478.7 9.8 %copy-start.12 = (bf16[256,768]{1,0:T(8,128)(2,1)S(1)}, bf16[256,768]{1,0:T(8,128)(2,1)}, u32[]{:S(2)}) copy-start(bf16[256,768]{1,0:T(8,128)(2,1)} %get-tuple-element.50.x) | copy-start | bytes 1179652
  478.7 98.8 %all-to-all-start = ((bf16[4,192,1024]{2,1,0:T(8,128)(2,1)}), bf16[4,192,1024]{2,1,0:T(8,128)(2,1)S(1)}, u32[]{:S(2)}, u32[]{:S(2)}) async-start(bf16[4,192,1024]{2,1,0:T(8,128)(2,1)} %bitcast.58), calls=%async_computation.1 | async-start | bytes 3145728 | tf_op jit(solution)/shard_map/all_to_all | solution.py:1068
  482.6 8.9 %copy-start.5 = (f32[256,768]{1,0:T(8,128)S(1)}, f32[256,768]{1,0:T(8,128)}, u32[]{:S(2)}) copy-start(f32[256,768]{1,0:T(8,128)} %get-tuple-element.68.grad_y) | copy-start | bytes 2359300
  482.6 8.9 %copy-start.7 = (f32[256,768]{1,0:T(8,128)S(1)}, f32[256,768]{1,0:T(8,128)}, u32[]{:S(2)}) copy-start(f32[256,768]{1,0:T(8,128)} %get-tuple-element.78) | copy-start | bytes 2359300
  484.5 76.8 %collective-permute-start.8 = (bf16[256,768]{1,0:T(8,128)(2,1)}, bf16[256,768]{1,0:T(8,128)(2,1)}, u32[]{:S(2)}, u32[]{:S(2)}) collective-permute-start(bf16[256,768]{1,0:T(8,128)(2,1)} %dynamic-slice_bitcast_fusion.1), channel_id=1, source_target_pairs={{0,2},{1,3},{2,0},{3,1},{4,6},{5,7},{6,4},{7,5},{8,10},{9,11},{10,... | collective-permute-start | bytes 1179656 | tf_op jit(solution)/shard_map/ppermute | solution.py:1065
  488.4 4.5 collective-permute-start.4
  490.3 83.3 %collective-permute-start.2 = (bf16[256,768]{1,0:T(8,128)(2,1)}, bf16[256,768]{1,0:T(8,128)(2,1)}, u32[]{:S(2)}, u32[]{:S(2)}) collective-permute-start(bf16[256,768]{1,0:T(8,128)(2,1)} %broadcast_select_fusion.11), channel_id=1, source_target_pairs={{0,16},{16,0},{1,17},{17,1},{2,18},{18,2},{3,19},{19,3},{4,20},{20... | collective-permute-start | bytes 1179656 | tf_op jit(solution)/shard_map/ppermute | solution.py:1038
  491.4 79.8 %collective-permute-start.7 = (bf16[256,768]{1,0:T(8,128)(2,1)S(1)}, bf16[256,768]{1,0:T(8,128)(2,1)}, u32[]{:S(2)}, u32[]{:S(2)}) collective-permute-start(bf16[256,768]{1,0:T(8,128)(2,1)S(1)} %dynamic-slice_bitcast_fusion.2), channel_id=1, source_target_pairs={{0,2},{1,3},{2,0},{3,1},{4,6},{5,7},{6,4},{7,5},{8,10},{9,11},{10,... | collective-permute-start | bytes 1179656 | tf_op jit(solution)/shard_map/ppermute | solution.py:1065
  492.5 88.8 %collective-permute-start.3 = (f32[256,768]{1,0:T(8,128)}, f32[256,768]{1,0:T(8,128)}, u32[]{:S(2)}, u32[]{:S(2)}) collective-permute-start(f32[256,768]{1,0:T(8,128)} %broadcast_select_fusion.9), channel_id=1, source_target_pairs={{0,16},{16,0},{1,17},{17,1},{2,18},{18,2},{3,19},{19,3},{4,20},{20... | collective-permute-start | bytes 2359304 | tf_op jit(solution)/shard_map/ppermute | solution.py:1038
  493.0 80.6 %copy-start.13 = (bf16[256,768]{1,0:T(8,128)(2,1)S(1)}, bf16[256,768]{1,0:T(8,128)(2,1)}, u32[]{:S(2)}) copy-start(bf16[256,768]{1,0:T(8,128)(2,1)} %get-tuple-element.50.x) | copy-start | bytes 1179652
  493.0 80.6 %copy-start.14 = (bf16[256,768]{1,0:T(8,128)(2,1)S(1)}, bf16[256,768]{1,0:T(8,128)(2,1)}, u32[]{:S(2)}) copy-start(bf16[256,768]{1,0:T(8,128)(2,1)} %get-tuple-element.67) | copy-start | bytes 1179652
  573.6 5.0 collective-permute-start.9
  578.0 6.4 %collective-permute-start.6 = (bf16[2,192,1024]{2,1,0:T(8,128)(2,1)S(1)}, bf16[2,192,1024]{2,1,0:T(8,128)(2,1)S(1)}, u32[]{:S(2)}, u32[]{:S(2)}) collective-permute-start(bf16[2,192,1024]{2,1,0:T(8,128)(2,1)S(1)} %broadcast_select_fusion.3), channel_id=1, source_target_pairs={{0,16},{16,0},{1,17},{17,1},{2,18},{18,2},{3,19},{19,3},{4,20},{20... | collective-permute-start | bytes 2359304 | tf_op jit(solution)/shard_map/ppermute | solution.py:1038
  590.3 13.0 %copy-start.1 = (f32[2,1,256,768]{3,2,1,0:T(8,128)S(1)}, f32[2,1,256,768]{3,2,1,0:T(8,128)}, u32[]{:S(2)}) copy-start(f32[2,1,256,768]{3,2,1,0:T(8,128)} %param.16) | copy-start | bytes 4718596
  (18 other events, 60.6 us)
Sparse Core Ops, SparseCore 0:
  411.3 156.3 reduce-scatter.1

commit v5 on v4

--- a/solution.py
+++ b/solution.py
@@ -101,7 +101,7 @@
 
 
 def gating(after, r, small, mix, gain_second, ints, prio_row, dims, packed_ref, slot_ref, r_next, buffer):
-    nffn, nexp, capacity, slots = dims
+    nffn, nexp, capacity, slots, _ = dims
     rows = after.shape[0]
     second_b = (after * inverse_norm(after) * gain_second).astype(BF16)
     lane = lane_of(rows)
@@ -152,7 +152,7 @@
 
 
 def combine(after, packed, slot_pair, ints, blocks, gain_second, vec_rows, dims, picked_ref):
-    nffn, nexp, _, slots = dims
+    nffn, nexp, _, slots, _ = dims
     nconst = nexp - nffn - 2
     rows = after.shape[0]
     second = after * inverse_norm(after) * gain_second
@@ -186,7 +186,7 @@
 def moe_back(
     grad_y, grad_log_in, after, packed, slot_pair, ints, picked, blocks, r, small, mix, gain_second, vec_rows, dims
 ):
-    nffn, nexp, _, slots = dims
+    nffn, nexp, _, slots, _ = dims
     nconst = nexp - nffn - 2
     rows = grad_y.shape[0]
     lane = lane_of(rows)
@@ -224,7 +224,7 @@
         grad_probs = grad_probs + jnp.where(lane == ints[:, k : k + 1], grad_gate, 0.0)
     probs = jnp.where(lane < nexp, packed, 0.0)
     grad_logits = probs * (grad_probs - jnp.sum(probs * grad_probs, axis=-1, keepdims=True)) + grad_log_in
-    grad_mix = mm(r, grad_logits, TN, HIGH)
+    grad_mix = mm(jnp.where(lane < nexp, r, 0.0), jnp.where(lane < nexp, grad_logits, 0.0), TN, HIGH)
     grad_r = mm(grad_logits, mix, NT, HIGH)
     high, low = hi_lo(jnp.where(lane < nexp, grad_logits, grad_lanes))
     small_rows = mm(high, second_b, TN) + mm(low, second_b, TN)
@@ -239,7 +239,7 @@
     return grad_after, grad_r, grad_mix, small_rows
 
 
-def attention_back(grad_after, x, qkv, probs_att, attended, small_rows, w, gain_first, cosine, sine, grads, grad_qkv):
+def attention_back(grad_after, x, qkv, probs_att, attended, small_rows, mix_tile, w, gain_first, cosine, sine, grads, grad_qkv):
     seq_len, width = x.shape
     inverse = inverse_norm(x)
     unit = x * inverse
@@ -276,7 +276,7 @@
     grad_x = grad_after + norm_back(grad_first * gain_first, unit, inverse)
     row = lax.broadcasted_iota(jnp.int32, small_rows.shape, 0)
     small_rows = jnp.where(row == AT_GAIN, grad_gain, small_rows)
-    grads[:, 4 * width :] = small_rows.T.astype(BF16)
+    grads[:, 4 * width :] = (small_rows.T + mix_tile).astype(BF16)
     return grad_x
 
 
@@ -340,9 +340,13 @@
     )
     grad_r[...] = grad_r_v
     grad_mix[...] = grad_mix_v
+    rows = dims[4]
+    mix_tile = 0.0
+    if rows:
+        mix_tile = jnp.concatenate([roll(grad_mix_v, AT_MIX)[:rows]] * (x.shape[1] // rows), axis=0)
     grad_x[...] = attention_back(
-        grad_after, x[...].astype(F32), qkv, probs_att, attended, small_rows, w, gain_first, cosine[...], sine[...],
-        grads, grad_qkv,
+        grad_after, x[...].astype(F32), qkv, probs_att, attended, small_rows, mix_tile, w, gain_first,
+        cosine[...], sine[...], grads, grad_qkv,
     )
 
 
@@ -912,14 +916,14 @@
         if inside:
             spread.begin()
             spread.pass_on()
+        spread.begin_experts()
+        if inside:
             spread.pass_over()
-        spread.begin_experts()
 
     @pl.when(second)
     def _():
         if inside:
             spread.over_ready()
-            spread.begin()
 
     small[0] = attn[0, :, 4 * width :]
     attend_kernel(
@@ -931,22 +935,18 @@
     @pl.when(second)
     def _():
         if inside:
-            spread.pass_on()
+            spread.begin()
 
     tokens.spread()
+
+    @pl.when(first)
+    def _():
+        spread.experts_ready(0)
 
     @pl.when(second)
     def _():
         if inside:
-            spread.pass_over()
-        spread.begin_experts()
-
-    @pl.when(first)
-    def _():
-        spread.experts_ready(0)
-
-    @pl.when(second)
-    def _():
+            spread.pass_on()
         spread.experts_ready(1)
 
     tokens.near_ready()
@@ -957,6 +957,13 @@
     set_half(tokens.partial, 1, experts_forward_half(half_rows(tokens.groups, 1), w_in.at[0], w_out.at[0]))
     tokens.to_sibling(1).start()
     tokens.return_far()
+
+    @pl.when(second)
+    def _():
+        if inside:
+            spread.pass_over()
+        spread.begin_experts()
+
     arrived[...] = tokens.groups[...]
     tokens.return_home()
     tokens.finish_dispatch()
@@ -1003,6 +1010,391 @@
             vmem_limit_bytes=VMEM_BYTES, collective_id=0, has_side_effects=True
         ),
         cost_estimate=pl.CostEstimate(flops=8 << 30, bytes_accessed=40 << 20, transcendentals=0),
+    )(*args)
+
+
+def place_of():
+    return lax.axis_index("section"), lax.axis_index("expert"), lax.axis_index("shard")
+
+
+def remote(source, target, send, recv, device):
+    return pltpu.make_async_remote_copy(source, target, send, recv, device_id=device, device_id_type=MESH)
+
+
+class ExpertSum:
+    def __init__(self, grad_in, grad_out, got_in, got_out, sems):
+        self.grad_in, self.grad_out, self.got_in, self.got_out = grad_in, grad_out, got_in, got_out
+        self.in_s, self.in_r, self.out_s, self.out_r = sems
+        self.core, self.column, self.place = place_of()
+        self.pieces = lax.axis_size("shard")
+
+    def place_by(self, by):
+        return lax.rem(self.place + by + self.pieces, self.pieces)
+
+    def in_rows(self, place):
+        rows = self.got_in.shape[1]
+        return pl.ds(pl.multiple_of(place * rows, rows), rows)
+
+    def out_rows(self, place):
+        rows = self.got_out.shape[1]
+        return pl.ds(pl.multiple_of(lax.div(place, 2) * rows, rows), rows)
+
+    def in_copy(self, by, way=1):
+        place = self.place_by(way * by)
+        return remote(
+            self.grad_in.at[self.in_rows(place)], self.got_in.at[by - 1], self.in_s.at[by - 1], self.in_r.at[by - 1],
+            (self.core, self.column, place),
+        )
+
+    def out_copy(self, by, way=1):
+        place = self.place_by(way * by)
+        at = by // 2 - 1
+        return remote(
+            self.grad_out.at[self.out_rows(place)], self.got_out.at[at], self.out_s.at[at], self.out_r.at[at],
+            (self.core, self.column, place),
+        )
+
+    def start(self):
+        for by in range(1, self.pieces):
+            self.in_copy(by).start()
+            if by % 2 == 0:
+                self.out_copy(by).start()
+
+    def wait(self):
+        for by in range(1, self.pieces):
+            self.in_copy(by, -1).wait_recv()
+            self.in_copy(by).wait_send()
+            if by % 2 == 0:
+                self.out_copy(by, -1).wait_recv()
+                self.out_copy(by).wait_send()
+
+
+def expert_sum_sems(pieces):
+    dma = pltpu.SemaphoreType.DMA
+    return [dma((pieces - 1,)), dma((pieces - 1,)), dma((max(pieces // 2 - 1, 1),)), dma((max(pieces // 2 - 1, 1),))]
+
+
+class AttnSum:
+    def __init__(self, grads, own, from_core, summed, from_plane, through, from_z, sems):
+        self.grads, self.own, self.from_core, self.summed = grads, own, from_core, summed
+        self.from_plane, self.through, self.from_z = from_plane, through, from_z
+        self.own_sem, self.core_s, self.core_r, self.plane_s, self.plane_r, self.z_s, self.z_r = sems
+        self.core, self.column, self.place = place_of()
+        self.owners, self.pieces = lax.axis_size("expert"), lax.axis_size("shard")
+
+    def block(self, column, k, core):
+        rows = self.own.shape[2]
+        return self.grads.at[pl.ds(pl.multiple_of((column * self.pieces + 2 * k + core) * rows, rows), rows)]
+
+    def each(self):
+        return [(column, k) for column in range(self.owners) for k in range(self.pieces // 2)]
+
+    def load(self, column, k):
+        return pltpu.make_async_copy(self.block(column, k, self.core), self.own.at[column, k], self.own_sem.at[column, k])
+
+    def to_core(self, column, k):
+        return remote(
+            self.block(column, k, 1 - self.core), self.from_core.at[column, k], self.core_s.at[column, k],
+            self.core_r.at[column, k], (1 - self.core, self.column, self.place),
+        )
+
+    def to_plane(self, by, way=1):
+        column = lax.rem(self.column + way * by + self.owners, self.owners)
+        return remote(
+            self.summed.at[column], self.from_plane.at[by - 1], self.plane_s.at[by - 1], self.plane_r.at[by - 1],
+            (self.core, column, self.place),
+        )
+
+    def place_by(self, by):
+        return lax.rem(self.place + by + self.pieces, self.pieces)
+
+    def along(self, by, way=1):
+        place = self.place_by(way * by)
+        return remote(
+            self.through.at[lax.div(place, 2)], self.from_z.at[by - 1], self.z_s.at[by - 1], self.z_r.at[by - 1],
+            (self.core, self.column, place),
+        )
+
+    def holds(self, place):
+        return lax.rem(place, 2) == self.core
+
+    def start(self):
+        for column, k in self.each():
+            self.to_core(column, k).start()
+        for column, k in self.each():
+            self.load(column, k).start()
+
+    def add_cores(self):
+        for column, k in self.each():
+            self.load(column, k).wait()
+            self.to_core(column, k).wait_recv()
+        for column in range(self.owners):
+            for k in range(self.pieces // 2):
+                self.summed[column, k] = (
+                    self.own[column, k].astype(F32) + self.from_core[column, k].astype(F32)
+                ).astype(BF16)
+        for by in range(1, self.owners):
+            self.to_plane(by).start()
+
+    def add_plane(self):
+        total = self.summed[self.column].astype(F32)
+        for by in range(1, self.owners):
+            self.to_plane(by, -1).wait_recv()
+            total = total + self.from_plane[by - 1].astype(F32)
+        self.through[...] = total.astype(BF16)
+        for by in range(1, self.pieces):
+
+            @pl.when(self.holds(self.place_by(by)))
+            def _():
+                self.along(by).start()
+
+    def add_z(self, target):
+        @pl.when(self.holds(self.place))
+        def _():
+            total = self.through[lax.div(self.place, 2)].astype(F32)
+            for by in range(1, self.pieces):
+                self.along(by, -1).wait_recv()
+                total = total + self.from_z[by - 1].astype(F32)
+            target[...] = total
+
+    def finish(self):
+        for column, k in self.each():
+            self.to_core(column, k).wait_send()
+        for by in range(1, self.owners):
+            self.to_plane(by).wait_send()
+        for by in range(1, self.pieces):
+
+            @pl.when(self.holds(self.place_by(by)))
+            def _():
+                self.along(by).wait_send()
+
+
+def attn_sum_scratch(owners, pieces, rows, columns):
+    blocks = (owners, pieces // 2, rows, columns)
+    dma = pltpu.SemaphoreType.DMA
+    return [
+        pltpu.VMEM(blocks, BF16), pltpu.VMEM(blocks, BF16), pltpu.VMEM(blocks, BF16),
+        pltpu.VMEM((owners - 1,) + blocks[1:], BF16), pltpu.VMEM(blocks[1:], BF16),
+        pltpu.VMEM((pieces - 1,) + blocks[2:], BF16),
+    ], [
+        dma(blocks[:2]), dma(blocks[:2]), dma(blocks[:2]), dma((owners - 1,)), dma((owners - 1,)),
+        dma((pieces - 1,)), dma((pieces - 1,)),
+    ]
+
+
+def greet_last(inside):
+    core, column, place = place_of()
+    owners, pieces = lax.axis_size("expert"), lax.axis_size("shard")
+    barrier = pltpu.get_barrier_semaphore()
+    others = [(1 - core, column, place)]
+    others += [(core, column, lax.rem(place + by, pieces)) for by in range(1, pieces)]
+    if inside:
+        others += [(core, lax.rem(column + by, owners), place) for by in range(1, owners)]
+    for device in others:
+        pl.semaphore_signal(barrier, inc=1, device_id=device, device_id_type=MESH)
+    pl.semaphore_wait(barrier, len(others))
+
+
+def spread_columns(target, halves_at, hidden_here):
+    rows, columns = target.shape
+    hidden = columns // 2
+    pieces = hidden // (2 * hidden_here)
+    parity = lax.rem(lax.axis_index("shard"), 2)
+    for first_parity in range(2):
+
+        @pl.when(parity == first_parity)
+        def _():
+            for half in range(2):
+                for q in range(2):
+                    odd = first_parity if q == 0 else 1 - first_parity
+                    for pair in range(pieces // 2):
+                        for side in range(2):
+                            for ahead in range(0, hidden_here, CHUNK):
+                                at = side * hidden + (2 * pair + odd) * 2 * hidden_here + half * hidden_here + ahead
+                                source = 2 * (pair * hidden_here + ahead) + side * CHUNK
+                                target[:, at : at + CHUNK] = halves_at(half, q)[:, source : source + CHUNK].astype(F32)
+
+
+def last_kernel(
+    inside, wide, out_0, out_1, grad_x_0, grad_x_1, grad_r_0, grad_r_1, in_0, gout_0, in_1, gout_1, attn_0, attn_1, *rest
+):
+    (both_out, both_x, both_r, in_total, out_total, attn_total, got_in_0, got_out_0, got_in_1, got_out_1, *scratch) = rest
+    (in_mine, out_mine, in_sent, out_sent, in_got, out_got, own_in, own_out, attn_sum_0, attn_sum_1,
+     swap_s, swap_r, local_sem, final_s, final_r, own_sems, *scratch) = scratch
+    core, column, place = place_of()
+    pieces = lax.axis_size("shard")
+    sibling = (1 - core, column, place)
+    experts = [
+        ExpertSum(in_0, gout_0, got_in_0, got_out_0, scratch[:4]),
+        ExpertSum(in_1, gout_1, got_in_1, got_out_1, scratch[4:8]),
+    ]
+    scratch = scratch[8:]
+    attn = []
+    if inside:
+        attn = [AttnSum(attn_0, *scratch[:6], scratch[6:13]), AttnSum(attn_1, *scratch[13:19], scratch[19:26])]
+    greet_last(inside)
+    pairs = ((out_0, out_1, both_out), (grad_x_0, grad_x_1, both_x), (grad_r_0, grad_r_1, both_r))
+
+    def swaps(section):
+        for i, (zero, one, both) in enumerate(pairs):
+            own, other = (zero, one) if section == 0 else (one, zero)
+            yield (
+                remote(other, both.at[section], swap_s.at[i], swap_r.at[i], sibling),
+                pltpu.make_async_copy(own, both.at[section], local_sem.at[i]),
+            )
+
+    def each_core(action):
+        for section in range(2):
+
+            @pl.when(core == section)
+            def _():
+                action(section)
+
+    for one in reversed(attn):
+        one.start()
+    experts[1].start()
+
+    @each_core
+    def _(section):
+        for away, here in swaps(section):
+            away.start()
+            here.start()
+
+    for one in reversed(attn):
+        one.add_cores()
+    experts[0].start()
+    loads = []
+    for s in (1, 0):
+        e = experts[s]
+        loads.append((
+            pltpu.make_async_copy(e.grad_in.at[e.in_rows(place)], own_in.at[s, 0], own_sems.at[s, 0]),
+            pltpu.make_async_copy(e.grad_out.at[e.out_rows(place)], own_out.at[s, 0], own_sems.at[s, 1]),
+        ))
+        for one in loads[-1]:
+            one.start()
+    for one in reversed(attn):
+        one.add_plane()
+    for n, s in enumerate((1, 0)):
+        e = experts[s]
+        e.wait()
+        for one in loads[n]:
+            one.wait()
+        copies = [pltpu.make_async_copy(e.got_in, own_in.at[s, pl.ds(1, pieces - 1)], own_sems.at[s, 2])]
+        if pieces > 2:
+            copies.append(pltpu.make_async_copy(e.got_out, own_out.at[s, pl.ds(1, pieces // 2 - 1)], own_sems.at[s, 3]))
+        for one in copies:
+            one.start()
+        for one in copies:
+            one.wait()
+        in_sum = [sum(own_in[s, by].astype(F32) for by in range(q, pieces, 2)) for q in range(2)]
+        out_sum = sum(own_out[s, i].astype(F32) for i in range(pieces // 2))
+
+        @pl.when(core == s)
+        def _():
+            for q in range(2):
+                in_mine[q] = in_sum[q]
+            out_mine[...] = out_sum
+
+        @pl.when(core != s)
+        def _():
+            for q in range(2):
+                in_sent[q] = in_sum[q].astype(BF16)
+            out_sent[...] = out_sum.astype(BF16)
+
+    finals = [
+        remote(in_sent, in_got, final_s.at[0], final_r.at[0], sibling),
+        remote(out_sent, out_got, final_s.at[1], final_r.at[1], sibling),
+    ]
+    for one in finals:
+        one.start()
+    if inside:
+        attn[1].add_z(attn_sum_1)
+        attn[0].add_z(attn_sum_0)
+        holder = attn[0].holds(place)
+        for section in range(2):
+            mine, other = (attn_sum_0, attn_sum_1) if section == 0 else (attn_sum_1, attn_sum_0)
+            home = remote(other, attn_total, final_s.at[2], final_r.at[2], sibling)
+
+            @pl.when(holder & (core == section))
+            def _():
+                home.start()
+                attn_total[...] = mine[...]
+                home.wait_send()
+
+            @pl.when(jnp.logical_not(holder) & (core == section))
+            def _():
+                home.wait_recv()
+
+    for one in finals:
+        one.wait()
+    for half in range(2):
+
+        @pl.when(core == half)
+        def _():
+            if wide:
+                hidden_here = out_mine.shape[0]
+                spread_columns(
+                    in_total, lambda at, q: in_mine[q] if at == half else in_got[q], hidden_here
+                )
+            else:
+                for q in range(2):
+                    in_total[half, q] = in_mine[q]
+                    in_total[1 - half, q] = in_got[q].astype(F32)
+            count = out_mine.shape[0]
+            out_total[half * count : (half + 1) * count] = out_mine[...]
+            out_total[(1 - half) * count : (2 - half) * count] = out_got[...].astype(F32)
+
+    @each_core
+    def _(section):
+        for away, here in swaps(section):
+            away.wait()
+            here.wait()
+
+    for one in attn:
+        one.finish()
+
+
+def run_last(inside, wide, args, owners, pieces, hidden_here, rows):
+    vmem, anywhere = pl.BlockSpec(memory_space=pltpu.VMEM), pl.BlockSpec(memory_space=pl.ANY)
+    seq_len, width = args[0].shape
+    columns = args[6].shape[1]
+    in_rows = width // pieces
+    attn_columns = args[10].shape[1]
+    in_shape = (in_rows, 4 * columns) if wide else (2, 2, in_rows, columns)
+    got = [
+        shaped((pieces - 1, in_rows, columns), BF16), shaped((max(pieces // 2 - 1, 1), hidden_here, width), BF16)
+    ] * 2
+    attn_shape = (rows, attn_columns) if inside else (8, LANES)
+    out = [
+        shaped((2,) + args[0].shape, BF16), shaped((2,) + args[2].shape, F32), shaped((2,) + args[4].shape, F32),
+        shaped(in_shape, F32), shaped((2 * hidden_here, width), F32), shaped(attn_shape, F32),
+    ] + got
+    dma = pltpu.SemaphoreType.DMA
+    scratch = [
+        pltpu.VMEM((2, in_rows, columns), F32), pltpu.VMEM((hidden_here, width), F32),
+        pltpu.VMEM((2, in_rows, columns), BF16), pltpu.VMEM((hidden_here, width), BF16),
+        pltpu.VMEM((2, in_rows, columns), BF16), pltpu.VMEM((hidden_here, width), BF16),
+        pltpu.VMEM((2, pieces, in_rows, columns), BF16), pltpu.VMEM((2, pieces // 2, hidden_here, width), BF16),
+        pltpu.VMEM(attn_shape, F32), pltpu.VMEM(attn_shape, F32),
+        dma((3,)), dma((3,)), dma((3,)), dma((3,)), dma((3,)), dma((2, 4)),
+    ]
+    for _ in range(2):
+        scratch += expert_sum_sems(pieces)
+    if inside:
+        for _ in range(2):
+            buffers, sems = attn_sum_scratch(owners, pieces, rows, attn_columns)
+            scratch += buffers + sems
+    specs = [anywhere] * 3 + [vmem] * 3 + [anywhere] * 4
+    return pl.pallas_call(
+        functools.partial(last_kernel, inside, wide),
+        out_shape=out,
+        in_specs=[anywhere] * len(args),
+        out_specs=specs,
+        scratch_shapes=scratch,
+        compiler_params=pltpu.CompilerParams(
+            vmem_limit_bytes=VMEM_BYTES, collective_id=3, has_side_effects=True
+        ),
+        cost_estimate=pl.CostEstimate(flops=1 << 28, bytes_accessed=40 << 20, transcendentals=0),
     )(*args)
 
 
@@ -1061,24 +1453,6 @@
     w_out = expert_out[0, 0].reshape(2, hidden_here, width)
     in_pieces = jnp.stack([as_chunks(w_in[:, :, :, :, half]) for half in range(2)])
 
-    def across(piece, hops):
-        return lax.ppermute(piece, "shard", [(i, (i + 2 * hops) % pieces) for i in range(pieces)])
-
-    def split_grads(grad_in, grad_out):
-        got = lax.all_to_all(
-            grad_in.reshape(pieces, in_rows, 2 * quarter), "shard", split_axis=0, concat_axis=0, tiled=True
-        )
-        in_sum = jnp.sum(got.reshape(pairs, 2, in_rows, 2 * quarter).astype(F32), axis=0).astype(BF16)
-        grad_out = grad_out.reshape(pairs, hidden_here, width)
-
-        def piece(hops):
-            return lax.dynamic_index_in_dim(grad_out, (pair_index + hops) % pairs, 0, False)
-
-        out_sum = piece(0).astype(F32)
-        for hops in range(1, pairs):
-            out_sum = out_sum + across(piece(hops), hops).astype(F32)
-        return in_sum, out_sum.astype(BF16)
-
     rows = attn_qkv.shape[1]
 
     def lanes(array, upto):
@@ -1116,7 +1490,7 @@
     cosine = jnp.concatenate([cosine] * 4, axis=1)
     sine = jnp.concatenate([-sine, sine, -sine, sine], axis=1)
 
-    dims = (nffn, nexp, capacity, slots)
+    dims = (nffn, nexp, capacity, slots, rows if inside else 0)
     heads = width // HEAD
     blocks = (owners, room, width)
     seg_col, seg_row = seg[:, None], seg[None, :]
@@ -1166,7 +1540,6 @@
         experts_both_kernel, 1, 2, blocks, (buffer.reshape(blocks), grad_buffer.reshape(blocks), *experts[1]),
         [block_shape, block_shape] + grad_shapes, kept, flops=9 * work,
     )
-    sums_1 = split_grads(grad_in_1, grad_out_1)
     out_1, grad_x_1, grad_r_1, grad_mix_1, grads_1, buffer = run(
         functools.partial(turn_kernel, dims),
         [token_b16] + back_out + [slot_shape],
@@ -1181,7 +1554,6 @@
         experts_back_kernel, 2, 1, blocks, (buffer.reshape(blocks), arrived, *experts[0]),
         [block_shape] + grad_shapes, kept, flops=9 * work,
     )
-    sums_0 = split_grads(grad_in_0, grad_out_0)
     grad_x_0, grad_r_0, grad_mix_0, grads_0 = run(
         functools.partial(back_kernel, dims),
         back_out,
@@ -1192,44 +1564,34 @@
         flops=5 << 30,
         scratch=[grad_qkv],
     )
-    results, x_grads = (out_0, out_1), (grad_x_0, grad_x_1)
-    r_grads = (grad_r_0[:, :nexp], grad_r_1[:, :nexp])
-    sums = []
-    for grads, grad_mix, expert_sums in ((grads_0, grad_mix_0, sums_0), (grads_1, grad_mix_1, sums_1)):
-        mix_lanes = -(-nexp * nexp // rows)
-        mix_flat = jnp.pad(grad_mix[:nexp, :nexp].reshape(-1), (0, rows * mix_lanes - nexp * nexp)).reshape(rows, mix_lanes)
-        mix_tile = jnp.tile(mix_flat, (owners * pieces, 1)).astype(BF16)
-        at = 4 * width + AT_MIX
-        grads = lax.dynamic_update_slice(grads, mix_tile, (0, at))
-        sums.append((grads, *expert_sums))
-    shared_own = jnp.where(first_core, sums[0][0], sums[1][0])
-    shared_other = jnp.where(first_core, sums[1][0], sums[0][0])
-    shared_sum = (shared_own.astype(F32) + swap(shared_other).astype(F32)).astype(BF16)
-    shared_sum = lax.psum_scatter(shared_sum, ("expert", "shard"), scatter_dimension=0, tiled=True).astype(F32)
-
-    def halves(index):
-        own = jnp.where(first_core, sums[0][index], sums[1][index])
-        got = swap(jnp.where(first_core, sums[1][index], sums[0][index]))
-        return jnp.where(first_core, own, got).astype(F32), jnp.where(first_core, got, own).astype(F32)
-
-    def from_chunks(half):
-        half = jnp.swapaxes(half.reshape(2, in_rows, chunks, 2, CHUNK), 2, 3)
-        return jnp.moveaxis(half.reshape(2, in_rows, 2, pairs, hidden_here), 0, 3)
-
-    in_grad = jnp.stack([from_chunks(half) for half in halves(1)], axis=4).reshape(in_rows, columns)
-    out_grad = jnp.concatenate(halves(2), axis=0)
-
-    def both_batches(pair):
-        own = jnp.where(first_core, pair[0], pair[1])
-        got = swap(jnp.where(first_core, pair[1], pair[0]))
-        return jnp.stack(by_section(own, got))[None, :, None]
-
+    wide = hidden_here % CHUNK == 0
+    both_out, both_x, both_r, in_grad, out_grad, shared_sum, *_ = run_last(
+        inside, wide,
+        (out_0, out_1, grad_x_0, grad_x_1, grad_r_0, grad_r_1, grad_in_0, grad_out_0, grad_in_1, grad_out_1, grads_0, grads_1),
+        owners, pieces, hidden_here, rows,
+    )
+    if not wide:
+        odd = lax.axis_index("shard") % 2
+        in_grad = jnp.where(odd == 0, in_grad, in_grad[:, ::-1])
+        in_grad = jnp.swapaxes(in_grad.reshape(2, 2, in_rows, chunks, 2, CHUNK), 3, 4)
+        in_grad = in_grad.reshape(2, 2, in_rows, 2, pairs, hidden_here)
+        in_grad = jnp.transpose(in_grad, (2, 3, 4, 1, 0, 5)).reshape(in_rows, columns)
+    if inside:
+        mix_grad = shared_sum[:nexp, 4 * width + AT_MIX : 4 * width + AT_MIX + nexp]
+    else:
+        own = jnp.where(first_core, grads_0, grads_1)
+        shared_sum = own.astype(F32) + swap(jnp.where(first_core, grads_1, grads_0)).astype(F32)
+        shared_sum = lax.psum_scatter(
+            shared_sum.astype(BF16), ("expert", "shard"), scatter_dimension=0, tiled=True
+        ).astype(F32)
+        own = jnp.where(first_core, grad_mix_0, grad_mix_1)
+        mix_grad = own + swap(jnp.where(first_core, grad_mix_1, grad_mix_0))
+        mix_grad = lax.psum(mix_grad, ("expert", "shard"))[:nexp, :nexp]
     small_sum = shared_sum[:, 4 * width :]
-    mix_grad = small_sum[:, AT_MIX : AT_MIX + mix_lanes].reshape(-1)[: nexp * nexp].reshape(nexp, nexp)
     return (
-        both_batches(results),
-        both_batches(x_grads),
-        both_batches(r_grads),
+        both_out[None, :, None],
+        both_x[None, :, None],
+        both_r[None, :, None, :, :nexp],
         shared_sum[None, :, : 3 * width],
         shared_sum[None, :, 3 * width : 4 * width],
         small_sum[None, :, :nexp],

time: 617 us -> 504 us (0.82)
  Pallas kernels: 339 us -> 443 us
  waiting for transfers between devices: 85.7 us -> 0.01 us
  blocking collectives: 66.1 us -> 0 us
  other arithmetic: 34.3 us -> 5.92 us
  between operations: 14.9 us -> 1.43 us
  local copies, waits for them, and re-layouts: 61.4 us -> 48 us
  starting transfers between devices: 8.72 us -> 0.61 us
    pallas_call x0 -> x1, Pallas kernels: none -> 137 us  [run_last(): pl.pallas_call(functools.partial(last_kernel, inside, wide), out_shape=ou...]
    ppermute x2 -> x0, waiting for transfers between devices: 77.4 us -> none  [across(): lax.ppermute(piece, 'shard', [(i, (i + 2 * hops) % pieces) for i in range...]
    all_to_all x1 -> x0, blocking collectives: 66.1 us -> none  [split_grads(): lax.all_to_all(grad_in.reshape(pieces, in_rows, 2 * quarter), 'shard', sp...]
    pallas_call x1, Pallas kernels: 192 us -> 158 us  [run_front(): pl.pallas_call(functools.partial(front_kernel, dims, inside), out_shape=o...]
    another operation x9 -> x0, local copies, waits for them, and re-layouts: 10.8 us -> none  [the longest x2 9.72 us: local(): in_grad[None, None]]
    select_n x8 -> x0, other arithmetic: 10.5 us -> none  [the longest x3 3.76 us: both_batches(): got = swap(jnp.where(first_core, pair[1], pair[0]))]
    convert_element_type x2 -> x0, other arithmetic: 8.92 us -> none  [the longest x1 7.91 us: local(): (shared_own.astype(F32) + swap(shared_other).astype(F32)).astype(BF16)]
    ppermute x8 -> x2, waiting for transfers between devices: 8.33 us -> 0.01 us  [swap(): return lax.ppermute(item, 'section', [(0, 1), (1, 0)])]
  transfers between devices with their start and end apart: 12 -> 2, of which waited for: 3 -> 0; matrix products, arithmetic and copies ran while one was open for 8% -> 4% of each run, Pallas kernels for 0% -> 0%
where the time goes in v5:
time: 504 us; the launch traced here: 499 us
  Pallas kernels  443 us (88%)
  local copies, waits for them, and re-layouts  48 us (10%)
  other arithmetic  5.92 us (1%)
    pallas_call x1, Pallas kernels, run_front(): pl.pallas_call(functools.partial(front_kernel, dims, inside), out_shape=o...  158 us
    pallas_call x1, Pallas kernels, run_last(): pl.pallas_call(functools.partial(last_kernel, inside, wide), out_shape=ou...  137 us
    pallas_call x2, Pallas kernels, run_experts(): pl.pallas_call(kernel, out_shape=out, in_specs=[pl.BlockSpec(memory_space...  110 us
    pallas_call x2, Pallas kernels, run(): pl.pallas_call(kernel, out_shape=out, in_specs=[pl.BlockSpec(memory_space...  38.6 us
  transfers between devices with their start and end apart: 2, of which 0 were waited for; matrix products, arithmetic and copies ran while one was open for 4% of the time, Pallas kernels for 0%

profile of v5, /device:TPU:0, one launch (start us, length us, event | category | flops | bytes accessed | tf_op | source)
XLA Modules:
  0.0 498.7 jit_solution(4553186402763498262)
XLA Ops:
  5.8 1.8 dynamic-slice_bitcast_fusion.1.x
  7.5 0.9 dynamic-slice_bitcast_fusion.grad_y
  8.5 1.2 reshape_squeeze.6
  9.7 2.2 fusion.5
  11.9 1.6 copy_bitcast_fusion
  15.3 1.3 pad_maximum_fusion.in_pieces
  16.6 1.0 pad_maximum_fusion.2
  23.5 157.8 %shard_map.238 = (bf16[2,768,3200]{2,1,0:T(8,128)(2,1)}, bf16[2,768,1024]{2,1,0:T(8,128)(2,1)}, bf16[2,512,768]{2,1,0:T(8,128)(2,1)}, bf16[4,4,80,768]{3,2,1,0:T...) custom-call(bf16[48,3200]{1,0:T(8,128)(2,1)} %concatenate.12.packed,, ...), custom_call_target="tpu_custom_call" | custom-call | flops 8589934592 | bytes 41943040 | tf_op jit(solution)/shard_map/pallas_call | solution.py:1001
  181.3 2.8 slice_bitcast_fusion.4
  184.1 2.0 slice_bitcast_fusion.2
  186.0 6.8 %slice_bitcast_fusion = (bf16[768,3200]{1,0:T(8,128)(2,1)S(1)}, bf16[768,3200]{1,0:T(8,128)(2,1)}) fusion(bf16[2,768,3200]{2,1,0:T(8,128)(2,1)} %get-tuple-element.65), kind=kLoop, calls=%fused_computation | loop fusion | bytes 19660800 | tf_op jit(solution)/shard_map/squeeze | solution.py:1535
  193.6 1.9 slice.85.small
  195.5 63.0 %shard_map.239 = (bf16[4,80,768]{2,1,0:T(8,128)(2,1)}, bf16[4,80,768]{2,1,0:T(8,128)(2,1)}, bf16[768,1024]{1,0:T(8,128)(2,1)}, bf16[512,768]{1,0:T(8,128)(2,1)}) custom-call(bf16[4,80,768]{2,1,0:T(8,128)(2,1)} %bitcast.104, bf16[4,80,768]{2,1,0:T(8,128)(2,1)} %bitcast.105, bf16[768,1024]{1,0:T(8,128)(2,1)} %get-tuple-element.159.w_in, ...), custom_call_target="tpu_custom_call" | custom-call | flops 9059696640 | bytes 16777216 | tf_op jit(solution)/shard_map/pallas_call | solution.py:691
  258.6 19.9 %shard_map.240 = (bf16[256,768]{1,0:T(8,128)(2,1)}, f32[256,768]{1,0:T(8,128)}, f32[256,128]{1,0:T(8,128)}, f32[128,128]{1,0:T(8,128)}, bf16[768,3200]{1,0:T(8,128)(2,1)}, /*index=5*/bf16[320,768]{1,0:T(8,128)(2,1)}) custom-call(f32[256,768]{1,0:T(8,128)} %dynamic-slice_bitcast_fusion.grad_y, f32[256,768]{1,0:T(8,128)} %get-tuple-element.55.after, ...), custom_call_target="tpu_custom_call" | custom-call | flops 5368709120 | bytes 8388608 | tf_op jit(solution)/shard_map/pallas_call | solution.py:358
  278.5 46.7 %shard_map.241 = (bf16[4,80,768]{2,1,0:T(8,128)(2,1)}, bf16[768,1024]{1,0:T(8,128)(2,1)}, bf16[512,768]{1,0:T(8,128)(2,1)}) custom-call(bf16[4,80,768]{2,1,0:T(8,128)(2,1)} %bitcast.106, bf16[4,4,80,768]{3,2,1,0:T(8,128)(2,1)} %get-tuple-element.77.arrived, bf16[768,1024]{1,0:T(8,128)(2,1)} %get-tuple-element.158.w_in, bf16[512,768]{1,0:T(8,128)(2,1)} %get-tuple-element.160.w_out), custom_call_target="tpu_custom_call" | custom-call | flops 9059696640 | bytes 16777216 | tf_op jit(solution)/shard_map/pallas_call | solution.py:691
  325.2 18.7 %shard_map.242 = (f32[256,768]{1,0:T(8,128)}, f32[256,128]{1,0:T(8,128)}, f32[128,128]{1,0:T(8,128)}, bf16[768,3200]{1,0:T(8,128)(2,1)}) custom-call(f32[256,768]{1,0:T(8,128)} %get-tuple-element.72.grad_y.grad_x_1, f32[256,128]{1,0:T(8,128)} %get-tuple-element.73.grad_log.grad_r_1, f32[256,768]{1,0:T(8,128)} %get-tuple-element.74.after, ...), custom_call_target="tpu_custom_call" | custom-call | flops 5368709120 | bytes 8388608 | tf_op jit(solution)/shard_map/pallas_call | solution.py:358
  343.9 136.6 %shard_map.243 = (bf16[2,256,768]{2,1,0:T(8,128)(2,1)}, f32[2,256,768]{2,1,0:T(8,128)}, f32[2,256,128]{2,1,0:T(8,128)}, f32[192,4096]{1,0:T(8,128)}, f32[512,768...) custom-call(bf16[256,768]{1,0:T(8,128)(2,1)} %get-tuple-element.54.x, ...), custom_call_target="tpu_custom_call" | custom-call | flops 268435456 | bytes 41943040 | tf_op jit(solution)/shard_map/pallas_call | solution.py:1388
  480.6 1.4 slice_bitcast_fusion.11
  484.4 1.6 slice_bitcast_fusion.8
  486.0 1.9 slice_bitcast_fusion.6
  492.2 1.1 copy.129
  493.3 1.3 copy-done.3
  494.6 1.7 copy.130
  497.2 1.1 copy.131
  (92 shorter events, 20.9 us)
Async XLA Ops:
  0.6 6.9 %copy-start = (f32[2,1,256,768]{3,2,1,0:T(8,128)S(1)}, f32[2,1,256,768]{3,2,1,0:T(8,128)}, u32[]{:S(2)}) copy-start(f32[2,1,256,768]{3,2,1,0:T(8,128)} %param.16) | copy-start | bytes 4718596
  0.7 7.8 %copy-start.5 = (bf16[1,1,192,4096]{3,2,1,0:T(8,128)(2,1)S(1)}, bf16[1,1,192,4096]{3,2,1,0:T(8,128)(2,1)}, u32[]{:S(2)}) copy-start(bf16[1,1,192,4096]{3,2,1,0:T(8,128)(2,1)} %param.28) | copy-start | bytes 4718596
  1.5 21.2 %collective-permute-start = (f32[128,128]{1,0:T(8,128)S(1)}, f32[128,128]{1,0:T(8,128)S(1)}, u32[]{:S(2)}, u32[]{:S(2)}) collective-permute-start(f32[128,128]{1,0:T(8,128)S(1)} %pad.29), channel_id=1, source_target_pairs={{0,16},{16,0},{1,17},{17,1},{2,18},{18,2},{3,19},{19,3},{4,20},{20... | collective-permute-start | bytes 196616 | tf_op jit(solution)/shard_map/ppermute | solution.py:1430
  2.8 18.3 %collective-permute-start.1 = (s32[256,3]{1,0:T(8,128)S(1)}, s32[256,3]{1,0:T(8,128)S(1)}, u32[]{:S(2)}, u32[]{:S(2)}) collective-permute-start(s32[256,3]{1,0:T(8,128)S(1)} %bitcast.90), channel_id=1, source_target_pairs={{0,16},{16,0},{1,17},{17,1},{2,18},{18,2},{3,19},{19,3},{4,20},{20... | collective-permute-start | bytes 9224 | tf_op jit(solution)/shard_map/ppermute | solution.py:1430
  15.2 2.3 copy-start.17
  15.2 2.9 copy-start.18
  15.3 3.0 copy-start.19
  15.3 3.1 copy-start.21
  15.3 3.2 copy-start.22
  15.3 5.0 %copy-start.14 = (bf16[1,48,2304]{2,1,0:T(8,128)(2,1)S(1)}, bf16[1,48,2304]{2,1,0:T(8,128)(2,1)}, u32[]{:S(2)}) copy-start(bf16[1,48,2304]{2,1,0:T(8,128)(2,1)} %param.21) | copy-start | bytes 663556
  15.3 5.0 %copy-start.15 = (bf16[1,48,768]{2,1,0:T(8,128)(2,1)S(1)}, bf16[1,48,768]{2,1,0:T(8,128)(2,1)}, u32[]{:S(2)}) copy-start(bf16[1,48,768]{2,1,0:T(8,128)(2,1)} %param.22) | copy-start | bytes 221188
  16.6 6.2 %copy-start.16 = (f32[1,8,8]{2,1,0:T(8,128)S(1)}, f32[1,8,8]{2,1,0:T(8,128)}, u32[]{:S(2)}) copy-start(f32[1,8,8]{2,1,0:T(8,128)} %param.27) | copy-start | bytes 772
  21.2 160.1 %copy-start.8 = (s32[256,3]{1,0:T(8,128)}, s32[256,3]{1,0:T(8,128)S(1)}, u32[]{:S(2)}) copy-start(s32[256,3]{1,0:T(8,128)S(1)} %get-tuple-element.166.ints) | copy-start | bytes 9220
  21.2 160.1 %copy-start.9 = (s32[256,3]{1,0:T(8,128)}, s32[256,3]{1,0:T(8,128)S(1)}, u32[]{:S(2)}) copy-start(s32[256,3]{1,0:T(8,128)S(1)} %get-tuple-element.167.ints) | copy-start | bytes 9220
  22.8 158.5 %copy-start.12 = (f32[128,128]{1,0:T(8,128)}, f32[128,128]{1,0:T(8,128)S(1)}, u32[]{:S(2)}) copy-start(f32[128,128]{1,0:T(8,128)S(1)} %get-tuple-element.168.mix) | copy-start | bytes 196612
  22.8 158.5 %copy-start.13 = (f32[128,128]{1,0:T(8,128)}, f32[128,128]{1,0:T(8,128)S(1)}, u32[]{:S(2)}) copy-start(f32[128,128]{1,0:T(8,128)S(1)} %get-tuple-element.169.mix) | copy-start | bytes 196612
  181.3 2.8 copy-start.4
  192.9 65.7 %copy-start.2 = (bf16[768,3200]{1,0:T(8,128)(2,1)}, bf16[768,3200]{1,0:T(8,128)(2,1)S(1)}, u32[]{:S(2)}) copy-start(bf16[768,3200]{1,0:T(8,128)(2,1)S(1)} %get-tuple-element.156.w) | copy-start | bytes 14745604
  480.5 10.0 %copy-start.11 = (f32[2,256,128]{2,1,0:T(8,128)S(1)}, f32[2,256,128]{2,1,0:T(8,128)}, u32[]{:S(2)}) copy-start(f32[2,256,128]{2,1,0:T(8,128)} %get-tuple-element.92) | copy-start | bytes 786436
  480.6 10.7 %copy-start.10 = (bf16[2,256,768]{2,1,0:T(8,128)(2,1)S(1)}, bf16[2,256,768]{2,1,0:T(8,128)(2,1)}, u32[]{:S(2)}) copy-start(bf16[2,256,768]{2,1,0:T(8,128)(2,1)} %get-tuple-element.90) | copy-start | bytes 2359300
  486.0 6.1 %copy-start.7 = (f32[2,256,768]{2,1,0:T(8,128)S(1)}, f32[2,256,768]{2,1,0:T(8,128)}, u32[]{:S(2)}) copy-start(f32[2,256,768]{2,1,0:T(8,128)} %get-tuple-element.91) | copy-start | bytes 4718596
  492.2 2.5 copy-start.3
  494.6 2.5 copy-start.6
  494.6 3.7 copy-start.1
  (1 other events, 1.1 us)
